TPU v7x, 32 devices: a whole 2x2x4 slice. The times are simulated.
32 devices in a mesh: batch: 8 (over y, x, core), tp: 4 (over z).
Axes of the slice: x: 2, y: 2, z: 4, core: 2. Of those that a mesh axis runs over, the one named last changes fastest.
Arguments:
- tokens: bfloat16 [64, 256, 1152], P(('batch', 'tp')), may hold values from -6 to 6
- conditioning: bfloat16 [64, 1152], P('batch'), may hold values from -6 to 6
- bucket: int32 [64], P('batch'), may hold values from 0 to 2, as said below
- kept_index: int32 [64, 128], P(('batch', 'tp')), may hold values from 0 to 255, as said below
- w_ada: bfloat16 [1152, 6912], P(None, 'tp'), may hold values from -0.1875 to 0.1875
- ada_bias: bfloat16 [6912], P('tp'), may hold values from -3 to 3
- w_qkv: bfloat16 [3, 1152, 1152], P(None, None, 'tp'), may hold values from -0.1875 to 0.1875
- qv_bias: bfloat16 [2, 1152], P(None, 'tp'), may hold values from -3 to 3
- w_proj: bfloat16 [1152, 1152], P('tp'), may hold values from -0.75 to 0.75
- proj_bias: bfloat16 [1152], replicated, may hold values from -3 to 3
- w_expand: bfloat16 [1152, 4608], P(None, 'tp'), may hold values from -0.1875 to 0.1875
- expand_bias: bfloat16 [4608], P('tp'), may hold values from -3 to 3
- w_reduce: bfloat16 [4608, 1152], P('tp'), may hold values from -0.09375 to 0.09375
- reduce_bias: bfloat16 [1152], replicated, may hold values from -3 to 3
- out_grad: bfloat16 [64, 256, 1152], P(('batch', 'tp')), may hold values from -6 to 6
Outputs:
- output: bfloat16 [64, 256, 1152], P(('batch', 'tp'))
- tokens_grad: bfloat16 [64, 256, 1152], P(('batch', 'tp'))
- w_ada_grad: float32 [1152, 6912], P(None, 'tp')
- ada_bias_grad: float32 [6912], P('tp')
- w_qkv_grad: float32 [3, 1152, 1152], P(None, None, 'tp')
- qv_bias_grad: float32 [2, 1152], P(None, 'tp')
- w_proj_grad: float32 [1152, 1152], P('tp')
- proj_bias_grad: float32 [1152], replicated
- w_expand_grad: float32 [1152, 4608], P(None, 'tp')
- expand_bias_grad: float32 [4608], P('tp')
- w_reduce_grad: float32 [4608, 1152], P('tp')
- reduce_bias_grad: float32 [1152], replicated
Inputs may be any that keep to these rules, and one draw needn't show every extreme that they name: The bucket of each latent: 0 for a 16 x 16 grid of 256 real tokens, 1 for 12 x 20 and 2 for 20 x 12, both of 240 real tokens; real tokens take the first slots, padding the rest. `kept_index`: row l lists distinct slots of latent l. Its first (real tokens) // 2 entries are real slots, the tokens that pass through the block; any later entries name padding slots and are ignored.
All inputs are finite; a program needn't handle non-finite values.
Results may differ from a plain program's by a relative error of at most 0.02.
Values may be sent and summed in bfloat16 or wider, within the bound.
A program may use at most 192 MiB of HBM per device.

v0:
```python
import jax
import jax.numpy as jnp
from jax import lax
from jax.sharding import PartitionSpec as P

HEAD_SIZE = 72


layer_eps = 1e-06
highest = lax.Precision.HIGHEST


def normalize(rows):
    center = rows - jnp.mean(rows, axis=-1, keepdims=True)
    spread = jnp.mean(center * center, axis=-1, keepdims=True)
    return center * lax.rsqrt(spread + layer_eps)


def gelu_tanh(values):
    return jax.nn.gelu(values, approximate=True)


def head_view(rows):
    return rows.reshape(rows.shape[0], rows.shape[1], rows.shape[2] // HEAD_SIZE, HEAD_SIZE)


def slot_mask(bucket, slots, positions):
    real = positions - positions // 16 * (bucket > 0).astype(jnp.int32)
    return (jnp.arange(slots, dtype=jnp.int32)[None, :] < (real // 2)[:, None]).astype(jnp.float32)


def masked_scores(queries, key_rows, valid):
    raw = jnp.einsum(
        "gqhd,gkhd->ghqk",
        head_view(queries),
        head_view(key_rows),
        preferred_element_type=jnp.float32,
    )
    return jnp.where(valid[:, None, None, :] > 0, raw * HEAD_SIZE ** (-0.5), -1000000000.0)


def attend(queries, key_rows, value_rows, valid):
    scores = masked_scores(queries, key_rows, valid)
    top = jnp.max(scores, axis=-1, keepdims=True)
    weights = jnp.exp(scores - top)
    total = jnp.sum(weights, axis=-1, keepdims=True)
    probs = (weights / total).astype(jnp.bfloat16)
    mixed = jnp.einsum(
        "ghqk,gkhd->gqhd", probs, head_view(value_rows), preferred_element_type=jnp.float32
    )
    return (mixed.reshape(queries.shape).astype(jnp.bfloat16), top + jnp.log(total))


def place_one(base, where_at, extra):
    return base.at[where_at].add(extra)


def place_rows(base, index, extra):
    return jax.vmap(place_one)(base, index, extra)


def body(
    tokens,
    conditioning,
    bucket,
    kept_index,
    w_ada,
    ada_bias,
    w_qkv,
    qv_bias,
    w_proj,
    proj_bias,
    w_expand,
    expand_bias,
    w_reduce,
    reduce_bias,
    out_grad,
):
    lat_own, positions, width = tokens.shape
    slots = kept_index.shape[1]
    valid_all = slot_mask(bucket, slots, positions)
    valid_own = lax.dynamic_slice_in_dim(valid_all, lax.axis_index("tp") * lat_own, lat_own, 0)
    mask_own = valid_own[:, :, None]
    silu_low = jax.nn.silu(conditioning.astype(jnp.float32)).astype(jnp.bfloat16)
    mod_cols = jnp.dot(silu_low, w_ada, preferred_element_type=jnp.float32) + ada_bias.astype(
        jnp.float32
    )
    modulation = lax.all_to_all(mod_cols, "tp", split_axis=0, concat_axis=1, tiled=True).reshape(
        lat_own, 6, 1, width
    )
    shift_a, scale_a, gate_a, shift_b, scale_b, gate_b = [
        modulation[:, index] for index in range(6)
    ]
    selected = jnp.take_along_axis(tokens, kept_index[:, :, None], axis=1).astype(jnp.float32)
    normed_a = normalize(selected)
    attn_in = (normed_a * (1.0 + scale_a) + shift_a).astype(jnp.bfloat16)
    bias_pair = qv_bias.astype(jnp.float32)
    piece = lax.all_gather(attn_in, "tp", axis=0, tiled=True)
    stacked = jnp.einsum("nkd,sdc->snkc", piece, w_qkv, preferred_element_type=jnp.float32)
    query_part = (stacked[0] + bias_pair[0]).astype(jnp.bfloat16)
    value_part = (stacked[2] + bias_pair[1]).astype(jnp.bfloat16)
    queries = query_part
    key_rows = stacked[1].astype(jnp.bfloat16)
    value_rows = value_part
    attn_rows = piece
    merged, log_total = attend(queries, key_rows, value_rows, valid_all)
    kept_attention = (queries, key_rows, value_rows, attn_rows, merged, log_total)
    attn_out = lax.psum_scatter(
        jnp.einsum("nkc,cd->nkd", merged, w_proj, preferred_element_type=jnp.float32).astype(
            jnp.bfloat16
        ),
        "tp",
        scatter_dimension=0,
        tiled=True,
    ).astype(jnp.float32) + proj_bias.astype(jnp.float32)
    hidden = selected + gate_a * attn_out
    normed_b = normalize(hidden)
    mlp_in = (normed_b * (1.0 + scale_b) + shift_b).astype(jnp.bfloat16)
    expand_add = expand_bias.astype(jnp.float32)
    piece = lax.all_gather(mlp_in, "tp", axis=0, tiled=True)
    pre_part = (
        jnp.einsum("nkd,df->nkf", piece, w_expand, preferred_element_type=jnp.float32) + expand_add
    )
    pre_all = pre_part
    act_all = gelu_tanh(pre_part).astype(jnp.bfloat16)
    mlp_rows = piece
    mlp_out = lax.psum_scatter(
        jnp.einsum("nkf,fd->nkd", act_all, w_reduce, preferred_element_type=jnp.float32).astype(
            jnp.bfloat16
        ),
        "tp",
        scatter_dimension=0,
        tiled=True,
    ).astype(jnp.float32) + reduce_bias.astype(jnp.float32)
    delta = (gate_a * attn_out + gate_b * mlp_out) * mask_own
    output = place_rows(tokens.astype(jnp.float32), kept_index, delta).astype(jnp.bfloat16)
    cot_kept = (
        jnp.take_along_axis(out_grad, kept_index[:, :, None], axis=1).astype(jnp.float32) * mask_own
    )
    d_mlp = (gate_b * cot_kept).astype(jnp.bfloat16)
    piece = lax.all_gather(d_mlp, "tp", axis=0, tiled=True)
    d_act_part = jnp.einsum("nkd,fd->nkf", piece, w_reduce, preferred_element_type=jnp.float32)
    pre_part = pre_all
    d_pre_all = jax.vjp(gelu_tanh, pre_part)[1](d_act_part)[0].astype(jnp.bfloat16)
    d_mlp_all = piece
    d_mlp_in = lax.psum_scatter(
        jnp.einsum("nkf,df->nkd", d_pre_all, w_expand, preferred_element_type=jnp.float32).astype(
            jnp.bfloat16
        ),
        "tp",
        scatter_dimension=0,
        tiled=True,
    ).astype(jnp.float32)
    expand_grad = jnp.einsum("gkd,gkf->df", mlp_rows, d_pre_all, preferred_element_type=jnp.float32)
    expand_add_grad = jnp.sum(d_pre_all, axis=(0, 1), dtype=jnp.float32)
    reduce_grad = jnp.einsum("gkf,gkd->fd", act_all, d_mlp_all, preferred_element_type=jnp.float32)
    reduce_add_grad = jnp.sum(d_mlp_all, axis=(0, 1), dtype=jnp.float32)
    back_b = jax.vjp(normalize, hidden)[1](d_mlp_in * (1.0 + scale_b))[0]
    d_hidden = cot_kept + back_b
    d_shift_b = jnp.sum(d_mlp_in, axis=1)
    d_scale_b = jnp.sum(d_mlp_in * normed_b, axis=1)
    d_gate_b = jnp.sum(cot_kept * mlp_out, axis=1)
    d_gate_a = jnp.sum(d_hidden * attn_out, axis=1)
    d_attn = (gate_a * d_hidden).astype(jnp.bfloat16)
    piece = lax.all_gather(d_attn, "tp", axis=0, tiled=True)
    d_merged = jnp.einsum("nkd,cd->nkc", piece, w_proj, preferred_element_type=jnp.float32).astype(
        jnp.bfloat16
    )
    queries, key_rows, value_rows, attn_rows, merged, log_total = kept_attention
    proj_grad = jnp.einsum("gkc,gkd->cd", merged, piece, preferred_element_type=jnp.float32)
    proj_add_grad = jnp.sum(piece, axis=(0, 1), dtype=jnp.float32)
    scores = masked_scores(queries, key_rows, valid_all)
    probs_full = jnp.exp(scores - log_total)
    d_heads = head_view(d_merged)
    d_values = jnp.einsum(
        "ghqk,gqhd->gkhd",
        probs_full.astype(jnp.bfloat16),
        d_heads,
        preferred_element_type=jnp.float32,
    )
    d_probs = jnp.einsum(
        "gqhd,gkhd->ghqk", d_heads, head_view(value_rows), preferred_element_type=jnp.float32
    )
    d_scores = (
        probs_full * (d_probs - jnp.sum(d_probs * probs_full, axis=-1, keepdims=True))
    ).astype(jnp.bfloat16)
    d_queries = jnp.einsum(
        "ghqk,gkhd->gqhd", d_scores, head_view(key_rows), preferred_element_type=jnp.float32
    ) * HEAD_SIZE ** (-0.5)
    d_keys = jnp.einsum(
        "ghqk,gqhd->gkhd", d_scores, head_view(queries), preferred_element_type=jnp.float32
    ) * HEAD_SIZE ** (-0.5)
    d_qkv = jnp.stack(
        [
            d_queries.reshape(queries.shape),
            d_keys.reshape(queries.shape),
            d_values.reshape(queries.shape),
        ]
    ).astype(jnp.bfloat16)
    qkv_grad = jnp.einsum("gkd,sgkc->sdc", attn_rows, d_qkv, preferred_element_type=jnp.float32)
    pair_grad = jnp.sum(d_qkv[::2], axis=(1, 2), dtype=jnp.float32)
    d_attn_in = lax.psum_scatter(
        jnp.einsum("sgkc,sdc->gkd", d_qkv, w_qkv, preferred_element_type=jnp.float32).astype(
            jnp.bfloat16
        ),
        "tp",
        scatter_dimension=0,
        tiled=True,
    ).astype(jnp.float32)
    back_a = jax.vjp(normalize, selected)[1](d_attn_in * (1.0 + scale_a))[0]
    d_shift_a = jnp.sum(d_attn_in, axis=1)
    d_scale_a = jnp.sum(d_attn_in * normed_a, axis=1)
    tokens_grad = place_rows(out_grad.astype(jnp.float32), kept_index, back_b + back_a).astype(
        jnp.bfloat16
    )
    d_modulation = jnp.stack(
        [d_shift_a, d_scale_a, d_gate_a, d_shift_b, d_scale_b, d_gate_b], axis=1
    ).reshape(lat_own, 6 * width)
    d_mod_cols = lax.all_to_all(
        d_modulation.astype(jnp.bfloat16), "tp", split_axis=1, concat_axis=0, tiled=True
    ).astype(d_modulation.dtype)
    ada_grad = jnp.dot(silu_low.astype(jnp.float32).T, d_mod_cols, precision=highest)
    ada_add_grad = jnp.sum(d_mod_cols, axis=0)
    summed = (
        lax.psum(ada_grad.astype(jnp.bfloat16), "batch").astype(jnp.float32),
        lax.psum(ada_add_grad.astype(jnp.bfloat16), "batch").astype(jnp.float32),
        lax.psum(qkv_grad.astype(jnp.bfloat16), "batch").astype(jnp.float32),
        lax.psum(pair_grad.astype(jnp.bfloat16), "batch").astype(jnp.float32),
        lax.psum(proj_grad.astype(jnp.bfloat16), "batch").astype(jnp.float32),
        lax.psum(proj_add_grad.astype(jnp.bfloat16), "batch").astype(jnp.float32),
        lax.psum(expand_grad.astype(jnp.bfloat16), "batch").astype(jnp.float32),
        lax.psum(expand_add_grad.astype(jnp.bfloat16), "batch").astype(jnp.float32),
        lax.psum(reduce_grad.astype(jnp.bfloat16), "batch").astype(jnp.float32),
        lax.psum(reduce_add_grad.astype(jnp.bfloat16), "batch").astype(jnp.float32),
    )
    return (
        output,
        tokens_grad,
        summed[0],
        summed[1],
        summed[2],
        summed[3],
        summed[4],
        summed[5],
        summed[6],
        summed[7],
        summed[8],
        summed[9],
    )


def solution(mesh):
    return jax.shard_map(
        body,
        mesh=mesh,
        in_specs=(
            P(("batch", "tp"), None, None),
            P("batch", None),
            P("batch"),
            P(("batch", "tp"), None),
            P(None, "tp"),
            P("tp"),
            P(None, None, "tp"),
            P(None, "tp"),
            P("tp", None),
            P(),
            P(None, "tp"),
            P("tp"),
            P("tp", None),
            P(),
            P(("batch", "tp"), None, None),
        ),
        out_specs=(
            P(("batch", "tp"), None, None),
            P(("batch", "tp"), None, None),
            P(None, "tp"),
            P("tp"),
            P(None, None, "tp"),
            P(None, "tp"),
            P("tp", None),
            P(),
            P(None, "tp"),
            P("tp"),
            P("tp", None),
            P(),
        ),
        check_vma=False,
    )
```

profile of v0, /device:TPU:17, one launch (start us, length us, event | category | flops | bytes accessed | tf_op | source)
XLA Modules:
  0.0 681.0 jit_solution(3336914458054770032)
XLA Ops:
  12.0 4.6 all-to-all-start
  20.6 4.3 gather_fusion.1
  29.3 50.7 %all-gather.5.cloned.1.call-done = bf16[8,128,1152]{2,1,0:T(8,128)(2,1)} async-done(((bf16[2,128,1152]{2,1,0:T(8,128)(2,1)}), bf16[8,128,1152]{2,1,0:T(8,128)(2,1)}) %all-gather.5.cloned.1.call-update) | async-done | bytes 2359312 | tf_op jit(solution)/shard_map/all_gather | solution.py:98
  80.0 4.7 fusion.20
  92.3 47.1 %reduce-scatter.5.cloned.1.call-done = bf16[2,128,1152]{2,1,0:T(8,128)(2,1)} async-done(((bf16[8,128,1152]{2,1,0:T(8,128)(2,1)}), bf16[2,128,1152]{2,1,0:T(8,128)(2,1)}) %reduce-scatter.5.cloned.1.call-update) | async-done | bytes 589840 | tf_op jit(solution)/shard_map/reduce_scatter | solution.py:108
  144.5 48.7 %all-gather.7.cloned.1.call-done = bf16[8,128,1152]{2,1,0:T(8,128)(2,1)} async-done(((bf16[2,128,1152]{2,1,0:T(8,128)(2,1)}), bf16[8,128,1152]{2,1,0:T(8,128)(2,1)}) %all-gather.7.cloned.1.call-update) | async-done | bytes 2359312 | tf_op jit(solution)/shard_map/all_gather | solution.py:120
  193.2 8.1 %convolution_add_fusion = f32[8,128,1152]{2,1,0:T(8,128)} fusion(bf16[8,128,1152]{2,1,0:T(8,128)(2,1)} %all-gather.7.cloned.1.call-done, bf16[1152,1152]{1,0:T(8,128)(2,1)} %param.27, f32[1152]{0:T(1024)S(1)} %convert_element_type.207), kind=kOutput, calls=%fused_computation.20 | convolution fusion | flops 2719088640 | bytes 9736704 | tf_op jit(solution)/shard_map/nkd,df->nkf/dot_general | solution.py:122
  201.4 43.2 %all-gather.9.cloned.1.call-done = bf16[8,128,1152]{2,1,0:T(8,128)(2,1)} async-done(((bf16[2,128,1152]{2,1,0:T(8,128)(2,1)}), bf16[8,128,1152]{2,1,0:T(8,128)(2,1)}) %all-gather.9.cloned.1.call-update) | async-done | bytes 2359312 | tf_op jit(solution)/shard_map/all_gather | solution.py:141
  244.6 9.3 %fusion.74 = (bf16[1152]{0:T(1024)(128)(2,1)S(1)}, bf16[8,128,1152]{2,1,0:T(8,128)(2,1)S(1)}) fusion(f32[8,128,1152]{2,1,0:T(8,128)} %convolution_add_fusion, bf16[8,128,1152]{2,1,0:T(8,128)(2,1)} %all-gather.9.cloned.1.call-done, bf16[1152,1152]{1,0:T(8,128)(2,1)S(1)} %copy-done), kind=kOutput, calls=%fused_computation.164 | convolution fusion | flops 2742680576 | bytes 12093696 | tf_op jit(solution)/shard_map/nkd,fd->nkf/dot_general | solution.py:142
  255.3 4.8 convolution_convert_fusion.2
  260.2 7.9 %convolution_convert_fusion.3 = bf16[8,128,1152]{2,1,0:T(8,128)(2,1)} fusion(bf16[1152,1152]{1,0:T(8,128)(2,1)S(1)} %copy-done, f32[8,128,1152]{2,1,0:T(8,128)} %convolution_add_fusion), kind=kOutput, calls=%fused_computation.24 | convolution fusion | flops 2729705472 | bytes 9732096 | tf_op jit(solution)/shard_map/nkf,fd->nkd/dot_general | solution.py:128
  268.1 11.6 %all-gather.11.cloned.1.call-start = ((), (), s32[]{:S(2)}) async-start(), calls=%async_computation.12 | async-start | bytes 2949120 | tf_op jit(solution)/shard_map/all_gather | solution.py:165
  279.7 28.1 %reduce-scatter.9.cloned.1.call-done = bf16[2,128,1152]{2,1,0:T(8,128)(2,1)} async-done(((bf16[8,128,1152]{2,1,0:T(8,128)(2,1)}), bf16[2,128,1152]{2,1,0:T(8,128)(2,1)}) %reduce-scatter.9.cloned.1.call-update) | async-done | bytes 589840 | tf_op jit(solution)/shard_map/reduce_scatter | solution.py:146
  309.7 48.5 %reduce-scatter.7.cloned.1.call-done = bf16[2,128,1152]{2,1,0:T(8,128)(2,1)} async-done(((bf16[8,128,1152]{2,1,0:T(8,128)(2,1)}), bf16[2,128,1152]{2,1,0:T(8,128)(2,1)}) %reduce-scatter.7.cloned.1.call-update) | async-done | bytes 589840 | tf_op jit(solution)/shard_map/reduce_scatter | solution.py:127
  361.8 49.3 %all-gather.11.cloned.1.call-done = bf16[8,128,1152]{2,1,0:T(8,128)(2,1)} async-done(((bf16[2,128,1152]{2,1,0:T(8,128)(2,1)}), bf16[8,128,1152]{2,1,0:T(8,128)(2,1)}) %all-gather.11.cloned.1.call-update) | async-done | bytes 2359312 | tf_op jit(solution)/shard_map/all_gather | solution.py:165
  426.0 6.6 fusion
  432.5 7.6 %fusion.1 = bf16[1152,1152]{1,0:T(8,128)(2,1)} fusion(bf16[8,128,1152]{2,1,0:T(8,128)(2,1)S(1)} %copy-done.28, f32[8,128,1152]{2,1,0:T(8,128)} %convolution_add_fusion), kind=kOutput, calls=%fused_computation.7 | convolution fusion | flops 2729852928 | bytes 9732096 | tf_op jit(solution)/shard_map/gkf,gkd->fd/dot_general | solution.py:156
  440.3 5.8 fusion.9
  446.1 25.9 %reduce-scatter.11.cloned.1.call-done = bf16[2,128,1152]{2,1,0:T(8,128)(2,1)} async-done(((bf16[8,128,1152]{2,1,0:T(8,128)(2,1)}), bf16[2,128,1152]{2,1,0:T(8,128)(2,1)}) %reduce-scatter.11.cloned.1.call-update) | async-done | bytes 589840 | tf_op jit(solution)/shard_map/reduce_scatter | solution.py:202
  492.5 41.1 %scatter_fusion = f32[2,256,1152]{2,1,0:T(8,128)} fusion(f32[2,256,1152]{2,1,0:T(8,128)} %convert_element_type.188, s32[256]{0:T(256)S(1)} %get-tuple-element.42, f32[256,1152]{1,0:T(8,128)} %bitcast.176), kind=kCustom, calls=%fused_computation.2 | custom fusion | flops 294912 | bytes 3540992 | tf_op jit(solution)/shard_map/vmap()/scatter-add | solution.py:55
  543.6 27.3 %scatter_fusion.1 = f32[2,256,1152]{2,1,0:T(8,128)S(1)} fusion(f32[2,256,1152]{2,1,0:T(8,128)S(1)} %convert_element_type.213, s32[256]{0:T(256)S(1)} %get-tuple-element.42, f32[256,1152]{1,0:T(8,128)} %bitcast.177), kind=kCustom, calls=%fused_computation.3 | custom fusion | flops 294912 | bytes 3540992 | tf_op jit(solution)/shard_map/vmap()/scatter-add | solution.py:55
  572.0 21.7 %all-reduce = (bf16[1728]{0:T(1024)(128)(2,1)S(1)}, bf16[2,288]{1,0:T(2,128)(2,1)S(1)}, bf16[1152]{0:T(1024)(128)(2,1)S(1)}, bf16[1152]{0:T(1024)(128)(2,1)S(1)}, bf16[1152]{0:T(1024)(128)(2,1)S(1)}) all-reduce(bf16[1728]{0:T(1024)(128)(2,1)S(1)} %reduce_sum.252, ...), channel_id=1, replica_groups=mesh['batch'=8,'tp'=4] {'batch'}, use_global_device_ids=true, to_apply=%region_25.27 | all-reduce | flops 5760 | bytes 23040 | tf_op jit(solution)/shard_map/psum | solution.py:226
  596.7 60.4 %all-reduce.4.cloned.1.call-done = (bf16[1152,1728]{0,1:T(8,128)(2,1)}, bf16[3,1152,288]{1,2,0:T(8,128)(2,1)}, bf16[288,1152]{1,0:T(8,128)(2,1)}, bf16[1152,1152]{1,0:T(8,128)(2,1)}, bf16[1152,1152]{1,0:T(8,128)(2,1)}) async-done(((bf16[1152,1728]{0,1:T(8,128)(2,1)}, bf16[3,1152,288]{1,2,0:T(8,128)(2,1)}, bf16[288,1152]{1,0:T(8,128)(2,1)}, bf16[1152,1152]{1,0:T(8,128)(2,1)}, bf16[1152,1152]{1,0:T(8,128)(2,1)}), ...) | async-done | bytes 11943952 | tf_op jit(solution)/shard_map/psum | solution.py:225
  659.3 6.0 convert_element_type.228
  (201 shorter events, 92.7 us)
Async XLA Ops:
  7.2 237.4 %copy-start = (bf16[1152,1152]{1,0:T(8,128)(2,1)S(1)}, bf16[1152,1152]{1,0:T(8,128)(2,1)}, u32[]{:S(2)}) copy-start(bf16[1152,1152]{1,0:T(8,128)(2,1)} %param.29) | copy-start | bytes 7962628
  8.0 8.6 %copy-start.40 = (s32[2,128]{1,0:T(2,128)S(1)}, s32[2,128]{1,0:T(2,128)}, u32[]{:S(2)}) copy-start(s32[2,128]{1,0:T(2,128)} %param.20) | copy-start | bytes 3076
  8.0 8.7 %copy-start.44 = (s32[8]{0:T(128)S(1)}, s32[8]{0:T(128)}, u32[]{:S(2)}) copy-start(s32[8]{0:T(128)} %param.19) | copy-start | bytes 100
  12.0 12.8 %all-to-all-start = ((f32[4,2,1728]{2,1,0:T(2,128)}), f32[4,2,1728]{2,1,0:T(2,128)S(1)}, u32[]{:S(2)}, u32[]{:S(2)}) async-start(f32[4,2,1728]{2,1,0:T(2,128)} %all_to_all.24), calls=%async_computation | async-start | bytes 114688 | tf_op jit(solution)/shard_map/all_to_all | solution.py:88
  16.7 63.4 %all-gather.5.cloned.1.call-start = ((), (), s32[]{:S(2)}) async-start(), calls=%async_computation.6 | async-start | bytes 2949120 | tf_op jit(solution)/shard_map/all_gather | solution.py:98
  29.1 110.3 %reduce-scatter.5.cloned.1.call-start = ((), (), s32[]{:S(2)}) async-start(), calls=%async_computation.7 | async-start | bytes 2949120 | tf_op jit(solution)/shard_map/reduce_scatter | solution.py:108
  91.6 101.6 %all-gather.7.cloned.1.call-start = ((), (), s32[]{:S(2)}) async-start(), calls=%async_computation.8 | async-start | bytes 2949120 | tf_op jit(solution)/shard_map/all_gather | solution.py:120
  143.9 100.7 %all-gather.9.cloned.1.call-start = ((), (), s32[]{:S(2)}) async-start(), calls=%async_computation.10 | async-start | bytes 2949120 | tf_op jit(solution)/shard_map/all_gather | solution.py:141
  144.4 163.4 %reduce-scatter.9.cloned.1.call-start = ((), (), s32[]{:S(2)}) async-start(), calls=%async_computation.11 | async-start | bytes 2949120 | tf_op jit(solution)/shard_map/reduce_scatter | solution.py:146
  244.6 10.7 %copy-start.41 = (bf16[1152,1152]{1,0:T(8,128)(2,1)S(1)}, bf16[1152,1152]{1,0:T(8,128)(2,1)}, u32[]{:S(2)}) copy-start(bf16[1152,1152]{1,0:T(8,128)(2,1)} %param.27) | copy-start | bytes 7962628
  260.1 98.0 %reduce-scatter.7.cloned.1.call-start = ((), (), s32[]{:S(2)}) async-start(), calls=%async_computation.9 | async-start | bytes 2949120 | tf_op jit(solution)/shard_map/reduce_scatter | solution.py:127
  268.1 11.6 %copy-start.38 = (bf16[1152]{0:T(1024)(128)(2,1)S(1)}, bf16[1152]{0:T(1024)(128)(2,1)}, u32[]{:S(2)}) copy-start(bf16[1152]{0:T(1024)(128)(2,1)} %param.30) | copy-start | bytes 6916
  268.1 39.8 %copy-start.14 = (f32[2,128,1152]{2,1,0:T(8,128)S(1)}, f32[2,128,1152]{2,1,0:T(8,128)}, u32[]{:S(2)}) copy-start(f32[2,128,1152]{2,1,0:T(8,128)} %copy-done.13) | copy-start | bytes 3538948
  268.1 143.0 %all-gather.11.cloned.1.call-start = ((), (), s32[]{:S(2)}) async-start(), calls=%async_computation.12 | async-start | bytes 2949120 | tf_op jit(solution)/shard_map/all_gather | solution.py:165
  309.2 48.9 %copy-start.10 = (bf16[2,128,1152]{2,1,0:T(8,128)(2,1)S(1)}, bf16[2,128,1152]{2,1,0:T(8,128)(2,1)}, u32[]{:S(2)}) copy-start(bf16[2,128,1152]{2,1,0:T(8,128)(2,1)} %reduce-scatter.5.cloned.1.call-done) | copy-start | bytes 1769476
  361.7 110.4 %reduce-scatter.11.cloned.1.call-start = ((), (), s32[]{:S(2)}) async-start(), calls=%async_computation.13 | async-start | bytes 2949120 | tf_op jit(solution)/shard_map/reduce_scatter | solution.py:202
  361.7 52.1 %copy-start.3 = (f32[8,4,128,128]{2,3,1,0:T(8,128)S(1)}, f32[8,4,128,128]{2,3,1,0:T(8,128)}, u32[]{:S(2)}) copy-start(f32[8,4,128,128]{2,3,1,0:T(8,128)} %copy-done.2) | copy-start | bytes 6291460
  426.0 6.6 copy-start.28
  432.5 7.6 %copy-start.7 = (bf16[2,128,1152]{2,1,0:T(8,128)(2,1)S(1)}, bf16[2,128,1152]{2,1,0:T(8,128)(2,1)}, u32[]{:S(2)}) copy-start(bf16[2,128,1152]{2,1,0:T(8,128)(2,1)} %reduce-scatter.9.cloned.1.call-done) | copy-start | bytes 1769476
  432.5 7.7 %copy-start.27 = (bf16[8,4,72,128]{3,2,1,0:T(8,128)(2,1)S(1)}, bf16[8,4,72,128]{3,2,1,0:T(8,128)(2,1)}, u32[]{:S(2)}) copy-start(bf16[8,4,72,128]{3,2,1,0:T(8,128)(2,1)} %copy-done.26) | copy-start | bytes 1769476
  440.3 31.8 %copy-start.11 = (bf16[2,128,1152]{2,1,0:T(8,128)(2,1)S(1)}, bf16[2,128,1152]{2,1,0:T(8,128)(2,1)}, u32[]{:S(2)}) copy-start(bf16[2,128,1152]{2,1,0:T(8,128)(2,1)} %reduce-scatter.5.cloned.1.call-done) | copy-start | bytes 1769476
  440.3 31.8 %copy-start.17 = (bf16[256,1152]{1,0:T(8,128)(2,1)S(1)}, bf16[256,1152]{1,0:T(8,128)(2,1)}, u32[]{:S(2)}) copy-start(bf16[256,1152]{1,0:T(8,128)(2,1)} %gather_fusion.1) | copy-start | bytes 1769476
  476.9 7.2 %all-to-all-start.1 = ((bf16[2,4,1728]{2,0,1:T(2,128)(2,1)}), bf16[2,4,1728]{2,0,1:T(2,128)(2,1)S(1)}, u32[]{:S(2)}, u32[]{:S(2)}) async-start(bf16[2,4,1728]{2,0,1:T(2,128)(2,1)} %copy.70), calls=%async_computation.5 | async-start | bytes 57344 | tf_op jit(solution)/shard_map/all_to_all | solution.py:219
  480.6 176.5 %all-reduce.4.cloned.1.call-start = ((), (), s32[]{:S(2)}) async-start(), calls=%async_computation.14 | async-start | bytes 23887872 | tf_op jit(solution)/shard_map/psum | solution.py:225
  (33 other events, 69.7 us)
Sparse Core Ops, SparseCore 0:
  29.2 50.8 all-gather.4
  91.7 47.5 reduce-scatter.4
  144.0 49.2 all-gather.6
  195.2 49.2 all-gather.8
  260.2 47.5 reduce-scatter.8
  310.6 47.5 reduce-scatter.6
  361.8 49.2 all-gather.10
  424.4 47.5 reduce-scatter.10
  487.4 169.6 all-reduce.3
where the time goes:
time: 694 us; the launch traced here: 681 us
  waiting for transfers between devices  403 us (58%)
  other arithmetic  120 us (17%)
  matrix products  79 us (11%)
  local copies, waits for them, and re-layouts  22.4 us (3%)
  blocking collectives  21.7 us (3%)
  starting transfers between devices  20.5 us (3%)
  between operations  14.8 us (2%)
    scatter-add x2, other arithmetic, place_one(): return base.at[where_at].add(extra)  68.4 us
    psum x1, waiting for transfers between devices, body(): lax.psum(ada_grad.astype(jnp.bfloat16), 'batch').astype(jnp.float32)  60.4 us
    all_gather x1, waiting for transfers between devices, body(): piece = lax.all_gather(attn_in, 'tp', axis=0, tiled=True)  50.7 us
    all_gather x1, waiting for transfers between devices, body(): piece = lax.all_gather(d_attn, 'tp', axis=0, tiled=True)  49.3 us
    all_gather x1, waiting for transfers between devices, body(): piece = lax.all_gather(mlp_in, 'tp', axis=0, tiled=True)  48.7 us
    reduce_scatter x1, waiting for transfers between devices, body(): lax.psum_scatter(jnp.einsum('nkf,fd->nkd', act_all, w_reduce, preferred_e...  48.5 us
    reduce_scatter x1, waiting for transfers between devices, body(): lax.psum_scatter(jnp.einsum('nkc,cd->nkd', merged, w_proj, preferred_elem...  47.1 us
    all_gather x1, waiting for transfers between devices, body(): piece = lax.all_gather(d_mlp, 'tp', axis=0, tiled=True)  43.2 us
  transfers between devices with their start and end apart: 11, of which 9 were waited for; matrix products, arithmetic and copies ran while one was open for 20% of the time, Pallas kernels for 0%

commit v1 on v0

v1 whole, which is shorter than its diff:
```python
import functools
import jax
import jax.numpy as jnp
from jax import lax
from jax.experimental import pallas as pl
from jax.experimental.pallas import tpu as pltpu
from jax.sharding import PartitionSpec as P

HEAD_SIZE = 72
EPS = 1e-06
F32 = jnp.float32
BF = jnp.bfloat16
MESH = pl.DeviceIdType.MESH
MIB = 2**20


def nn(a, b):
    return lax.dot_general(a, b, (((1,), (0,)), ((), ())), preferred_element_type=F32)


def nt(a, b):
    return lax.dot_general(a, b, (((1,), (1,)), ((), ())), preferred_element_type=F32)


def tn(a, b):
    return lax.dot_general(a, b, (((0,), (0,)), ((), ())), preferred_element_type=F32)


def flip(b, mask):
    out, bit = b, 1
    while bit <= mask:
        if mask & bit:
            out = out + bit - 2 * bit * ((b // bit) % 2)
        bit *= 2
    return out


def group_size(ff_shard, width_shard):
    for size in (8, 4, 2):
        rows = ff_shard // size
        if ff_shard % size == 0 and rows % 16 == 0 and 4 * width_shard == size * rows:
            return size
    raise ValueError("no group")


def link_orders(group):
    bits = []
    bit = 2
    while bit < group:
        bits.append(bit)
        bit *= 2
    return bits, bits[::-1]


def span(bits):
    out = [0]
    for bit in bits:
        out = out + [item ^ bit for item in out]
    return out


def near_shard(z, k, count):
    low = jnp.minimum(z, count - 1 - z)
    both = z + (k // 2 + 1) * (1 - 2 * (k % 2))
    one = z + jnp.where(2 * z < count - 1, 1, -1) * (k - low + 1)
    return jnp.where(k < 2 * low, both, one)


class Gather:
    def __init__(self, b, z, group, region, send_sem, recv_sem, halves=2):
        self.b, self.z = b, z
        self.region, self.send_sem, self.recv_sem = region, send_sem, recv_sem
        self.orders = link_orders(group)[:halves] if halves == 2 else link_orders(group)[:1]
        self.group = group
        self.sent = []

    def copy(self, m, bit, p):
        return pltpu.make_async_remote_copy(
            src_ref=self.region(m, p, m),
            dst_ref=self.region(m, p, m ^ bit),
            send_sem=self.send_sem(m ^ bit, p),
            recv_sem=self.recv_sem(m ^ bit, p),
            device_id=(flip(self.b, bit), self.z),
            device_id_type=MESH,
        )

    def send(self, m, bit, p):
        cp = self.copy(m, bit, p)
        cp.start()
        self.sent.append(cp)

    def wait(self, m, p):
        ref = self.region(m, p, m)
        pltpu.make_async_remote_copy(
            src_ref=ref, dst_ref=ref, send_sem=self.send_sem(m, p), recv_sem=self.recv_sem(m, p),
            device_id=(flip(self.b, 1), self.z), device_id_type=MESH,
        ).wait_recv()

    def step(self, i):
        for p, order in enumerate(self.orders):
            if i == 0:
                fresh = [0]
            elif i <= len(order):
                fresh = [item ^ order[i - 1] for item in span(order[: i - 1])]
                for m in fresh:
                    self.wait(m, p)
            else:
                continue
            if i < len(order):
                for m in span(order[:i]):
                    self.send(m, order[i], p)
            for m in fresh:
                self.send(m, 1, p)

    def steps(self):
        return len(self.orders[0]) + 1

    def wait_core(self, m=None):
        for p in range(len(self.orders)):
            for item in range(1, self.group, 2):
                if m is None or item == m:
                    self.wait(item, p)

    def wait_sent(self):
        for cp in self.sent:
            cp.wait_send()


class Scatter:
    def __init__(self, b, z, group, mine, inbox, send_sem, recv_sem, add):
        self.b, self.z, self.group = b, z, group
        self.mine, self.inbox, self.add = mine, inbox, add
        self.send_sem, self.recv_sem = send_sem, recv_sem
        self.orders = link_orders(group)
        self.sent = []

    def top(self, m, p):
        if m & 1:
            return 1
        for bit in reversed(self.orders[p]):
            if m & bit:
                return bit

    def copy(self, m, p):
        return pltpu.make_async_remote_copy(
            src_ref=self.mine(m, p),
            dst_ref=self.inbox(m, p),
            send_sem=self.send_sem(m, p),
            recv_sem=self.recv_sem(m, p),
            device_id=(flip(self.b, self.top(m, p)), self.z),
            device_id_type=MESH,
        )

    def keys(self, m, p):
        if m & 1:
            return []
        out = [m ^ 1]
        order = self.orders[p]
        above = order if m == 0 else order[order.index(self.top(m, p)) + 1 :]
        return out + [m ^ bit for bit in reversed(above)]

    def fold(self, m, p):
        for key in self.keys(m, p):
            self.copy(key, p).wait_recv()
            self.add(m, key, p)

    def send(self, m, p):
        cp = self.copy(m, p)
        cp.start()
        self.sent.append(cp)

    def wait_sent(self):
        for cp in self.sent:
            cp.wait_send()


def barrier(b, z, group, count):
    sem = pltpu.get_barrier_semaphore()
    for m in range(1, group):
        pl.semaphore_signal(sem, 1, device_id=(flip(b, m), z), device_id_type=MESH)
    for d in range(1, count):
        pl.semaphore_signal(sem, 1, device_id=(b, lax.rem(z + d, count)), device_id_type=MESH)
    pl.semaphore_wait(sem, group - 1 + count - 1)


def stats(rows):
    center = rows - jnp.mean(rows, axis=-1, keepdims=True)
    return center, lax.rsqrt(jnp.mean(center * center, axis=-1, keepdims=True) + EPS)


def head_window(h, width):
    start = jnp.minimum(h * HEAD_SIZE // 128, width // 128 - 2) * 128
    lane = lax.broadcasted_iota(jnp.int32, (1, 256), 1) + (start - h * HEAD_SIZE)
    own = jnp.where((lane >= 0) & (lane < HEAD_SIZE), 1.0, 0.0)
    return pl.ds(pl.multiple_of(start, 128), 256), own


def first_kernel(
    dims, lat, real_ref, cond_ref, wada_ref, abias_ref, tok_ref, cot_in_ref, kept_ref, qvb_ref, projb_ref,
    own_qkv, own_proj, own_1, own_2,
    attn_in_o, q_o, k_o, v_o, merged_o, attn_out_o, hidden_o, mlp_in_o, cot_o, mod_o,
    full_o, all_1, all_2, dmlp_o,
    full, sm_send, sm_recv, nrm, sel, mg, mod8,
    sm_ss, sm_rs, za_ss, za_rs, zm_ss, zm_rs, ga_ss, ga_rs, gd_ss, gd_rs, loc,
):
    group, count, rows_s, width = dims
    b, z = lax.axis_index("batch"), lax.axis_index("tp")
    g = b % group
    ds = width // count
    slots = kept_ref.shape[1]
    barrier(b, z, group, count)

    cut = (rows_s // 2 + 15) // 16 * 16
    parts = ((0, cut), (cut, rows_s - cut))

    def piece(member, shard, p):
        at = member * rows_s
        lo, ln = parts[p] if p is not None else (0, rows_s)
        return full.at[at // ds, shard, pl.ds(at % ds + lo, ln)]

    own_copy = [
        pltpu.make_async_copy(own_qkv, full.at[0:3, z], loc.at[0]),
        pltpu.make_async_copy(own_proj, full.at[3, z], loc.at[5]),
    ]
    for cp in own_copy:
        cp.start()

    def line_a(shard, src, step, k):
        return pltpu.make_async_remote_copy(
            src_ref=src, dst_ref=piece(g, shard, None), send_sem=za_ss.at[k], recv_sem=za_rs.at[shard],
            device_id=(b, z + step), device_id_type=MESH,
        )

    def line_m(shard, src1, src2, step, k):
        return [
            pltpu.make_async_remote_copy(
                src_ref=src, dst_ref=dst.at[shard], send_sem=zm_ss.at[i, k], recv_sem=zm_rs.at[i, shard],
                device_id=(b, z + step), device_id_type=MESH,
            )
            for i, (src, dst) in enumerate(((src1, all_1), (src2, all_2)))
        ]

    slice_at = pl.ds(pl.multiple_of(g * rows_s, 16), rows_s)
    own_m = [
        pltpu.make_async_copy(own_1.at[slice_at], all_1.at[z], loc.at[2]),
        pltpu.make_async_copy(own_2.at[slice_at], all_2.at[z], loc.at[3]),
    ]
    for cp in own_m:
        cp.start()

    def both_ways(fn):
        @pl.when(z < count - 1)
        def _():
            fn(1, 0)

        @pl.when(z > 0)
        def _():
            fn(-1, 1)

    for cp in own_copy:
        cp.wait()
    both_ways(lambda step, k: line_a(z, piece(g, z, None), step, k).start())

    cond = cond_ref[...].astype(F32)
    silu = (cond / (1.0 + jnp.exp(-cond))).astype(BF)
    mod8[...] = jnp.zeros_like(mod8)
    cols = wada_ref.shape[0]
    mod8[:, 0:cols] = nt(silu, wada_ref[...]) + abias_ref[...].astype(F32)
    framed = pltpu.roll(mod8[...], (z * cols) % width, 1)
    for t in range(count):
        for i in range(2):
            sm_send[t, i] = framed[lat * t : lat * (t + 1), i * width : (i + 1) * width]
        sm_send[t, 2] = qvb_ref[...]

    def small(d):
        peer = lax.rem(z + d, count)
        return pltpu.make_async_remote_copy(
            src_ref=sm_send.at[peer], dst_ref=sm_recv.at[z], send_sem=sm_ss.at[d], recv_sem=sm_rs.at[d],
            device_id=(b, peer), device_id_type=MESH,
        )

    for d in range(1, count):
        small(d).start()
    small_own = pltpu.make_async_copy(sm_send.at[z], sm_recv.at[z], loc.at[1])
    small_own.start()

    valid = []
    for l in range(lat):
        real = real_ref[z * lat + l]
        row = lax.broadcasted_iota(jnp.int32, (slots, 1), 0)
        valid.append(jnp.where(row < real, 1.0, 0.0))
        place = lax.broadcasted_iota(jnp.int32, (slots, tok_ref.shape[1]), 1)
        pick = jnp.where(place == kept_ref[l], 1.0, 0.0).astype(BF)
        at = slice(l * slots, (l + 1) * slots)
        rows = nn(pick, tok_ref[l])
        sel[at] = rows
        center, inv = stats(rows)
        nrm[at] = center * inv
        cot_o[at] = (nn(pick, cot_in_ref[l]) * valid[l]).astype(BF)

    gathers = []
    for k in range(count - 1):
        shard = near_shard(z, k, count)

        def region(m, p, slot, shard=shard):
            return piece(flip(g, m), shard, p)

        gathers.append(
            Gather(b, z, group, region, lambda m, p, k=k: ga_ss.at[k, p, m], lambda m, p, shard=shard: ga_rs.at[shard, p, m])
        )

    def arrive_a(k):
        shard = near_shard(z, k, count)
        ref = piece(g, shard, None)
        line_a(shard, ref, 0, 2 + k).wait_recv()
        gathers[k].step(0)

        @pl.when((shard < z) & (z < count - 1))
        def _():
            line_a(shard, ref, 1, 2 + k).start()

        @pl.when((shard > z) & (z > 0))
        def _():
            line_a(shard, ref, -1, 2 + k).start()

    def arrive_m(k):
        shard = near_shard(z, k, count)
        r1, r2 = all_1.at[shard], all_2.at[shard]
        for cp in line_m(shard, r1, r2, 0, 2 + k):
            cp.wait_recv()

        @pl.when((shard < z) & (z < count - 1))
        def _():
            for cp in line_m(shard, r1, r2, 1, 2 + k):
                cp.start()

        @pl.when((shard > z) & (z > 0))
        def _():
            for cp in line_m(shard, r1, r2, -1, 2 + k):
                cp.start()

    def send_m(step, k):
        for cp in line_m(z, all_1.at[z], all_2.at[z], step, k):
            cp.start()

    arrive_a(0)
    for cp in own_m:
        cp.wait()

    for d in range(1, count):
        peer = lax.rem(z + d, count)
        ref = sm_recv.at[lax.rem(z - d + count, count)]
        pltpu.make_async_remote_copy(
            src_ref=ref, dst_ref=ref, send_sem=sm_ss.at[d], recv_sem=sm_rs.at[d], device_id=(b, peer),
            device_id_type=MESH,
        ).wait_recv()
    small_own.wait()
    blocks = [None] * 6
    for t in range(count):
        first = t * cols // width
        for i in range(2):
            if first + i < 6:
                part = sm_recv[t, i]
                blocks[first + i] = part if blocks[first + i] is None else blocks[first + i] + part
    for i in range(6):
        mod_o[i] = blocks[i]
    qv_bias = sm_recv[0, 2]
    for t in range(1, count):
        qv_bias = qv_bias + sm_recv[t, 2]
    for l in range(lat):
        at = slice(l * slots, (l + 1) * slots)
        attn_in_o[at] = (nrm[at] * (1.0 + mod_o[1, l : l + 1]) + mod_o[0, l : l + 1]).astype(BF)
        dmlp_o[0, at] = (cot_o[at].astype(F32) * mod_o[5, l : l + 1]).astype(BF)

    for k in range(1, count - 1):
        arrive_a(k)
        if k == 1:
            both_ways(send_m)
        gathers[k - 1].step(1)
    depth = gathers[0].steps()
    todo = [(i, k) for k in range(count - 1) for i in range(1, depth) if not (i == 1 and k < count - 2)]
    half_rows = slots * lat // 2

    def dm_region(m, p, slot):
        return dmlp_o.at[slot, pl.ds(p * half_rows, half_rows)]

    dm = Gather(b, z, group, dm_region, lambda m, p: gd_ss.at[p, m], lambda m, p: gd_rs.at[p, m])
    links = depth - 1
    todo.sort(key=lambda item: (item[0] >= links, item[0] + item[1], item[1]))
    started = False
    for i, k in todo:
        if i >= links and not started:
            dm.step(0)
            arrive_m(0)
            started = True
        gathers[k].step(i)
    for k in range(count - 1):
        gathers[k].wait_core()
    full_out = pltpu.make_async_copy(full, full_o, loc.at[4])
    full_out.start()

    for k in range(1, count - 2):
        arrive_m(k)
    dm.step(1)

    x = attn_in_o[...]
    for j, out in enumerate((q_o, k_o, v_o)):
        y = nt(x, full[j].reshape(width, width))
        if j != 1:
            y = y + qv_bias[j // 2 : j // 2 + 1]
        out[...] = y.astype(BF)

    scale = HEAD_SIZE**-0.5

    heads = width // HEAD_SIZE

    def some_heads(step, _):
        for h in (step, step + heads // 2):
            win, own = head_window(h, width)
            for l in range(lat):
                at = pl.ds(l * slots, slots)
                q = (q_o[at, win].astype(F32) * own).astype(BF)
                s = nt(q, k_o[at, win]) * scale
                key = lax.broadcasted_iota(jnp.int32, (1, slots), 1)
                s = jnp.where(key < real_ref[z * lat + l], s, -1000000000.0)
                w = jnp.exp(s - jnp.max(s, axis=-1, keepdims=True))
                pr = (w / jnp.sum(w, axis=-1, keepdims=True)).astype(BF)
                o = nn(pr, v_o[at, win])
                mg[at, win] = jnp.where(own > 0, o, mg[at, win])
        return 0

    lax.fori_loop(0, heads // 2, some_heads, 0)
    for i in range(2, dm.steps()):
        dm.step(i)
    merged_o[...] = mg[...].astype(BF)
    a_out = nn(merged_o[...], full[3].reshape(width, width)) + projb_ref[...].astype(F32)
    attn_out_o[...] = a_out
    for l in range(lat):
        at = slice(l * slots, (l + 1) * slots)
        rows = sel[at] + mod_o[2, l : l + 1] * attn_out_o[at]
        hidden_o[at] = rows
        center, inv = stats(rows)
        mlp_in_o[at] = (center * inv * (1.0 + mod_o[4, l : l + 1]) + mod_o[3, l : l + 1]).astype(BF)

    arrive_m(count - 2)
    dm.wait_core()
    for d in range(1, count):
        small(d).wait_send()
    both_ways(lambda step, k: line_a(z, piece(g, z, None), step, k).wait_send())

    def sent_m(step, k):
        for cp in line_m(z, all_1.at[z], all_2.at[z], step, k):
            cp.wait_send()

    both_ways(sent_m)
    for k in range(count - 1):
        shard = near_shard(z, k, count)

        @pl.when(((shard < z) & (z < count - 1)) | ((shard > z) & (z > 0)))
        def _():
            line_a(shard, piece(g, shard, None), 0, 2 + k).wait_send()
            for cp in line_m(shard, all_1.at[shard], all_2.at[shard], 0, 2 + k):
                cp.wait_send()

        gathers[k].wait_sent()
    dm.wait_sent()
    full_out.wait()


def run_first(dims, lat, real, cond, wada, abias, tok, cot, kept, qvb, projb, own_qkv, own_proj, own_1, own_2):
    group, count, rows_s, width = dims
    slots = kept.shape[1]
    rows = lat * slots
    vm = pl.BlockSpec(memory_space=pltpu.VMEM)
    hb = pl.BlockSpec(memory_space=pl.ANY)
    sm = pl.BlockSpec(memory_space=pltpu.SMEM)
    sd = jax.ShapeDtypeStruct
    row_bf, row_f = sd((rows, width), BF), sd((rows, width), F32)
    dma = pltpu.SemaphoreType.DMA
    return pl.pallas_call(
        functools.partial(first_kernel, dims, lat),
        out_shape=(
            row_bf, row_bf, row_bf, row_bf, row_bf, row_f, row_f, row_bf, row_bf, sd((6, lat, width), F32),
            sd((4, count, width // count, width), BF),
            sd((count, rows_s, own_1.shape[1]), BF),
            sd((count, rows_s, width), BF),
            sd((group, rows, width), BF),
        ),
        in_specs=[sm] + [vm] * 8 + [hb] * 4,
        out_specs=tuple([vm] * 10 + [hb] + [vm] * 3),
        scratch_shapes=[
            pltpu.VMEM((4, count, width // count, width), BF),
            pltpu.VMEM((count, 3, lat, width), F32),
            pltpu.VMEM((count, 3, lat, width), F32),
            pltpu.VMEM((rows, width), F32),
            pltpu.VMEM((rows, width), F32),
            pltpu.VMEM((rows, width), F32),
            pltpu.VMEM((cond.shape[0], 2 * width), F32),
            dma((count,)), dma((count,)),
            dma((count + 1,)), dma((count,)),
            dma((2, count + 1)), dma((2, count)),
            dma((count - 1, 2, group)), dma((count, 2, group)),
            dma((2, group)), dma((2, group)),
            dma((6,)),
        ],
        compiler_params=pltpu.CompilerParams(collective_id=1, has_side_effects=True, vmem_limit_bytes=56 * MIB),
        name="forward_attention",
    )(real, cond, wada, abias, tok, cot, kept, qvb, projb, own_qkv, own_proj, own_1, own_2)


GELU_C = 0.7978845608028654


def gelu_pair(v):
    sq = v * v
    t = jnp.tanh(GELU_C * v * (1.0 + 0.044715 * sq))
    half = 0.5 + 0.5 * t
    slope = half + 0.5 * GELU_C * v * (1.0 - t * t) * (1.0 + 3 * 0.044715 * sq)
    return v * half, slope


def middle_kernel(
    dims, x_ref, d_ref, w1_ref, w2_ref,
    din_o, out_o, g1_o, g2_o,
    xb, act, dpre, y, inbox, yo, inbox_o,
    ag_ss, ag_rs, rs_ss, rs_rs, ro_ss, ro_rs,
):
    group, count, rows_s, width = dims
    b, z = lax.axis_index("batch"), lax.axis_index("tp")
    rows = x_ref.shape[0]
    half = rows // 2
    hid = w1_ref.shape[0]
    xb[0] = x_ref[...]
    barrier(b, z, group, count)

    def part(ref):
        return lambda m, p: ref.at[m, pl.ds(p * half, half)]

    gather = Gather(
        b, z, group, lambda m, p, slot: part(xb)(slot, p), lambda m, p: ag_ss.at[p, m], lambda m, p: ag_rs.at[p, m]
    )
    gather.step(0)
    bias = nt(jnp.ones((8, w1_ref.shape[1] - width), BF), w1_ref[:, width:])[0:1]

    def forward(pair):
        (m0, p0), (m1, p1) = pair
        at = [(m0, slice(p0 * half, (p0 + 1) * half)), (m1, slice(p1 * half, (p1 + 1) * half))]
        x = jnp.concatenate([xb[m, s] for m, s in at], axis=0)
        d = jnp.concatenate([d_ref[m, s] for m, s in at], axis=0)
        a, slope = gelu_pair(nt(x, w1_ref[:, 0:width]) + bias)
        dp = (slope * nt(d, w2_ref[...])).astype(BF)
        a = a.astype(BF)
        for i, (m, s) in enumerate(at):
            to = slice(m * rows + s.start, m * rows + s.stop)
            act[to] = a[i * half : (i + 1) * half]
            dpre[to] = dp[i * half : (i + 1) * half]

    forward(((0, 0), (0, 1)))
    for p in range(2):
        gather.wait(1, p)
    forward(((1, 0), (1, 1)))
    for i in range(1, gather.steps()):
        gather.step(i)
        fresh = [[m ^ order[i - 1] for m in span(order[: i - 1])] for order in gather.orders]
        for m0, m1 in zip(*fresh):
            forward(((m0, 0), (m1, 1)))
        for m0, m1 in zip(*fresh):
            gather.wait(m0 ^ 1, 0)
            gather.wait(m1 ^ 1, 1)
            forward(((m0 ^ 1, 0), (m1 ^ 1, 1)))

    def reduction(own, boxes, ss, rs):
        mine, arrived = part(own), part(boxes)

        def add(m, key, p):
            mine(m, p)[...] = (mine(m, p)[...].astype(F32) + arrived(key, p)[...].astype(F32)).astype(BF)

        return Scatter(b, z, group, mine, arrived, lambda m, p: ss.at[p, m], lambda m, p: rs.at[p, m], add)

    rs_in = reduction(y, inbox, rs_ss, rs_rs)
    rs_out = reduction(yo, inbox_o, ro_ss, ro_rs)
    links = len(rs_in.orders[0])

    def part_in(m):
        y[m] = nn(dpre[m * rows : (m + 1) * rows], w1_ref[:, 0:width]).astype(BF)

    def part_out(m):
        yo[m] = nn(act[m * rows : (m + 1) * rows], w2_ref[...]).astype(BF)

    def send_core(rs, make):
        for m in range(group - 1, 0, -2):
            make(m)
            for p in range(2):
                rs.send(m, p)

    def last_link(rs, m):
        for p in range(2):
            if rs.top(m, p) == rs.orders[p][-1]:
                rs.fold(m, p)
                rs.send(m, p)

    def next_link(rs, i):
        for p in range(2):
            order = rs.orders[p]
            for m in span(order[: i - 1]):
                rs.fold(m ^ order[i - 1], p)
                rs.send(m ^ order[i - 1], p)

    def finish(rs, out):
        for p in range(2):
            total = rs.mine(0, p)[...].astype(F32)
            for key in rs.keys(0, p):
                rs.copy(key, p).wait_recv()
                total = total + rs.inbox(key, p)[...].astype(F32)
            out[p * half : (p + 1) * half] = total

    chunks = [slice(c, min(c + 128, hid)) for c in range(0, hid, 128)]

    def grads_1():
        ones = jnp.ones((group * rows, g1_o.shape[1] - width), BF)
        x = xb[...].reshape(group * rows, width)
        for c in chunks:
            g1_o[c, 0:width] = tn(dpre[:, c], x).astype(BF)
            g1_o[c, width:] = tn(dpre[:, c], ones).astype(BF)

    def grads_2():
        d = d_ref[...].reshape(group * rows, width)
        for c in chunks:
            g2_o[c] = tn(act[:, c], d).astype(BF)

    send_core(rs_in, part_in)
    for m in range(group - 2, 0, -2):
        part_in(m)
        last_link(rs_in, m)
    part_in(0)
    send_core(rs_out, part_out)
    for m in range(group - 2, -1, -2):
        part_out(m)
    for i in range(links - 1, 0, -1):
        next_link(rs_in, i)
    for m in range(group - 2, 0, -2):
        last_link(rs_out, m)
    grads_1()
    finish(rs_in, din_o)
    grads_2()
    for i in range(links - 1, 0, -1):
        next_link(rs_out, i)
    finish(rs_out, out_o)
    gather.wait_sent()
    rs_in.wait_sent()
    rs_out.wait_sent()


def run_middle(dims, x, d_all, w1, w2):
    group, count, rows_s, width = dims
    rows, hid = x.shape[0], w1.shape[0]
    vm = pl.BlockSpec(memory_space=pltpu.VMEM)
    sd = jax.ShapeDtypeStruct
    dma = pltpu.SemaphoreType.DMA
    blocks = pltpu.VMEM((group, rows, width), BF)
    return pl.pallas_call(
        functools.partial(middle_kernel, dims),
        out_shape=(
            sd((rows, width), F32), sd((rows, width), F32), sd(w1.shape, BF), sd(w2.shape, BF),
        ),
        in_specs=[vm] * 4,
        out_specs=tuple([vm] * 4),
        scratch_shapes=[
            blocks, pltpu.VMEM((group * rows, hid), BF), pltpu.VMEM((group * rows, hid), BF), blocks, blocks,
            blocks, blocks,
            dma((2, group)), dma((2, group)), dma((2, group)), dma((2, group)), dma((2, group)), dma((2, group)),
        ],
        compiler_params=pltpu.CompilerParams(collective_id=2, has_side_effects=True, vmem_limit_bytes=58 * MIB),
        name="feed_forward",
    )(x, d_all, w1, w2)


def last_kernel(
    dims, lat, real_ref, kept_ref, tok_ref, cot_in_ref, attn_in_ref, q_ref, k_ref, v_ref, merged_ref,
    attn_out_ref, hidden_ref, cot_ref, mod_ref, d_in_ref, mlp_out_ref, redb_ref, cond_ref,
    full_ref, g1_ref, g2_ref,
    out_o, dtok_o, ga_o, gm1_o, gm2_o, small_o,
    wbuf, gbuf, abox, ar, gm1, gm2, mr1, mr2, back_b, d3, d_attn, dm, dain, sm_send, sm_recv, dmod,
    loc, ra_ss, ra_rs, za_ss, za_rs, zm_ss, zm_rs, gm_ss, gm_rs, ga_ss, ga_rs, sz_ss, sz_rs, sp_ss, sp_rs,
):
    group, count, rows_s, width = dims
    b, z = lax.axis_index("batch"), lax.axis_index("tp")
    g = b % group
    ds = width // count
    slots = kept_ref.shape[1]
    scale = HEAD_SIZE**-0.5
    loads = [
        pltpu.make_async_copy(g1_ref, gm1, loc.at[0]),
        pltpu.make_async_copy(g2_ref, gm2, loc.at[1]),
        pltpu.make_async_copy(full_ref.at[3], wbuf.at[0], loc.at[2]),
        pltpu.make_async_copy(full_ref.at[0], wbuf.at[1], loc.at[3]),
    ]
    for cp in loads:
        cp.start()
    barrier(b, z, group, count)
    cut = (rows_s // 2 + 15) // 16 * 16
    parts = ((0, cut), (cut, rows_s - cut))

    loads[0].wait()
    loads[1].wait()

    def line_m(d):
        peer = lax.rem(z + d, count)
        at = pl.ds(pl.multiple_of(peer * rows_s, 16), rows_s)
        return [
            pltpu.make_async_remote_copy(
                src_ref=src.at[at], dst_ref=dst.at[d], send_sem=zm_ss.at[i, d], recv_sem=zm_rs.at[i, d],
                device_id=(b, peer), device_id_type=MESH,
            )
            for i, (src, dst) in enumerate(((gm1, mr1), (gm2, mr2)))
        ]

    for d in range(1, count):
        for cp in line_m(d):
            cp.start()

    def rows_of(l):
        return slice(l * slots, (l + 1) * slots)

    def back(n, inv, grad):
        return (grad - jnp.mean(grad, axis=-1, keepdims=True) - n * jnp.mean(grad * n, axis=-1, keepdims=True)) * inv

    def total(rows):
        return jnp.sum(rows, axis=0, keepdims=True)

    valid = []
    for l in range(lat):
        at = rows_of(l)
        one = slice(l, l + 1)
        row = lax.broadcasted_iota(jnp.int32, (slots, 1), 0)
        valid.append(jnp.where(row < real_ref[z * lat + l], 1.0, 0.0))
        center, inv = stats(hidden_ref[at])
        n = center * inv
        d_in = d_in_ref[at]
        cot = cot_ref[at].astype(F32)
        back_b[at] = back(n, inv, d_in * (1.0 + mod_ref[4, one]))
        d_hidden = cot + back_b[at]
        d_attn[at] = (mod_ref[2, one] * d_hidden).astype(BF)
        dmod[3, one] = total(d_in)
        dmod[4, one] = total(d_in * n)
        dmod[2, one] = total(d_hidden * attn_out_ref[at])
        mlp_out = mlp_out_ref[at] + redb_ref[...].astype(F32)
        dmod[5, one] = total(cot * mlp_out)

    loads[2].wait()
    dm[...] = nt(d_attn[...], wbuf[0]).astype(BF)
    load_k = pltpu.make_async_copy(full_ref.at[1], wbuf.at[0], loc.at[2])
    load_k.start()
    chunk = 384

    def weight_grad(j, left, right):
        for c in range(0, width, chunk):
            to = slice(c, c + chunk)
            gbuf[j, to] = tn(left(to), right).astype(BF)

    weight_grad(3, lambda to: merged_ref[:, to], d_attn[...])

    heads = width // HEAD_SIZE

    def some_heads(step, _):
        for h in (step, step + heads // 2):
            win, own = head_window(h, width)
            for l in range(lat):
                at = pl.ds(l * slots, slots)
                q, k, v, dmh = q_ref[at, win], k_ref[at, win], v_ref[at, win], dm[at, win]
                s = nt((q.astype(F32) * own).astype(BF), k) * scale
                key = lax.broadcasted_iota(jnp.int32, (1, slots), 1)
                s = jnp.where(key < real_ref[z * lat + l], s, -1000000000.0)
                w = jnp.exp(s - jnp.max(s, axis=-1, keepdims=True))
                pr = w / jnp.sum(w, axis=-1, keepdims=True)
                dp = nt((dmh.astype(F32) * own).astype(BF), v)
                dsc = (pr * (dp - jnp.sum(pr * dp, axis=-1, keepdims=True))).astype(BF)
                for j, grad in enumerate(
                    (nn(dsc, k) * scale, tn(dsc, q) * scale, tn(pr.astype(BF), dmh))
                ):
                    d3[j, at, win] = jnp.where(own > 0, grad, d3[j, at, win].astype(F32)).astype(BF)
        return 0

    lax.fori_loop(0, heads // 2, some_heads, 0)

    for j in range(3):
        weight_grad(j, lambda to, j=j: d3[j, :, to], attn_in_ref[...])

    def wave_shard(w):
        return lax.rem(z + 1 + w, count)

    waves = []
    for w in range(count):
        def mine(m, p, w=w):
            at = flip(g, m) * rows_s
            lo, ln = parts[p]
            return gbuf.at[at // ds, pl.ds(pl.multiple_of(ds * wave_shard(w) + at % ds + lo, 16), ln)]

        def box(m, p, w=w):
            lo, ln = parts[p]
            return abox.at[w, m - 1, pl.ds(lo, ln)]

        def add(m, key, p, mine=mine, box=box):
            mine(m, p)[...] = (mine(m, p)[...].astype(F32) + box(key, p)[...].astype(F32)).astype(BF)

        waves.append(
            Scatter(b, z, group, mine, box, lambda m, p, w=w: ra_ss.at[w, p, m], lambda m, p, w=w: ra_rs.at[w, p, m], add)
        )
    links = len(waves[0].orders[0])

    def own_slice(shard):
        at = g * rows_s
        return gbuf.at[at // ds, pl.ds(pl.multiple_of(ds * shard + at % ds, 16), rows_s)]

    def line_a(w):
        return pltpu.make_async_remote_copy(
            src_ref=own_slice(wave_shard(w)), dst_ref=ar.at[w], send_sem=za_ss.at[w], recv_sem=za_rs.at[w],
            device_id=(b, wave_shard(w)), device_id_type=MESH,
        )

    def wave_step(w, st):
        rs = waves[w]
        if 0 <= st < links:
            for p in range(2):
                order = rs.orders[p]
                i = links - st
                for m in span(order[: i - 1]):
                    rs.fold(m ^ order[i - 1], p)
                    rs.send(m ^ order[i - 1], p)
        elif st == links:
            for p in range(2):
                rs.fold(0, p)
            if w < count - 1:
                line_a(w).start()

    for rs in waves:
        for m in range(group - 1, 0, -2):
            for p in range(2):
                rs.send(m, p)

    def wave_round(t):
        for w in range(count):
            wave_step(w, t - w)

    loads[3].wait()
    dain[...] = nn(d3[0], wbuf[1])
    load_v = pltpu.make_async_copy(full_ref.at[2], wbuf.at[1], loc.at[3])
    load_v.start()
    wave_round(0)
    load_k.wait()
    dain[...] += nn(d3[1], wbuf[0])
    load_v.wait()
    dain[...] += nn(d3[2], wbuf[1])
    wave_round(1)

    place = lax.broadcasted_iota(jnp.int32, (slots, tok_ref.shape[1]), 1)

    def put(pick, rows):
        high = rows.astype(BF)
        return tn(pick, high) + tn(pick, (rows - high.astype(F32)).astype(BF))

    for l in range(lat):
        at = rows_of(l)
        one = slice(l, l + 1)
        pick = jnp.where(place == kept_ref[l], 1.0, 0.0).astype(BF)
        center, inv = stats(nn(pick, tok_ref[l]))
        n = center * inv
        d_ai = dain[at]
        dmod[0, one] = total(d_ai)
        dmod[1, one] = total(d_ai * n)
        d_sel = back_b[at] + back(n, inv, d_ai * (1.0 + mod_ref[1, one]))
        dtok_o[l] = (cot_in_ref[l].astype(F32) + put(pick, d_sel)).astype(BF)

    cols = 6 * width // count
    vectors = [
        sum(total((cot_ref[rows_of(l)].astype(F32) * mod_ref[5, l : l + 1]).astype(BF).astype(F32)) for l in range(lat)),
        total(d_attn[...].astype(F32)),
        total(d3[0].astype(F32)),
        total(d3[2].astype(F32)),
    ]
    for t in range(count):
        first = t * cols // width
        for i in range(2):
            sm_send[t, i] = dmod[min(first + i, 5)]
        for i in range(4):
            sm_send[t, 2 + i // 2, i % 2 : i % 2 + 1] = vectors[i]

    def small(d):
        peer = lax.rem(z + d, count)
        return pltpu.make_async_remote_copy(
            src_ref=sm_send.at[peer], dst_ref=sm_recv.at[z], send_sem=sz_ss.at[d], recv_sem=sz_rs.at[d],
            device_id=(b, peer), device_id_type=MESH,
        )

    for d in range(1, count):
        small(d).start()
    small_own = pltpu.make_async_copy(sm_send.at[z], sm_recv.at[z], loc.at[4])
    small_own.start()
    wave_round(2)
    for l in range(lat):
        at = rows_of(l)
        one = slice(l, l + 1)
        pick = jnp.where(place == kept_ref[l], 1.0, 0.0).astype(BF)
        mlp_out = mlp_out_ref[at] + redb_ref[...].astype(F32)
        delta = (mod_ref[2, one] * attn_out_ref[at] + mod_ref[5, one] * mlp_out) * valid[l]
        out_o[l] = (tok_ref[l].astype(F32) + put(pick, delta)).astype(BF)
    for d in range(1, count):
        ref = sm_recv.at[lax.rem(z - d + count, count)]
        pltpu.make_async_remote_copy(
            src_ref=ref, dst_ref=ref, send_sem=sz_ss.at[d], recv_sem=sz_rs.at[d],
            device_id=(b, lax.rem(z + d, count)), device_id_type=MESH,
        ).wait_recv()
    small_own.wait()
    small_o[0] = jnp.zeros(small_o.shape[1:], F32)
    for i in range(2):
        for t in range(count):
            small_o[0, i, lat * t : lat * (t + 1)] = sm_recv[t, i]
    for i in range(2):
        acc = sm_recv[0, 2 + i]
        for t in range(1, count):
            acc = acc + sm_recv[t, 2 + i]
        small_o[0, 2, lat * i : lat * (i + 1)] = acc
    cond = cond_ref[...].astype(F32)
    small_o[0, 3] = (cond / (1.0 + jnp.exp(-cond))).astype(BF).astype(F32)
    sp = Gather(
        b, z, group, lambda m, p, slot: small_o.at[slot], lambda m, p: sp_ss.at[m], lambda m, p: sp_rs.at[m], halves=1
    )
    sp.step(0)
    for t in range(3, count + links):
        wave_round(t)
        if t - 2 < sp.steps():
            sp.step(t - 2)

    def spread(out, ss, rs):
        def region(m, p, slot):
            lo, ln = parts[p]
            return out.at[pl.ds(pl.multiple_of(flip(g, m) * rows_s + lo, 16), ln)]

        return Gather(b, z, group, region, lambda m, p: ss.at[p, m], lambda m, p: rs.at[p, m])

    g_at = pl.ds(pl.multiple_of(g * rows_s, 16), rows_s)
    z_at = pl.ds(pl.multiple_of(z * rows_s, 16), rows_s)
    acc = own_slice(z)[...].astype(F32)
    for w in range(count - 1):
        line_a(w).wait_recv()
        acc = acc + ar[w].astype(F32)
    ga_o[g_at] = acc.astype(BF)
    spread_a = spread(ga_o, ga_ss, ga_rs)
    spread_a.step(0)
    for d in range(1, count):
        for cp in line_m(d):
            cp.wait_recv()
    for own, box, out in ((gm1, mr1, gm1_o), (gm2, mr2, gm2_o)):
        acc = own[z_at].astype(F32)
        for d in range(1, count):
            acc = acc + box[d].astype(F32)
        out[g_at] = acc.astype(BF)
    spread_1 = spread(gm1_o, gm_ss.at[0], gm_rs.at[0])
    spread_2 = spread(gm2_o, gm_ss.at[1], gm_rs.at[1])
    spread_1.step(0)
    spread_2.step(0)
    for i in range(1, spread_a.steps()):
        for item in (spread_a, spread_1, spread_2):
            item.step(i)
    for i in range(max(1, count + links - 2), sp.steps()):
        sp.step(i)
    for item in (sp, spread_a, spread_1, spread_2):
        item.wait_core()
        item.wait_sent()
    for rs in waves:
        rs.wait_sent()
    for w in range(count - 1):
        line_a(w).wait_send()
    for d in range(1, count):
        small(d).wait_send()
        for cp in line_m(d):
            cp.wait_send()


def run_last(dims, lat, real, kept, tok, cot_in, attn_in, q, k, v, merged, attn_out, hidden, cot, mod, d_in, mlp_out, redb, cond, full, g1, g2):
    group, count, rows_s, width = dims
    rows = attn_in.shape[0]
    vm = pl.BlockSpec(memory_space=pltpu.VMEM)
    hb = pl.BlockSpec(memory_space=pl.ANY)
    sm = pl.BlockSpec(memory_space=pltpu.SMEM)
    sd = jax.ShapeDtypeStruct
    dma = pltpu.SemaphoreType.DMA
    ext = g1.shape[1]
    small = (group, 4, cond.shape[0], width)
    return pl.pallas_call(
        functools.partial(last_kernel, dims, lat),
        out_shape=(
            sd(tok.shape, BF), sd(tok.shape, BF), sd((group * rows_s, width), BF),
            sd((group * rows_s, ext), BF), sd((group * rows_s, width), BF), sd(small, F32),
        ),
        in_specs=[sm] + [vm] * 16 + [hb] * 3,
        out_specs=tuple([vm] * 6),
        scratch_shapes=[
            pltpu.VMEM((2, width, width), BF),
            pltpu.VMEM((4, width, width), BF),
            pltpu.VMEM((count, group - 1, rows_s, width), BF),
            pltpu.VMEM((count, rows_s, width), BF),
            pltpu.VMEM(g1.shape, BF), pltpu.VMEM(g2.shape, BF),
            pltpu.VMEM((count, rows_s, ext), BF), pltpu.VMEM((count, rows_s, width), BF),
            pltpu.VMEM((rows, width), F32),
            pltpu.VMEM((3, rows, width), BF),
            pltpu.VMEM((rows, width), BF), pltpu.VMEM((rows, width), BF),
            pltpu.VMEM((rows, width), F32),
            pltpu.VMEM((count, 4, lat, width), F32), pltpu.VMEM((count, 4, lat, width), F32),
            pltpu.VMEM((6, lat, width), F32),
            dma((5,)),
            dma((count, 2, group)), dma((count, 2, group)),
            dma((count,)), dma((count,)),
            dma((2, count)), dma((2, count)),
            dma((2, 2, group)), dma((2, 2, group)),
            dma((2, group)), dma((2, group)),
            dma((count,)), dma((count,)),
            dma((group,)), dma((group,)),
        ],
        compiler_params=pltpu.CompilerParams(collective_id=3, has_side_effects=True, vmem_limit_bytes=63 * MIB),
        name="backward_attention",
    )(real, kept, tok, cot_in, attn_in, q, k, v, merged, attn_out, hidden, cot, mod, d_in, mlp_out, redb, cond, full, g1, g2)


def own_frame(part, total, axis):
    size = part.shape[-1]
    frame = jnp.zeros(part.shape[:-1] + (total,), F32)
    return lax.dynamic_update_slice_in_dim(frame, part.astype(F32), lax.axis_index("tp") * size, frame.ndim - 1)


def body(
    tokens, conditioning, bucket, kept_index, w_ada, ada_bias, w_qkv, qv_bias, w_proj, proj_bias,
    w_expand, expand_bias, w_reduce, reduce_bias, out_grad, count, batch,
):
    lat, positions, width = tokens.shape
    shard_w, shard_f = w_qkv.shape[2], w_expand.shape[1]
    group = group_size(shard_f, shard_w)
    rows_s = shard_f // group
    dims = (group, count, rows_s, width)
    real = (positions - positions // 16 * (bucket > 0).astype(jnp.int32)) // 2
    own_1 = jnp.concatenate(
        [w_expand.T, jnp.pad(expand_bias[:, None], ((0, 0), (0, 127)))], axis=1
    )
    out1 = run_first(
        dims, lat, real, conditioning, w_ada.T, ada_bias[None], tokens, out_grad, kept_index[:, :, None],
        own_frame(qv_bias, width, "tp"), proj_bias[None], jnp.swapaxes(w_qkv, 1, 2), w_proj, own_1, w_reduce,
    )
    (attn_in, queries, key_rows, value_rows, merged, attn_out, hidden, mlp_in, cot, mod, full, all_1, all_2, d_all) = out1
    flat = lambda a: a.reshape((-1,) + a.shape[2:])
    d_in, mlp_out, g1, g2 = run_middle(dims, mlp_in, d_all, flat(all_1), flat(all_2))
    output, tokens_grad, ga, gm1, gm2, small = run_last(
        dims, lat, real, kept_index[:, :, None], tokens, out_grad, attn_in, queries, key_rows, value_rows, merged,
        attn_out, hidden, cot, mod, d_in, mlp_out, reduce_bias[None], conditioning,
        full.reshape(4, width, width), g1, g2,
    )

    cols = 6 * width // count
    start = lax.axis_index("tp") * cols % width
    pair = jnp.concatenate([flat(small[:, 0]), flat(small[:, 1])], axis=1)
    d_mod = lax.dynamic_slice_in_dim(pair, start, cols, 1)
    ada_grad = tn(flat(small[:, 3]).astype(BF), d_mod.astype(BF))
    ada_add_grad = jnp.sum(d_mod, axis=0)
    sums = jnp.sum(small[:, 2, 0:4], axis=0)
    pair_grad = lax.dynamic_slice_in_dim(sums[2:4], lax.axis_index("tp") * shard_w, shard_w, 1)
    grads = (
        ada_grad, ada_add_grad, ga, gm1, gm2, pair_grad, sums[0], sums[1],
    )
    if batch > group:
        grads = tuple(lax.psum(item * (1.0 / group), "batch") for item in grads)
    ada_grad, ada_add_grad, ga, gm1, gm2, pair_grad, reduce_add, proj_add = grads
    ga = ga.reshape(4, shard_w, width)
    return (
        output,
        tokens_grad,
        ada_grad,
        ada_add_grad,
        jnp.swapaxes(ga[:3], 1, 2).astype(F32),
        pair_grad,
        ga[3].astype(F32),
        proj_add,
        gm1[:, :width].T.astype(F32),
        gm1[:, width].astype(F32),
        gm2.astype(F32),
        reduce_add,
    )


def solution(mesh):
    rows = P(("batch", "tp"), None, None)
    return jax.shard_map(
        functools.partial(body, count=mesh.shape["tp"], batch=mesh.shape["batch"]),
        mesh=mesh,
        in_specs=(
            rows, P("batch", None), P("batch"), P(("batch", "tp"), None), P(None, "tp"), P("tp"),
            P(None, None, "tp"), P(None, "tp"), P("tp", None), P(), P(None, "tp"), P("tp"), P("tp", None), P(), rows,
        ),
        out_specs=(
            rows, rows, P(None, "tp"), P("tp"), P(None, None, "tp"), P(None, "tp"), P("tp", None), P(),
            P(None, "tp"), P("tp"), P("tp", None), P(),
        ),
        check_vma=False,
    )
```

time: 694 us -> 383 us (0.55)
  the two profiles are of different devices: /device:TPU:17 before, /device:TPU:27 now
where the time goes in v1:
time: 383 us; the launch traced here: 378 us
  Pallas kernels  329 us (86%)
  local copies, waits for them, and re-layouts  23.8 us (6%)
  other arithmetic  17.4 us (5%)
  matrix products  5.9 us (2%)
    pallas_call x1, Pallas kernels, run_last(): pl.pallas_call(functools.partial(last_kernel, dims, lat), out_shape=(sd(t...  155 us
    pallas_call x1, Pallas kernels, run_first(): pl.pallas_call(functools.partial(first_kernel, dims, lat), out_shape=(row...  95.9 us
    pallas_call x1, Pallas kernels, run_middle(): pl.pallas_call(functools.partial(middle_kernel, dims), out_shape=(sd((row...  78.6 us
    unnamed x16, local copies, waits for them, and re-layouts  14.8 us

profile of v1, /device:TPU:27, one launch (start us, length us, event | category | flops | bytes accessed | tf_op | source)
XLA Modules:
  0.0 377.5 jit_solution(8483792851969308067)
XLA Ops:
  0.7 1.2 and_select_fusion.real_ref
  2.5 1.3 broadcast_in_dim.22.projb_ref
  3.8 1.3 broadcast_in_dim.24.redb_ref
  5.1 1.3 broadcast_in_dim.20.abias_ref
  6.6 1.5 copy.32.kept_ref
  8.1 0.9 broadcast_in_dim.25
  9.0 4.1 %copy.29 = bf16[1152,1152]{0,1:T(8,128)(2,1)S(1)} copy(bf16[1152,1152]{1,0:T(8,128)(2,1)} %param.25) | data formatting | bytes 5308416 | tf_op args[10]
  13.1 1.8 fusion.1.own_1
  15.0 95.9 %forward_attention.1 = (bf16[256,1152]{1,0:T(8,128)(2,1)}, bf16[256,1152]{1,0:T(8,128)(2,1)}, bf16[256,1152]{1,0:T(8,128)(2,1)}, bf16[256,1152]{1,0:T(8,128)(2,1...) custom-call(s32[8]{0:T(128)} %and_select_fusion.real_ref, ...), custom_call_target="tpu_custom_call" | custom-call | tf_op jit(solution)/shard_map/forward_attention/pallas_call | solution.py:480
  110.9 78.6 %feed_forward.1 = (f32[256,1152]{1,0:T(8,128)}, f32[256,1152]{1,0:T(8,128)}, bf16[576,1280]{1,0:T(8,128)(2,1)}, bf16[576,1152]{1,0:T(8,128)(2,1)}) custom-call(bf16[256,1152]{1,0:T(8,128)(2,1)} %get-tuple-element.45.x_ref, bf16[8,256,1152]{2,1,0:T(8,128)(2,1)} %get-tuple-element.46.d_ref, bf16[576,1280]{1,0:T(8,128)(2,1)} %bitcast.25, bf16[576,1152]{1,0:T(8,128)(2,1)} %bitcast.26), custom_call_target="tpu_custom_call" | custom-call | tf_op jit(solution)/shard_map/feed_forward/pallas_call | solution.py:661
  189.5 154.6 %backward_attention.1 = (bf16[2,256,1152]{2,1,0:T(8,128)(2,1)}, bf16[2,256,1152]{2,1,0:T(8,128)(2,1)}, bf16[1152,1152]{1,0:T(8,128)(2,1)}, bf16[1152,1280]{1,0:T...) custom-call(s32[8]{0:T(128)} %and_select_fusion.real_ref, s32[2,128,1]{2,1,0:T(8,128)} %copy.32.kept_ref, ...), custom_call_target="tpu_custom_call" | custom-call | tf_op jit(solution)/shard_map/backward_attention/pallas_call | solution.py:990
  344.1 1.9 convert_reduce_fusion
  346.0 1.0 slice_reduce_fusion
  348.3 1.1 slice_bitcast_fusion
  349.4 0.9 fusion.8
  350.3 2.2 slice_convert_fusion
  352.7 2.3 convert_bitcast_fusion.1
  355.0 1.0 copy-done
  355.9 2.7 convert_bitcast_fusion
  358.7 7.0 %copy.33 = f32[1152,1152]{1,0:T(8,128)} copy(f32[1152,1152]{0,1:T(8,128)} %convert_bitcast_fusion) | data formatting | bytes 10616832
  365.7 2.7 convert_element_type.51
  368.4 5.9 %fusion.3 = f32[1152,1728]{0,1:T(8,128)} fusion(f32[8,4,8,1152]{3,2,1,0:T(8,128)} %get-tuple-element.56, s32[]{:T(128)S(6)} %select_n.22, f32[64,1152]{1,0:T(8,128)S(1)} %get-tuple-element.87, f32[64,1152]{1,0:T(8,128)S(1)} %get-tuple-element.86), kind=kOutput, calls=%fused_computation.13 | convolution fusion | flops 255246336 | bytes 8699908 | tf_op jit(solution)/shard_map/dot_general | solution.py:26
  374.3 1.0 copy.37
  376.0 1.0 copy.38
  (18 shorter events, 3.1 us)
Async XLA Ops:
  6.6 6.5 %copy-start.5 = (f32[2,1152]{1,0:T(2,128)}, f32[2,1152]{1,0:T(2,128)S(1)}, u32[]{:S(2)}) copy-start(f32[2,1152]{1,0:T(2,128)S(1)} %dynamic_update_slice.3.qvb_ref) | copy-start | bytes 27652
  344.1 8.4 %copy-start.1 = (bf16[1152,1152]{1,0:T(8,128)(2,1)S(1)}, bf16[1152,1152]{1,0:T(8,128)(2,1)}, u32[]{:S(2)}) copy-start(bf16[1152,1152]{1,0:T(8,128)(2,1)} %get-tuple-element.57) | copy-start | bytes 7962628
  352.7 3.3 copy-start
  358.7 7.0 %copy-start.2 = (bf16[1152,1152]{1,0:T(8,128)(2,1)S(1)}, bf16[1152,1152]{1,0:T(8,128)(2,1)}, u32[]{:S(2)}) copy-start(bf16[1152,1152]{1,0:T(8,128)(2,1)} %get-tuple-element.59) | copy-start | bytes 7962628
  368.4 5.9 %copy-start.4 = (bf16[2,256,1152]{2,1,0:T(8,128)(2,1)S(1)}, bf16[2,256,1152]{2,1,0:T(8,128)(2,1)}, u32[]{:S(2)}) copy-start(bf16[2,256,1152]{2,1,0:T(8,128)(2,1)} %get-tuple-element.100) | copy-start | bytes 3538948
  374.3 1.7 copy-start.3

commit v2 on v1

--- a/solution.py
+++ b/solution.py
@@ -195,19 +195,83 @@
     return pl.ds(pl.multiple_of(start, 128), 256), own
 
 
-def first_kernel(
-    dims, lat, real_ref, cond_ref, wada_ref, abias_ref, tok_ref, cot_in_ref, kept_ref, qvb_ref, projb_ref,
-    own_qkv, own_proj, own_1, own_2,
-    attn_in_o, q_o, k_o, v_o, merged_o, attn_out_o, hidden_o, mlp_in_o, cot_o, mod_o,
-    full_o, all_1, all_2, dmlp_o,
-    full, sm_send, sm_recv, nrm, sel, mg, mod8,
-    sm_ss, sm_rs, za_ss, za_rs, zm_ss, zm_rs, ga_ss, ga_rs, gd_ss, gd_rs, loc,
+def kept_half(bucket, positions):
+    return jnp.where(bucket > 0, (positions - positions // 16) // 2, positions // 2)
+
+
+def row_mask(count, slots):
+    return jnp.where(lax.broadcasted_iota(jnp.int32, (slots, 1), 0) < count, 1.0, 0.0)
+
+
+def placing(kept_row, positions):
+    place = lax.broadcasted_iota(jnp.int32, (positions, kept_row.shape[1]), 0)
+    return jnp.where(place == kept_row, 1.0, 0.0).astype(BF)
+
+
+GELU_C = 0.7978845608028654
+
+
+def gelu_pair(v):
+    sq = v * v
+    t = jnp.tanh(GELU_C * v * (1.0 + 0.044715 * sq))
+    half = 0.5 + 0.5 * t
+    slope = half + 0.5 * GELU_C * v * (1.0 - t * t) * (1.0 + 3 * 0.044715 * sq)
+    return v * half, slope
+
+
+class Steps:
+    def __init__(self, rs):
+        self.rs = rs
+        self.links = len(rs.orders[0])
+
+    def send_core(self, make=None):
+        for m in range(self.rs.group - 1, 0, -2):
+            if make is not None:
+                make(m)
+            for p in range(2):
+                self.rs.send(m, p)
+
+    def last_link(self, m):
+        for p in range(2):
+            if self.rs.top(m, p) == self.rs.orders[p][-1]:
+                self.rs.fold(m, p)
+                self.rs.send(m, p)
+
+    def link(self, i):
+        for p in range(2):
+            order = self.rs.orders[p]
+            for m in span(order[: i - 1]):
+                self.rs.fold(m ^ order[i - 1], p)
+                self.rs.send(m ^ order[i - 1], p)
+
+    def finish(self, out, half):
+        for p in range(2):
+            total = self.rs.mine(0, p)[...].astype(F32)
+            for key in self.rs.keys(0, p):
+                self.rs.copy(key, p).wait_recv()
+                total = total + self.rs.inbox(key, p)[...].astype(F32)
+            out[p * half : (p + 1) * half] = total
+
+
+def forward_kernel(
+    dims, lat, bucket_ref, cond_ref, tok_ref, cot_in_ref, kept_ref, vec_ref,
+    wada_hbm, own_qkv, own_proj, own_1, own_2,
+    attn_in_o, q_o, k_o, v_o, merged_o, attn_out_o, hidden_o, cot_o, mod_o, din_o, zp_o, g1_o, g2_o, full_o,
+    full, sm_send, sm_recv, nrm, sel, mg, mod8, all_1, all_2, d_all, xb, act, dpre, y, inbox, bcol,
+    sm_ss, sm_rs, za_ss, za_rs, zm_ss, zm_rs, ga_ss, ga_rs, gd_ss, gd_rs, ag_ss, ag_rs, rs_ss, rs_rs, loc,
 ):
     group, count, rows_s, width = dims
     b, z = lax.axis_index("batch"), lax.axis_index("tp")
     g = b % group
     ds = width // count
     slots = kept_ref.shape[1]
+    positions = tok_ref.shape[1]
+    rows = lat * slots
+    half = rows // 2
+    cols = wada_hbm.shape[0]
+    load_ada = pltpu.make_async_copy(wada_hbm, y.at[0:cols], loc.at[1])
+    load_ada.start()
+    real = [kept_half(bucket_ref[z * lat + l], positions) for l in range(lat)]
     barrier(b, z, group, count)
 
     cut = (rows_s // 2 + 15) // 16 * 16
@@ -242,7 +306,7 @@
 
     slice_at = pl.ds(pl.multiple_of(g * rows_s, 16), rows_s)
     own_m = [
-        pltpu.make_async_copy(own_1.at[slice_at], all_1.at[z], loc.at[2]),
+        pltpu.make_async_copy(own_1.at[slice_at], all_1.at[z, :, 0:width], loc.at[2]),
         pltpu.make_async_copy(own_2.at[slice_at], all_2.at[z], loc.at[3]),
     ]
     for cp in own_m:
@@ -263,14 +327,14 @@
 
     cond = cond_ref[...].astype(F32)
     silu = (cond / (1.0 + jnp.exp(-cond))).astype(BF)
-    mod8[...] = jnp.zeros_like(mod8)
-    cols = wada_ref.shape[0]
-    mod8[:, 0:cols] = nt(silu, wada_ref[...]) + abias_ref[...].astype(F32)
+    mod8[...] = jnp.concatenate([vec_ref[4:5], vec_ref[5:6]], axis=1) + jnp.zeros_like(mod8)
+    load_ada.wait()
+    mod8[:, 0:cols] += nt(silu, y[0:cols])
     framed = pltpu.roll(mod8[...], (z * cols) % width, 1)
     for t in range(count):
         for i in range(2):
             sm_send[t, i] = framed[lat * t : lat * (t + 1), i * width : (i + 1) * width]
-        sm_send[t, 2] = qvb_ref[...]
+        sm_send[t, 2] = vec_ref[2:4]
 
     def small(d):
         peer = lax.rem(z + d, count)
@@ -281,22 +345,24 @@
 
     for d in range(1, count):
         small(d).start()
-    small_own = pltpu.make_async_copy(sm_send.at[z], sm_recv.at[z], loc.at[1])
+    small_own = pltpu.make_async_copy(sm_send.at[z], sm_recv.at[z], loc.at[6])
     small_own.start()
 
-    valid = []
     for l in range(lat):
-        real = real_ref[z * lat + l]
-        row = lax.broadcasted_iota(jnp.int32, (slots, 1), 0)
-        valid.append(jnp.where(row < real, 1.0, 0.0))
-        place = lax.broadcasted_iota(jnp.int32, (slots, tok_ref.shape[1]), 1)
-        pick = jnp.where(place == kept_ref[l], 1.0, 0.0).astype(BF)
+        pick = placing(kept_ref[l : l + 1], positions)
         at = slice(l * slots, (l + 1) * slots)
-        rows = nn(pick, tok_ref[l])
-        sel[at] = rows
-        center, inv = stats(rows)
+        picked = tn(pick, tok_ref[l])
+        sel[at] = picked
+        center, inv = stats(picked)
         nrm[at] = center * inv
-        cot_o[at] = (nn(pick, cot_in_ref[l]) * valid[l]).astype(BF)
+        cot_o[at] = (tn(pick, cot_in_ref[l]) * row_mask(real[l], slots)).astype(BF)
+
+    hid_s = own_1.shape[0]
+    first_row = lax.broadcasted_iota(jnp.int32, (8, 1), 0) == 0
+    corner = jnp.where(first_row & (lax.broadcasted_iota(jnp.int32, (1, 128), 1) == 0), 1.0, 0.0)
+    bias_row = jnp.where(first_row, vec_ref[6:7, 0:hid_s], 0.0)
+    bcol[...] = tn(bias_row.astype(BF), corner.astype(BF)).astype(BF)
+    all_1[z, :, width:] = bcol[slice_at]
 
     gathers = []
     for k in range(count - 1):
@@ -370,7 +436,7 @@
     for l in range(lat):
         at = slice(l * slots, (l + 1) * slots)
         attn_in_o[at] = (nrm[at] * (1.0 + mod_o[1, l : l + 1]) + mod_o[0, l : l + 1]).astype(BF)
-        dmlp_o[0, at] = (cot_o[at].astype(F32) * mod_o[5, l : l + 1]).astype(BF)
+        d_all[0, at] = (cot_o[at].astype(F32) * mod_o[5, l : l + 1]).astype(BF)
 
     for k in range(1, count - 1):
         arrive_a(k)
@@ -379,10 +445,8 @@
         gathers[k - 1].step(1)
     depth = gathers[0].steps()
     todo = [(i, k) for k in range(count - 1) for i in range(1, depth) if not (i == 1 and k < count - 2)]
-    half_rows = slots * lat // 2
-
     def dm_region(m, p, slot):
-        return dmlp_o.at[slot, pl.ds(p * half_rows, half_rows)]
+        return d_all.at[slot, pl.ds(p * half, half)]
 
     dm = Gather(b, z, group, dm_region, lambda m, p: gd_ss.at[p, m], lambda m, p: gd_rs.at[p, m])
     links = depth - 1
@@ -405,10 +469,10 @@
 
     x = attn_in_o[...]
     for j, out in enumerate((q_o, k_o, v_o)):
-        y = nt(x, full[j].reshape(width, width))
+        part_j = nt(x, full[j].reshape(width, width))
         if j != 1:
-            y = y + qv_bias[j // 2 : j // 2 + 1]
-        out[...] = y.astype(BF)
+            part_j = part_j + qv_bias[j // 2 : j // 2 + 1]
+        out[...] = part_j.astype(BF)
 
     scale = HEAD_SIZE**-0.5
 
@@ -422,7 +486,7 @@
                 q = (q_o[at, win].astype(F32) * own).astype(BF)
                 s = nt(q, k_o[at, win]) * scale
                 key = lax.broadcasted_iota(jnp.int32, (1, slots), 1)
-                s = jnp.where(key < real_ref[z * lat + l], s, -1000000000.0)
+                s = jnp.where(key < real[l], s, -1000000000.0)
                 w = jnp.exp(s - jnp.max(s, axis=-1, keepdims=True))
                 pr = (w / jnp.sum(w, axis=-1, keepdims=True)).astype(BF)
                 o = nn(pr, v_o[at, win])
@@ -433,105 +497,14 @@
     for i in range(2, dm.steps()):
         dm.step(i)
     merged_o[...] = mg[...].astype(BF)
-    a_out = nn(merged_o[...], full[3].reshape(width, width)) + projb_ref[...].astype(F32)
+    a_out = nn(merged_o[...], full[3].reshape(width, width)) + vec_ref[0:1]
     attn_out_o[...] = a_out
     for l in range(lat):
         at = slice(l * slots, (l + 1) * slots)
-        rows = sel[at] + mod_o[2, l : l + 1] * attn_out_o[at]
-        hidden_o[at] = rows
-        center, inv = stats(rows)
-        mlp_in_o[at] = (center * inv * (1.0 + mod_o[4, l : l + 1]) + mod_o[3, l : l + 1]).astype(BF)
-
-    arrive_m(count - 2)
-    dm.wait_core()
-    for d in range(1, count):
-        small(d).wait_send()
-    both_ways(lambda step, k: line_a(z, piece(g, z, None), step, k).wait_send())
-
-    def sent_m(step, k):
-        for cp in line_m(z, all_1.at[z], all_2.at[z], step, k):
-            cp.wait_send()
-
-    both_ways(sent_m)
-    for k in range(count - 1):
-        shard = near_shard(z, k, count)
-
-        @pl.when(((shard < z) & (z < count - 1)) | ((shard > z) & (z > 0)))
-        def _():
-            line_a(shard, piece(g, shard, None), 0, 2 + k).wait_send()
-            for cp in line_m(shard, all_1.at[shard], all_2.at[shard], 0, 2 + k):
-                cp.wait_send()
-
-        gathers[k].wait_sent()
-    dm.wait_sent()
-    full_out.wait()
-
-
-def run_first(dims, lat, real, cond, wada, abias, tok, cot, kept, qvb, projb, own_qkv, own_proj, own_1, own_2):
-    group, count, rows_s, width = dims
-    slots = kept.shape[1]
-    rows = lat * slots
-    vm = pl.BlockSpec(memory_space=pltpu.VMEM)
-    hb = pl.BlockSpec(memory_space=pl.ANY)
-    sm = pl.BlockSpec(memory_space=pltpu.SMEM)
-    sd = jax.ShapeDtypeStruct
-    row_bf, row_f = sd((rows, width), BF), sd((rows, width), F32)
-    dma = pltpu.SemaphoreType.DMA
-    return pl.pallas_call(
-        functools.partial(first_kernel, dims, lat),
-        out_shape=(
-            row_bf, row_bf, row_bf, row_bf, row_bf, row_f, row_f, row_bf, row_bf, sd((6, lat, width), F32),
-            sd((4, count, width // count, width), BF),
-            sd((count, rows_s, own_1.shape[1]), BF),
-            sd((count, rows_s, width), BF),
-            sd((group, rows, width), BF),
-        ),
-        in_specs=[sm] + [vm] * 8 + [hb] * 4,
-        out_specs=tuple([vm] * 10 + [hb] + [vm] * 3),
-        scratch_shapes=[
-            pltpu.VMEM((4, count, width // count, width), BF),
-            pltpu.VMEM((count, 3, lat, width), F32),
-            pltpu.VMEM((count, 3, lat, width), F32),
-            pltpu.VMEM((rows, width), F32),
-            pltpu.VMEM((rows, width), F32),
-            pltpu.VMEM((rows, width), F32),
-            pltpu.VMEM((cond.shape[0], 2 * width), F32),
-            dma((count,)), dma((count,)),
-            dma((count + 1,)), dma((count,)),
-            dma((2, count + 1)), dma((2, count)),
-            dma((count - 1, 2, group)), dma((count, 2, group)),
-            dma((2, group)), dma((2, group)),
-            dma((6,)),
-        ],
-        compiler_params=pltpu.CompilerParams(collective_id=1, has_side_effects=True, vmem_limit_bytes=56 * MIB),
-        name="forward_attention",
-    )(real, cond, wada, abias, tok, cot, kept, qvb, projb, own_qkv, own_proj, own_1, own_2)
-
-
-GELU_C = 0.7978845608028654
-
-
-def gelu_pair(v):
-    sq = v * v
-    t = jnp.tanh(GELU_C * v * (1.0 + 0.044715 * sq))
-    half = 0.5 + 0.5 * t
-    slope = half + 0.5 * GELU_C * v * (1.0 - t * t) * (1.0 + 3 * 0.044715 * sq)
-    return v * half, slope
-
-
-def middle_kernel(
-    dims, x_ref, d_ref, w1_ref, w2_ref,
-    din_o, out_o, g1_o, g2_o,
-    xb, act, dpre, y, inbox, yo, inbox_o,
-    ag_ss, ag_rs, rs_ss, rs_rs, ro_ss, ro_rs,
-):
-    group, count, rows_s, width = dims
-    b, z = lax.axis_index("batch"), lax.axis_index("tp")
-    rows = x_ref.shape[0]
-    half = rows // 2
-    hid = w1_ref.shape[0]
-    xb[0] = x_ref[...]
-    barrier(b, z, group, count)
+        mixed = sel[at] + mod_o[2, l : l + 1] * attn_out_o[at]
+        hidden_o[at] = mixed
+        center, inv = stats(mixed)
+        xb[0, at] = (center * inv * (1.0 + mod_o[4, l : l + 1]) + mod_o[3, l : l + 1]).astype(BF)
 
     def part(ref):
         return lambda m, p: ref.at[m, pl.ds(p * half, half)]
@@ -540,15 +513,17 @@
         b, z, group, lambda m, p, slot: part(xb)(slot, p), lambda m, p: ag_ss.at[p, m], lambda m, p: ag_rs.at[p, m]
     )
     gather.step(0)
-    bias = nt(jnp.ones((8, w1_ref.shape[1] - width), BF), w1_ref[:, width:])[0:1]
+    arrive_m(count - 2)
+    hid = count * rows_s
+    bias = nt(jnp.ones((8, all_1.shape[2] - width), BF), all_1[:, :, width:].reshape(hid, all_1.shape[2] - width))[0:1]
 
     def forward(pair):
         (m0, p0), (m1, p1) = pair
         at = [(m0, slice(p0 * half, (p0 + 1) * half)), (m1, slice(p1 * half, (p1 + 1) * half))]
         x = jnp.concatenate([xb[m, s] for m, s in at], axis=0)
-        d = jnp.concatenate([d_ref[m, s] for m, s in at], axis=0)
-        a, slope = gelu_pair(nt(x, w1_ref[:, 0:width]) + bias)
-        dp = (slope * nt(d, w2_ref[...])).astype(BF)
+        d = jnp.concatenate([d_all[m, s] for m, s in at], axis=0)
+        a, slope = gelu_pair(nt(x, all_1[:, :, 0:width].reshape(hid, width)) + bias)
+        dp = (slope * nt(d, all_2[...].reshape(hid, width))).astype(BF)
         a = a.astype(BF)
         for i, (m, s) in enumerate(at):
             to = slice(m * rows + s.start, m * rows + s.stop)
@@ -558,6 +533,7 @@
     forward(((0, 0), (0, 1)))
     for p in range(2):
         gather.wait(1, p)
+        dm.wait(1, p)
     forward(((1, 0), (1, 1)))
     for i in range(1, gather.steps()):
         gather.step(i)
@@ -565,139 +541,150 @@
         for m0, m1 in zip(*fresh):
             forward(((m0, 0), (m1, 1)))
         for m0, m1 in zip(*fresh):
-            gather.wait(m0 ^ 1, 0)
-            gather.wait(m1 ^ 1, 1)
+            for item in (gather, dm):
+                item.wait(m0 ^ 1, 0)
+                item.wait(m1 ^ 1, 1)
             forward(((m0 ^ 1, 0), (m1 ^ 1, 1)))
 
-    def reduction(own, boxes, ss, rs):
-        mine, arrived = part(own), part(boxes)
-
-        def add(m, key, p):
-            mine(m, p)[...] = (mine(m, p)[...].astype(F32) + arrived(key, p)[...].astype(F32)).astype(BF)
-
-        return Scatter(b, z, group, mine, arrived, lambda m, p: ss.at[p, m], lambda m, p: rs.at[p, m], add)
-
-    rs_in = reduction(y, inbox, rs_ss, rs_rs)
-    rs_out = reduction(yo, inbox_o, ro_ss, ro_rs)
-    links = len(rs_in.orders[0])
+    mine = lambda m, p: y.at[pl.ds(m * rows + p * half, half)]
+    arrived = lambda m, p: inbox.at[m - 1, pl.ds(p * half, half)]
+
+    def add(m, key, p):
+        mine(m, p)[...] = (mine(m, p)[...].astype(F32) + arrived(key, p)[...].astype(F32)).astype(BF)
+
+    rs = Steps(Scatter(b, z, group, mine, arrived, lambda m, p: rs_ss.at[p, m], lambda m, p: rs_rs.at[p, m], add))
 
     def part_in(m):
-        y[m] = nn(dpre[m * rows : (m + 1) * rows], w1_ref[:, 0:width]).astype(BF)
-
-    def part_out(m):
-        yo[m] = nn(act[m * rows : (m + 1) * rows], w2_ref[...]).astype(BF)
-
-    def send_core(rs, make):
-        for m in range(group - 1, 0, -2):
-            make(m)
-            for p in range(2):
-                rs.send(m, p)
-
-    def last_link(rs, m):
-        for p in range(2):
-            if rs.top(m, p) == rs.orders[p][-1]:
-                rs.fold(m, p)
-                rs.send(m, p)
-
-    def next_link(rs, i):
-        for p in range(2):
-            order = rs.orders[p]
-            for m in span(order[: i - 1]):
-                rs.fold(m ^ order[i - 1], p)
-                rs.send(m ^ order[i - 1], p)
-
-    def finish(rs, out):
-        for p in range(2):
-            total = rs.mine(0, p)[...].astype(F32)
-            for key in rs.keys(0, p):
-                rs.copy(key, p).wait_recv()
-                total = total + rs.inbox(key, p)[...].astype(F32)
-            out[p * half : (p + 1) * half] = total
+        at = slice(m * rows, (m + 1) * rows)
+        y[at] = nn(dpre[at], all_1[:, :, 0:width].reshape(hid, width)).astype(BF)
 
     chunks = [slice(c, min(c + 128, hid)) for c in range(0, hid, 128)]
-
-    def grads_1():
-        ones = jnp.ones((group * rows, g1_o.shape[1] - width), BF)
-        x = xb[...].reshape(group * rows, width)
-        for c in chunks:
-            g1_o[c, 0:width] = tn(dpre[:, c], x).astype(BF)
-            g1_o[c, width:] = tn(dpre[:, c], ones).astype(BF)
-
-    def grads_2():
-        d = d_ref[...].reshape(group * rows, width)
-        for c in chunks:
-            g2_o[c] = tn(act[:, c], d).astype(BF)
-
-    send_core(rs_in, part_in)
+    rs.send_core(part_in)
     for m in range(group - 2, 0, -2):
         part_in(m)
-        last_link(rs_in, m)
+        rs.last_link(m)
     part_in(0)
-    send_core(rs_out, part_out)
-    for m in range(group - 2, -1, -2):
-        part_out(m)
-    for i in range(links - 1, 0, -1):
-        next_link(rs_in, i)
-    for m in range(group - 2, 0, -2):
-        last_link(rs_out, m)
-    grads_1()
-    finish(rs_in, din_o)
-    grads_2()
-    for i in range(links - 1, 0, -1):
-        next_link(rs_out, i)
-    finish(rs_out, out_o)
+    ones = jnp.ones((group * rows, g1_o.shape[1] - width), BF)
+    for c in chunks:
+        g1_o[c, 0:width] = tn(dpre[:, c], xb[...].reshape(group * rows, width)).astype(BF)
+        g1_o[c, width:] = tn(dpre[:, c], ones).astype(BF)
+    for i in range(rs.links - 1, 0, -1):
+        rs.link(i)
+    for c in chunks:
+        g2_o[c] = tn(act[:, c], d_all[...].reshape(group * rows, width)).astype(BF)
+    for m in range(group):
+        zp_o[m] = nn(act[m * rows : (m + 1) * rows], all_2[...].reshape(hid, width)).astype(BF)
+    rs.finish(din_o, half)
     gather.wait_sent()
-    rs_in.wait_sent()
-    rs_out.wait_sent()
-
-
-def run_middle(dims, x, d_all, w1, w2):
+    rs.rs.wait_sent()
+
+    for d in range(1, count):
+        small(d).wait_send()
+    both_ways(lambda step, k: line_a(z, piece(g, z, None), step, k).wait_send())
+
+    def sent_m(step, k):
+        for cp in line_m(z, all_1.at[z], all_2.at[z], step, k):
+            cp.wait_send()
+
+    both_ways(sent_m)
+    for k in range(count - 1):
+        shard = near_shard(z, k, count)
+
+        @pl.when(((shard < z) & (z < count - 1)) | ((shard > z) & (z > 0)))
+        def _():
+            line_a(shard, piece(g, shard, None), 0, 2 + k).wait_send()
+            for cp in line_m(shard, all_1.at[shard], all_2.at[shard], 0, 2 + k):
+                cp.wait_send()
+
+        gathers[k].wait_sent()
+    dm.wait_sent()
+    full_out.wait()
+
+
+def run_forward(dims, lat, bucket, cond, tok, cot, kept, vec, wada, own_qkv, own_proj, own_1, own_2):
     group, count, rows_s, width = dims
-    rows, hid = x.shape[0], w1.shape[0]
+    slots = kept.shape[1]
+    rows = lat * slots
+    hid = count * rows_s
+    ext = width + 128
     vm = pl.BlockSpec(memory_space=pltpu.VMEM)
+    hb = pl.BlockSpec(memory_space=pl.ANY)
+    sm = pl.BlockSpec(memory_space=pltpu.SMEM)
     sd = jax.ShapeDtypeStruct
+    row_bf, row_f = sd((rows, width), BF), sd((rows, width), F32)
+    blocks = sd((group, rows, width), BF)
     dma = pltpu.SemaphoreType.DMA
-    blocks = pltpu.VMEM((group, rows, width), BF)
+    vmem = pltpu.VMEM
     return pl.pallas_call(
-        functools.partial(middle_kernel, dims),
+        functools.partial(forward_kernel, dims, lat),
         out_shape=(
-            sd((rows, width), F32), sd((rows, width), F32), sd(w1.shape, BF), sd(w2.shape, BF),
+            row_bf, row_bf, row_bf, row_bf, row_bf, row_f, row_f, row_bf, sd((6, lat, width), F32),
+            row_f, blocks, sd((hid, ext), BF), sd((hid, width), BF), sd((4, count, width // count, width), BF),
         ),
-        in_specs=[vm] * 4,
-        out_specs=tuple([vm] * 4),
+        in_specs=[sm] + [vm] * 5 + [hb] * 5,
+        out_specs=tuple([vm] * 13 + [hb]),
         scratch_shapes=[
-            blocks, pltpu.VMEM((group * rows, hid), BF), pltpu.VMEM((group * rows, hid), BF), blocks, blocks,
-            blocks, blocks,
+            vmem((4, count, width // count, width), BF),
+            vmem((count, 3, lat, width), F32), vmem((count, 3, lat, width), F32),
+            vmem((rows, width), F32), vmem((rows, width), F32), vmem((rows, width), F32),
+            vmem((cond.shape[0], 2 * width), F32),
+            vmem((count, rows_s, ext), BF), vmem((count, rows_s, width), BF),
+            vmem((group, rows, width), BF), vmem((group, rows, width), BF),
+            vmem((group * rows, hid), BF), vmem((group * rows, hid), BF),
+            vmem((group * rows, width), BF), vmem((group - 1, rows, width), BF),
+            vmem((own_1.shape[0], 128), BF),
+            dma((count,)), dma((count,)),
+            dma((count + 1,)), dma((count,)),
+            dma((2, count + 1)), dma((2, count)),
+            dma((count - 1, 2, group)), dma((count, 2, group)),
             dma((2, group)), dma((2, group)), dma((2, group)), dma((2, group)), dma((2, group)), dma((2, group)),
+            dma((7,)),
         ],
-        compiler_params=pltpu.CompilerParams(collective_id=2, has_side_effects=True, vmem_limit_bytes=58 * MIB),
-        name="feed_forward",
-    )(x, d_all, w1, w2)
-
-
-def last_kernel(
-    dims, lat, real_ref, kept_ref, tok_ref, cot_in_ref, attn_in_ref, q_ref, k_ref, v_ref, merged_ref,
-    attn_out_ref, hidden_ref, cot_ref, mod_ref, d_in_ref, mlp_out_ref, redb_ref, cond_ref,
-    full_ref, g1_ref, g2_ref,
+        compiler_params=pltpu.CompilerParams(collective_id=1, has_side_effects=True, vmem_limit_bytes=63 * MIB),
+        name="forward_attention",
+    )(bucket, cond, tok, cot, kept, vec, wada, own_qkv, own_proj, own_1, own_2)
+
+
+def backward_kernel(
+    dims, lat, bucket_ref, kept_ref, tok_ref, cot_in_ref, attn_in_ref, q_ref, k_ref, v_ref, merged_ref,
+    attn_out_ref, hidden_ref, cot_ref, mod_ref, d_in_ref, vec_ref, cond_ref,
+    full_ref, g1_ref, g2_ref, zp_ref,
     out_o, dtok_o, ga_o, gm1_o, gm2_o, small_o,
-    wbuf, gbuf, abox, ar, gm1, gm2, mr1, mr2, back_b, d3, d_attn, dm, dain, sm_send, sm_recv, dmod,
-    loc, ra_ss, ra_rs, za_ss, za_rs, zm_ss, zm_rs, gm_ss, gm_rs, ga_ss, ga_rs, sz_ss, sz_rs, sp_ss, sp_rs,
+    wbuf, gbuf, abox, ar, gm1, gm2, mr1, mr2, back_b, d3, d_attn, dm, dain, mlp, inbox, sm_send, sm_recv, dmod,
+    loc, ro_ss, ro_rs, ra_ss, ra_rs, za_ss, za_rs, zm_ss, zm_rs, gm_ss, gm_rs, ga_ss, ga_rs, sz_ss, sz_rs, sp_ss, sp_rs,
 ):
     group, count, rows_s, width = dims
     b, z = lax.axis_index("batch"), lax.axis_index("tp")
     g = b % group
     ds = width // count
     slots = kept_ref.shape[1]
+    positions = tok_ref.shape[1]
+    rows = lat * slots
+    half = rows // 2
     scale = HEAD_SIZE**-0.5
     loads = [
         pltpu.make_async_copy(g1_ref, gm1, loc.at[0]),
         pltpu.make_async_copy(g2_ref, gm2, loc.at[1]),
         pltpu.make_async_copy(full_ref.at[3], wbuf.at[0], loc.at[2]),
         pltpu.make_async_copy(full_ref.at[0], wbuf.at[1], loc.at[3]),
+        pltpu.make_async_copy(zp_ref, gbuf.at[0 : group * rows], loc.at[5]),
     ]
     for cp in loads:
         cp.start()
+    real = [kept_half(bucket_ref[z * lat + l], positions) for l in range(lat)]
     barrier(b, z, group, count)
+
+    mine_out = lambda m, p: gbuf.at[pl.ds(m * rows + p * half, half)]
+    box_out = lambda m, p: inbox.at[m - 1, pl.ds(p * half, half)]
+
+    def add_out(m, key, p):
+        mine_out(m, p)[...] = (mine_out(m, p)[...].astype(F32) + box_out(key, p)[...].astype(F32)).astype(BF)
+
+    rs_out = Steps(
+        Scatter(b, z, group, mine_out, box_out, lambda m, p: ro_ss.at[p, m], lambda m, p: ro_rs.at[p, m], add_out)
+    )
+    loads[4].wait()
+    rs_out.send_core()
     cut = (rows_s // 2 + 15) // 16 * 16
     parts = ((0, cut), (cut, rows_s - cut))
 
@@ -709,7 +696,7 @@
         at = pl.ds(pl.multiple_of(peer * rows_s, 16), rows_s)
         return [
             pltpu.make_async_remote_copy(
-                src_ref=src.at[at], dst_ref=dst.at[d], send_sem=zm_ss.at[i, d], recv_sem=zm_rs.at[i, d],
+                src_ref=src.at[at], dst_ref=dst.at[d - 1], send_sem=zm_ss.at[i, d], recv_sem=zm_rs.at[i, d],
                 device_id=(b, peer), device_id_type=MESH,
             )
             for i, (src, dst) in enumerate(((gm1, mr1), (gm2, mr2)))
@@ -728,12 +715,11 @@
     def total(rows):
         return jnp.sum(rows, axis=0, keepdims=True)
 
-    valid = []
+    for m in range(group - 2, 0, -2):
+        rs_out.last_link(m)
     for l in range(lat):
         at = rows_of(l)
         one = slice(l, l + 1)
-        row = lax.broadcasted_iota(jnp.int32, (slots, 1), 0)
-        valid.append(jnp.where(row < real_ref[z * lat + l], 1.0, 0.0))
         center, inv = stats(hidden_ref[at])
         n = center * inv
         d_in = d_in_ref[at]
@@ -744,8 +730,6 @@
         dmod[3, one] = total(d_in)
         dmod[4, one] = total(d_in * n)
         dmod[2, one] = total(d_hidden * attn_out_ref[at])
-        mlp_out = mlp_out_ref[at] + redb_ref[...].astype(F32)
-        dmod[5, one] = total(cot * mlp_out)
 
     loads[2].wait()
     dm[...] = nt(d_attn[...], wbuf[0]).astype(BF)
@@ -756,7 +740,7 @@
     def weight_grad(j, left, right):
         for c in range(0, width, chunk):
             to = slice(c, c + chunk)
-            gbuf[j, to] = tn(left(to), right).astype(BF)
+            gbuf[j * width + c : j * width + c + chunk] = tn(left(to), right).astype(BF)
 
     weight_grad(3, lambda to: merged_ref[:, to], d_attn[...])
 
@@ -770,7 +754,7 @@
                 q, k, v, dmh = q_ref[at, win], k_ref[at, win], v_ref[at, win], dm[at, win]
                 s = nt((q.astype(F32) * own).astype(BF), k) * scale
                 key = lax.broadcasted_iota(jnp.int32, (1, slots), 1)
-                s = jnp.where(key < real_ref[z * lat + l], s, -1000000000.0)
+                s = jnp.where(key < real[l], s, -1000000000.0)
                 w = jnp.exp(s - jnp.max(s, axis=-1, keepdims=True))
                 pr = w / jnp.sum(w, axis=-1, keepdims=True)
                 dp = nt((dmh.astype(F32) * own).astype(BF), v)
@@ -781,7 +765,15 @@
                     d3[j, at, win] = jnp.where(own > 0, grad, d3[j, at, win].astype(F32)).astype(BF)
         return 0
 
-    lax.fori_loop(0, heads // 2, some_heads, 0)
+    lax.fori_loop(0, heads // 4, some_heads, 0)
+    for i in range(rs_out.links - 1, 0, -1):
+        rs_out.link(i)
+    lax.fori_loop(heads // 4, heads // 2, some_heads, 0)
+    rs_out.finish(mlp, half)
+    mlp[...] += vec_ref[1:2]
+    for l in range(lat):
+        dmod[5, l : l + 1] = total(cot_ref[rows_of(l)].astype(F32) * mlp[rows_of(l)])
+    rs_out.rs.wait_sent()
 
     for j in range(3):
         weight_grad(j, lambda to, j=j: d3[j, :, to], attn_in_ref[...])
@@ -794,7 +786,7 @@
         def mine(m, p, w=w):
             at = flip(g, m) * rows_s
             lo, ln = parts[p]
-            return gbuf.at[at // ds, pl.ds(pl.multiple_of(ds * wave_shard(w) + at % ds + lo, 16), ln)]
+            return gbuf.at[pl.ds(pl.multiple_of(at // ds * width + ds * wave_shard(w) + at % ds + lo, 16), ln)]
 
         def box(m, p, w=w):
             lo, ln = parts[p]
@@ -810,7 +802,7 @@
 
     def own_slice(shard):
         at = g * rows_s
-        return gbuf.at[at // ds, pl.ds(pl.multiple_of(ds * shard + at % ds, 16), rows_s)]
+        return gbuf.at[pl.ds(pl.multiple_of(at // ds * width + ds * shard + at % ds, 16), rows_s)]
 
     def line_a(w):
         return pltpu.make_async_remote_copy(
@@ -839,7 +831,7 @@
                 rs.send(m, p)
 
     def wave_round(t):
-        for w in range(count):
+        for w in reversed(range(count)):
             wave_step(w, t - w)
 
     loads[3].wait()
@@ -853,17 +845,15 @@
     dain[...] += nn(d3[2], wbuf[1])
     wave_round(1)
 
-    place = lax.broadcasted_iota(jnp.int32, (slots, tok_ref.shape[1]), 1)
-
     def put(pick, rows):
         high = rows.astype(BF)
-        return tn(pick, high) + tn(pick, (rows - high.astype(F32)).astype(BF))
+        return nn(pick, high) + nn(pick, (rows - high.astype(F32)).astype(BF))
 
     for l in range(lat):
         at = rows_of(l)
         one = slice(l, l + 1)
-        pick = jnp.where(place == kept_ref[l], 1.0, 0.0).astype(BF)
-        center, inv = stats(nn(pick, tok_ref[l]))
+        pick = placing(kept_ref[one], positions)
+        center, inv = stats(tn(pick, tok_ref[l]))
         n = center * inv
         d_ai = dain[at]
         dmod[0, one] = total(d_ai)
@@ -900,9 +890,8 @@
     for l in range(lat):
         at = rows_of(l)
         one = slice(l, l + 1)
-        pick = jnp.where(place == kept_ref[l], 1.0, 0.0).astype(BF)
-        mlp_out = mlp_out_ref[at] + redb_ref[...].astype(F32)
-        delta = (mod_ref[2, one] * attn_out_ref[at] + mod_ref[5, one] * mlp_out) * valid[l]
+        pick = placing(kept_ref[one], positions)
+        delta = (mod_ref[2, one] * attn_out_ref[at] + mod_ref[5, one] * mlp[at]) * row_mask(real[l], slots)
         out_o[l] = (tok_ref[l].astype(F32) + put(pick, delta)).astype(BF)
     for d in range(1, count):
         ref = sm_recv.at[lax.rem(z - d + count, count)]
@@ -926,7 +915,7 @@
         b, z, group, lambda m, p, slot: small_o.at[slot], lambda m, p: sp_ss.at[m], lambda m, p: sp_rs.at[m], halves=1
     )
     sp.step(0)
-    for t in range(3, count + links):
+    for t in range(3, count + links - 1):
         wave_round(t)
         if t - 2 < sp.steps():
             sp.step(t - 2)
@@ -940,6 +929,19 @@
 
     g_at = pl.ds(pl.multiple_of(g * rows_s, 16), rows_s)
     z_at = pl.ds(pl.multiple_of(z * rows_s, 16), rows_s)
+    for d in range(1, count):
+        for cp in line_m(d):
+            cp.wait_recv()
+    for own, box, out in ((gm1, mr1, gm1_o), (gm2, mr2, gm2_o)):
+        acc = own[z_at].astype(F32)
+        for d in range(count - 1):
+            acc = acc + box[d].astype(F32)
+        out[g_at] = acc.astype(BF)
+    spread_1 = spread(gm1_o, gm_ss.at[0], gm_rs.at[0])
+    spread_2 = spread(gm2_o, gm_ss.at[1], gm_rs.at[1])
+    spread_1.step(0)
+    spread_2.step(0)
+    wave_round(count + links - 1)
     acc = own_slice(z)[...].astype(F32)
     for w in range(count - 1):
         line_a(w).wait_recv()
@@ -947,22 +949,10 @@
     ga_o[g_at] = acc.astype(BF)
     spread_a = spread(ga_o, ga_ss, ga_rs)
     spread_a.step(0)
-    for d in range(1, count):
-        for cp in line_m(d):
-            cp.wait_recv()
-    for own, box, out in ((gm1, mr1, gm1_o), (gm2, mr2, gm2_o)):
-        acc = own[z_at].astype(F32)
-        for d in range(1, count):
-            acc = acc + box[d].astype(F32)
-        out[g_at] = acc.astype(BF)
-    spread_1 = spread(gm1_o, gm_ss.at[0], gm_rs.at[0])
-    spread_2 = spread(gm2_o, gm_ss.at[1], gm_rs.at[1])
-    spread_1.step(0)
-    spread_2.step(0)
     for i in range(1, spread_a.steps()):
-        for item in (spread_a, spread_1, spread_2):
+        for item in (spread_1, spread_2, spread_a):
             item.step(i)
-    for i in range(max(1, count + links - 2), sp.steps()):
+    for i in range(max(1, count + links - 3), sp.steps()):
         sp.step(i)
     for item in (sp, spread_a, spread_1, spread_2):
         item.wait_core()
@@ -977,7 +967,10 @@
             cp.wait_send()
 
 
-def run_last(dims, lat, real, kept, tok, cot_in, attn_in, q, k, v, merged, attn_out, hidden, cot, mod, d_in, mlp_out, redb, cond, full, g1, g2):
+def run_backward(
+    dims, lat, bucket, kept, tok, cot_in, attn_in, q, k, v, merged, attn_out, hidden, cot, mod, d_in, vec, cond,
+    full, g1, g2, zp,
+):
     group, count, rows_s, width = dims
     rows = attn_in.shape[0]
     vm = pl.BlockSpec(memory_space=pltpu.VMEM)
@@ -985,30 +978,33 @@
     sm = pl.BlockSpec(memory_space=pltpu.SMEM)
     sd = jax.ShapeDtypeStruct
     dma = pltpu.SemaphoreType.DMA
+    vmem = pltpu.VMEM
     ext = g1.shape[1]
     small = (group, 4, cond.shape[0], width)
     return pl.pallas_call(
-        functools.partial(last_kernel, dims, lat),
+        functools.partial(backward_kernel, dims, lat),
         out_shape=(
             sd(tok.shape, BF), sd(tok.shape, BF), sd((group * rows_s, width), BF),
             sd((group * rows_s, ext), BF), sd((group * rows_s, width), BF), sd(small, F32),
         ),
-        in_specs=[sm] + [vm] * 16 + [hb] * 3,
+        in_specs=[sm] + [vm] * 15 + [hb] * 4,
         out_specs=tuple([vm] * 6),
         scratch_shapes=[
-            pltpu.VMEM((2, width, width), BF),
-            pltpu.VMEM((4, width, width), BF),
-            pltpu.VMEM((count, group - 1, rows_s, width), BF),
-            pltpu.VMEM((count, rows_s, width), BF),
-            pltpu.VMEM(g1.shape, BF), pltpu.VMEM(g2.shape, BF),
-            pltpu.VMEM((count, rows_s, ext), BF), pltpu.VMEM((count, rows_s, width), BF),
-            pltpu.VMEM((rows, width), F32),
-            pltpu.VMEM((3, rows, width), BF),
-            pltpu.VMEM((rows, width), BF), pltpu.VMEM((rows, width), BF),
-            pltpu.VMEM((rows, width), F32),
-            pltpu.VMEM((count, 4, lat, width), F32), pltpu.VMEM((count, 4, lat, width), F32),
-            pltpu.VMEM((6, lat, width), F32),
-            dma((5,)),
+            vmem((2, width, width), BF),
+            vmem((4 * width, width), BF),
+            vmem((count, group - 1, rows_s, width), BF),
+            vmem((count - 1, rows_s, width), BF),
+            vmem(g1.shape, BF), vmem(g2.shape, BF),
+            vmem((count - 1, rows_s, ext), BF), vmem((count - 1, rows_s, width), BF),
+            vmem((rows, width), F32),
+            vmem((3, rows, width), BF),
+            vmem((rows, width), BF), vmem((rows, width), BF),
+            vmem((rows, width), F32), vmem((rows, width), F32),
+            vmem((group - 1, rows, width), BF),
+            vmem((count, 4, lat, width), F32), vmem((count, 4, lat, width), F32),
+            vmem((6, lat, width), F32),
+            dma((6,)),
+            dma((2, group)), dma((2, group)),
             dma((count, 2, group)), dma((count, 2, group)),
             dma((count,)), dma((count,)),
             dma((2, count)), dma((2, count)),
@@ -1019,13 +1015,62 @@
         ],
         compiler_params=pltpu.CompilerParams(collective_id=3, has_side_effects=True, vmem_limit_bytes=63 * MIB),
         name="backward_attention",
-    )(real, kept, tok, cot_in, attn_in, q, k, v, merged, attn_out, hidden, cot, mod, d_in, mlp_out, redb, cond, full, g1, g2)
-
-
-def own_frame(part, total, axis):
-    size = part.shape[-1]
-    frame = jnp.zeros(part.shape[:-1] + (total,), F32)
-    return lax.dynamic_update_slice_in_dim(frame, part.astype(F32), lax.axis_index("tp") * size, frame.ndim - 1)
+    )(bucket, kept, tok, cot_in, attn_in, q, k, v, merged, attn_out, hidden, cot, mod, d_in, vec, cond, full, g1, g2, zp)
+
+
+def widen_kernel(dims, ga_ref, gm1_ref, gm2_ref, small_ref, qkv_o, proj_o, exp_o, red_o, ada_o, vec_o, addb_o,
+                 qkv, proj, exp, red, ada, sem):
+    group, count, rows_s, width = dims
+    ds = width // count
+    cols = ada.shape[0]
+    members = small_ref.shape[0] * small_ref.shape[2]
+
+    def out(src, dst, k):
+        cp = pltpu.make_async_copy(src, dst, sem.at[k])
+        cp.start()
+        return cp
+
+    def item(k):
+        return small_ref[:, k].reshape(members, width)
+
+    pair = jnp.concatenate([item(0), item(1)], axis=1)
+    start = lax.rem(lax.axis_index("tp") * cols, width)
+    pair = pltpu.roll(pair, lax.rem(2 * width - start, 2 * width), 1)[:, 0:cols]
+    addb_o[...] = jnp.sum(pair, axis=0, keepdims=True)
+    ada[...] = tn(pair.astype(BF), item(3).astype(BF))
+    done = [out(ada, ada_o, 0)]
+    red[...] = gm2_ref[...].astype(F32)
+    done.append(out(red, red_o, 1))
+    qkv[...] = ga_ref[0 : 3 * ds].astype(F32)
+    done.append(out(qkv, qkv_o, 2))
+    proj[...] = ga_ref[3 * ds :].astype(F32)
+    done.append(out(proj, proj_o, 3))
+    exp[...] = gm1_ref[:, 0:width].T.astype(F32)
+    done.append(out(exp, exp_o, 4))
+    acc = small_ref[0, 2]
+    for i in range(1, small_ref.shape[0]):
+        acc = acc + small_ref[i, 2]
+    vec_o[...] = acc
+    for cp in done:
+        cp.wait()
+
+
+def run_widen(dims, cols, ga, gm1, gm2, small):
+    group, count, rows_s, width = dims
+    ds = width // count
+    vm = pl.BlockSpec(memory_space=pltpu.VMEM)
+    hb = pl.BlockSpec(memory_space=pl.ANY)
+    big = [(3 * ds, width), (ds, width), (width, gm1.shape[0]), gm2.shape, (cols, width)]
+    vecs = [small.shape[2:], (1, cols)]
+    return pl.pallas_call(
+        functools.partial(widen_kernel, dims),
+        out_shape=tuple(jax.ShapeDtypeStruct(item, F32) for item in big + vecs),
+        in_specs=[vm] * 4,
+        out_specs=tuple([hb] * 5 + [vm] * 2),
+        scratch_shapes=[pltpu.VMEM(item, F32) for item in big] + [pltpu.SemaphoreType.DMA((5,))],
+        compiler_params=pltpu.CompilerParams(vmem_limit_bytes=60 * MIB),
+        name="widen_gradients",
+    )(ga, gm1, gm2, small)
 
 
 def body(
@@ -1035,53 +1080,53 @@
     lat, positions, width = tokens.shape
     shard_w, shard_f = w_qkv.shape[2], w_expand.shape[1]
     group = group_size(shard_f, shard_w)
-    rows_s = shard_f // group
-    dims = (group, count, rows_s, width)
-    real = (positions - positions // 16 * (bucket > 0).astype(jnp.int32)) // 2
-    own_1 = jnp.concatenate(
-        [w_expand.T, jnp.pad(expand_bias[:, None], ((0, 0), (0, 127)))], axis=1
+    dims = (group, count, shard_f // group, width)
+    cols = ada_bias.shape[0]
+
+    def padded(part, size):
+        return jnp.pad(part.astype(F32), (0, size - part.shape[0]))
+
+    def framed(part):
+        return lax.dynamic_update_slice(jnp.zeros((width,), F32), part.astype(F32), (lax.axis_index("tp") * shard_w,))
+
+    vec = jnp.concatenate(
+        [
+            proj_bias.astype(F32), reduce_bias.astype(F32), framed(qv_bias[0]), framed(qv_bias[1]),
+            padded(ada_bias, 2 * width), padded(expand_bias, 2 * width),
+        ]
+    ).reshape(8, width)
+    (attn_in, queries, key_rows, value_rows, merged, attn_out, hidden, cot, mod, d_in, zp, g1, g2, full) = run_forward(
+        dims, lat, bucket, conditioning, tokens, out_grad, kept_index, vec,
+        w_ada.T, jnp.swapaxes(w_qkv, 1, 2), w_proj, w_expand.T, w_reduce,
     )
-    out1 = run_first(
-        dims, lat, real, conditioning, w_ada.T, ada_bias[None], tokens, out_grad, kept_index[:, :, None],
-        own_frame(qv_bias, width, "tp"), proj_bias[None], jnp.swapaxes(w_qkv, 1, 2), w_proj, own_1, w_reduce,
+    output, tokens_grad, ga, gm1, gm2, small = run_backward(
+        dims, lat, bucket, kept_index, tokens, out_grad, attn_in, queries, key_rows, value_rows, merged,
+        attn_out, hidden, cot, mod, d_in, vec, conditioning,
+        full.reshape(4, width, width), g1, g2, zp.reshape(-1, width),
     )
-    (attn_in, queries, key_rows, value_rows, merged, attn_out, hidden, mlp_in, cot, mod, full, all_1, all_2, d_all) = out1
-    flat = lambda a: a.reshape((-1,) + a.shape[2:])
-    d_in, mlp_out, g1, g2 = run_middle(dims, mlp_in, d_all, flat(all_1), flat(all_2))
-    output, tokens_grad, ga, gm1, gm2, small = run_last(
-        dims, lat, real, kept_index[:, :, None], tokens, out_grad, attn_in, queries, key_rows, value_rows, merged,
-        attn_out, hidden, cot, mod, d_in, mlp_out, reduce_bias[None], conditioning,
-        full.reshape(4, width, width), g1, g2,
-    )
-
-    cols = 6 * width // count
-    start = lax.axis_index("tp") * cols % width
-    pair = jnp.concatenate([flat(small[:, 0]), flat(small[:, 1])], axis=1)
-    d_mod = lax.dynamic_slice_in_dim(pair, start, cols, 1)
-    ada_grad = tn(flat(small[:, 3]).astype(BF), d_mod.astype(BF))
-    ada_add_grad = jnp.sum(d_mod, axis=0)
-    sums = jnp.sum(small[:, 2, 0:4], axis=0)
+
+    def over_batch(items):
+        if batch > group:
+            return tuple(lax.psum(item * (1.0 / group), "batch") for item in items)
+        return items
+
+    ga, gm1, gm2 = over_batch((ga, gm1, gm2))
+    qkv_grad, proj_grad, expand_grad, reduce_grad, ada_grad, sums, ada_add = run_widen(dims, cols, ga, gm1, gm2, small)
+    ada_grad, sums, ada_add = over_batch((ada_grad, sums, ada_add))
     pair_grad = lax.dynamic_slice_in_dim(sums[2:4], lax.axis_index("tp") * shard_w, shard_w, 1)
-    grads = (
-        ada_grad, ada_add_grad, ga, gm1, gm2, pair_grad, sums[0], sums[1],
-    )
-    if batch > group:
-        grads = tuple(lax.psum(item * (1.0 / group), "batch") for item in grads)
-    ada_grad, ada_add_grad, ga, gm1, gm2, pair_grad, reduce_add, proj_add = grads
-    ga = ga.reshape(4, shard_w, width)
     return (
         output,
         tokens_grad,
-        ada_grad,
-        ada_add_grad,
-        jnp.swapaxes(ga[:3], 1, 2).astype(F32),
+        ada_grad.T,
+        ada_add.reshape(cols),
+        jnp.swapaxes(qkv_grad.reshape(3, shard_w, width), 1, 2),
         pair_grad,
-        ga[3].astype(F32),
-        proj_add,
-        gm1[:, :width].T.astype(F32),
+        proj_grad,
+        sums[1],
+        expand_grad,
         gm1[:, width].astype(F32),
-        gm2.astype(F32),
-        reduce_add,
+        reduce_grad,
+        sums[0],
     )
 
 

time: 383 us -> 336 us (0.88)
  the two profiles are of different devices: /device:TPU:27 before, /device:TPU:0 now
where the time goes in v2:
time: 336 us; the launch traced here: 331 us
  Pallas kernels  311 us (93%)
  local copies, waits for them, and re-layouts  11.3 us (3%)
  other arithmetic  6.7 us (2%)
    pallas_call x1, Pallas kernels, run_backward(): pl.pallas_call(functools.partial(backward_kernel, dims, lat), out_shape=(...  149 us
    pallas_call x1, Pallas kernels, run_forward(): pl.pallas_call(functools.partial(forward_kernel, dims, lat), out_shape=(r...  148 us
    pallas_call x1, Pallas kernels, run_widen(): pl.pallas_call(functools.partial(widen_kernel, dims), out_shape=tuple((ja...  14.1 us
    unnamed x9, local copies, waits for them, and re-layouts  7.27 us

profile of v2, /device:TPU:0, one launch (start us, length us, event | category | flops | bytes accessed | tf_op | source)
XLA Modules:
  0.0 330.7 jit_solution(9302550445205523431)
XLA Ops:
  0.6 0.8 convert_reduce_fusion.1
  1.4 0.3 dynamic_update_slice.6
  1.7 0.3 dynamic_update_slice.7
  2.0 0.7 convert_dynamic-update-slice_fusion.3
  2.7 0.7 convert_dynamic-update-slice_fusion.2
  3.4 0.7 convert_dynamic-update-slice_fusion.1
  4.1 0.7 convert_dynamic-update-slice_fusion
  4.8 0.6 reshape.45.vec_ref
  5.4 5.2 %copy.28 = bf16[1152,1152]{0,1:T(8,128)(2,1)} copy(bf16[1152,1152]{1,0:T(8,128)(2,1)} %param.25) | data formatting | bytes 5308416 | tf_op args[10]
  10.6 148.2 %forward_attention.1 = (bf16[256,1152]{1,0:T(8,128)(2,1)}, bf16[256,1152]{1,0:T(8,128)(2,1)}, bf16[256,1152]{1,0:T(8,128)(2,1)}, bf16[256,1152]{1,0:T(8,128)(2,1...) custom-call(s32[8]{0:T(128)} %bucket_ref.3, ...), custom_call_target="tpu_custom_call" | custom-call | tf_op jit(solution)/shard_map/forward_attention/pallas_call | solution.py:618
  158.8 149.1 %backward_attention.1 = (bf16[2,256,1152]{2,1,0:T(8,128)(2,1)}, bf16[2,256,1152]{2,1,0:T(8,128)(2,1)}, bf16[1152,1152]{1,0:T(8,128)(2,1)}, bf16[1152,1280]{1,0:T...) custom-call(s32[8]{0:T(128)} %bucket_ref.3, s32[2,128]{1,0:T(2,128)} %kept_ref.3, ...), custom_call_target="tpu_custom_call" | custom-call | tf_op jit(solution)/shard_map/backward_attention/pallas_call | solution.py:984
  308.0 1.7 convert_reduce_fusion
  309.7 0.0 copy-start.1
  309.7 14.1 %widen_gradients.1 = (f32[864,1152]{1,0:T(8,128)}, f32[288,1152]{1,0:T(8,128)}, f32[1152,1152]{1,0:T(8,128)}, f32[1152,1152]{1,0:T(8,128)}, f32[1728,1152]{1,0:T...) custom-call(bf16[1152,1152]{1,0:T(8,128)(2,1)} %get-tuple-element.55.ga_ref, ...), custom_call_target="tpu_custom_call" | custom-call | tf_op jit(solution)/shard_map/widen_gradients/pallas_call | solution.py:1065
  323.8 0.0 copy-start
  323.8 1.4 reduce.2
  325.3 0.8 slice.20
  326.0 1.5 slice_reduce_fusion
  327.5 0.7 constant_dynamic-slice_fusion
  328.2 0.0 copy-done.1
  328.2 1.0 copy.39
  329.2 0.0 copy-done
  329.2 1.0 copy.40
  (5 shorter events, 0.0 us)
Async XLA Ops:
  309.7 18.5 %copy-start.1 = (bf16[2,256,1152]{2,1,0:T(8,128)(2,1)S(1)}, bf16[2,256,1152]{2,1,0:T(8,128)(2,1)}, u32[]{:S(2)}) copy-start(bf16[2,256,1152]{2,1,0:T(8,128)(2,1)} %get-tuple-element.82) | copy-start | bytes 3538948
  323.8 5.3 %copy-start = (bf16[2,256,1152]{2,1,0:T(8,128)(2,1)S(1)}, bf16[2,256,1152]{2,1,0:T(8,128)(2,1)}, u32[]{:S(2)}) copy-start(bf16[2,256,1152]{2,1,0:T(8,128)(2,1)} %get-tuple-element.83) | copy-start | bytes 3538948

commit v3 on v2

--- a/solution.py
+++ b/solution.py
@@ -96,8 +96,10 @@
             device_id=(flip(self.b, 1), self.z), device_id_type=MESH,
         ).wait_recv()
 
-    def step(self, i):
+    def step(self, i, only=None):
         for p, order in enumerate(self.orders):
+            if only is not None and p != only:
+                continue
             if i == 0:
                 fresh = [0]
             elif i <= len(order):
@@ -254,12 +256,23 @@
 
 
 def forward_kernel(
-    dims, lat, bucket_ref, cond_ref, tok_ref, cot_in_ref, kept_ref, vec_ref,
-    wada_hbm, own_qkv, own_proj, own_1, own_2,
-    attn_in_o, q_o, k_o, v_o, merged_o, attn_out_o, hidden_o, cot_o, mod_o, din_o, zp_o, g1_o, g2_o, full_o,
-    full, sm_send, sm_recv, nrm, sel, mg, mod8, all_1, all_2, d_all, xb, act, dpre, y, inbox, bcol,
-    sm_ss, sm_rs, za_ss, za_rs, zm_ss, zm_rs, ga_ss, ga_rs, gd_ss, gd_rs, ag_ss, ag_rs, rs_ss, rs_rs, loc,
+    dims, lat, bucket_ref, cond_ref, tok_ref, cot_in_ref, kept_ref, projb_ref, qvb_ref, adab_ref, expb_ref,
+    wada_hbm, own_qkv, own_proj, own_1, own_2, *rest,
 ):
+    outs, rest = rest[:14], rest[14:]
+    kept, rest = rest[:13], rest[13:]
+    (attn_in_o, q_o, k_o, v_o, merged_o, attn_out_o, hidden_o, cot_o, mod_o, din_o, zp_o, g1_o, g2_o) = kept
+    (full, sm_send, sm_recv, nrm, sel, mg, mod8, all_1, all_2, d_all, xb, act, dpre, y, inbox, wexp, qvs,
+     sm_ss, sm_rs, za_ss, za_rs, zm_ss, zm_rs, ga_ss, ga_rs, gd_ss, gd_rs, ag_ss, ag_rs, rs_ss, rs_rs, loc, out_sem) = rest
+    full_o = outs[13]
+    given = []
+
+    def give(first, last):
+        for k in range(first, last):
+            cp = pltpu.make_async_copy(kept[k], outs[k], out_sem.at[k])
+            cp.start()
+            given.append(cp)
+
     group, count, rows_s, width = dims
     b, z = lax.axis_index("batch"), lax.axis_index("tp")
     g = b % group
@@ -271,6 +284,10 @@
     cols = wada_hbm.shape[0]
     load_ada = pltpu.make_async_copy(wada_hbm, y.at[0:cols], loc.at[1])
     load_ada.start()
+    hid_s = expb_ref.shape[0]
+    if hid_s == width:
+        wexp = y.at[0:width]
+    load_exp = pltpu.make_async_copy(own_1, wexp, loc.at[2])
     real = [kept_half(bucket_ref[z * lat + l], positions) for l in range(lat)]
     barrier(b, z, group, count)
 
@@ -289,26 +306,34 @@
     for cp in own_copy:
         cp.start()
 
-    def line_a(shard, src, step, k):
+    def line_a(shard, step, k, p):
+        ref = piece(g, shard, p)
         return pltpu.make_async_remote_copy(
-            src_ref=src, dst_ref=piece(g, shard, None), send_sem=za_ss.at[k], recv_sem=za_rs.at[shard],
+            src_ref=ref, dst_ref=ref, send_sem=za_ss.at[p, k], recv_sem=za_rs.at[p, shard],
             device_id=(b, z + step), device_id_type=MESH,
         )
 
-    def line_m(shard, src1, src2, step, k):
-        return [
-            pltpu.make_async_remote_copy(
-                src_ref=src, dst_ref=dst.at[shard], send_sem=zm_ss.at[i, k], recv_sem=zm_rs.at[i, shard],
-                device_id=(b, z + step), device_id_type=MESH,
-            )
-            for i, (src, dst) in enumerate(((src1, all_1), (src2, all_2)))
-        ]
+    def line_m(shard, step, k, i):
+        ref = (all_1, all_2)[i].at[shard]
+        return pltpu.make_async_remote_copy(
+            src_ref=ref, dst_ref=ref, send_sem=zm_ss.at[i, k], recv_sem=zm_rs.at[i, shard],
+            device_id=(b, z + step), device_id_type=MESH,
+        )
+
+    def passes_on(shard):
+        return ((shard < z) & (z < count - 1)) | ((shard > z) & (z > 0))
+
+    def pass_on(shard, fn):
+        @pl.when((shard < z) & (z < count - 1))
+        def _():
+            fn(1)
+
+        @pl.when((shard > z) & (z > 0))
+        def _():
+            fn(-1)
 
     slice_at = pl.ds(pl.multiple_of(g * rows_s, 16), rows_s)
-    own_m = [
-        pltpu.make_async_copy(own_1.at[slice_at], all_1.at[z, :, 0:width], loc.at[2]),
-        pltpu.make_async_copy(own_2.at[slice_at], all_2.at[z], loc.at[3]),
-    ]
+    own_m = [pltpu.make_async_copy(own_2.at[slice_at], all_2.at[z], loc.at[3])]
     for cp in own_m:
         cp.start()
 
@@ -323,18 +348,27 @@
 
     for cp in own_copy:
         cp.wait()
-    both_ways(lambda step, k: line_a(z, piece(g, z, None), step, k).start())
+    def start_own_a(step, k):
+        for p in range(2):
+            line_a(z, step, k, p).start()
+
+    both_ways(start_own_a)
 
     cond = cond_ref[...].astype(F32)
     silu = (cond / (1.0 + jnp.exp(-cond))).astype(BF)
-    mod8[...] = jnp.concatenate([vec_ref[4:5], vec_ref[5:6]], axis=1) + jnp.zeros_like(mod8)
+    mod8[...] = jnp.zeros_like(mod8)
+    mod8[:, 0:cols] = adab_ref[...].astype(F32).reshape(1, cols) + jnp.zeros((mod8.shape[0], cols), F32)
+    qvs[...] = jnp.zeros_like(qvs)
+    qvs[0:2, 0:ds] = qvb_ref[...].astype(F32)
+    qv_own = pltpu.roll(qvs[...], z * ds, 1)[0:2]
     load_ada.wait()
     mod8[:, 0:cols] += nt(silu, y[0:cols])
+    load_exp.start()
     framed = pltpu.roll(mod8[...], (z * cols) % width, 1)
     for t in range(count):
         for i in range(2):
             sm_send[t, i] = framed[lat * t : lat * (t + 1), i * width : (i + 1) * width]
-        sm_send[t, 2] = vec_ref[2:4]
+        sm_send[t, 2] = qv_own
 
     def small(d):
         peer = lax.rem(z + d, count)
@@ -357,12 +391,14 @@
         nrm[at] = center * inv
         cot_o[at] = (tn(pick, cot_in_ref[l]) * row_mask(real[l], slots)).astype(BF)
 
-    hid_s = own_1.shape[0]
-    first_row = lax.broadcasted_iota(jnp.int32, (8, 1), 0) == 0
-    corner = jnp.where(first_row & (lax.broadcasted_iota(jnp.int32, (1, 128), 1) == 0), 1.0, 0.0)
-    bias_row = jnp.where(first_row, vec_ref[6:7, 0:hid_s], 0.0)
-    bcol[...] = tn(bias_row.astype(BF), corner.astype(BF)).astype(BF)
-    all_1[z, :, width:] = bcol[slice_at]
+    take = lax.broadcasted_iota(jnp.int32, (rows_s, hid_s), 1) - lax.broadcasted_iota(jnp.int32, (rows_s, hid_s), 0)
+    take = jnp.where(take == g * rows_s, 1.0, 0.0).astype(BF)
+    load_exp.wait()
+    all_1[z, :, 0:width] = nt(take, wexp[...]).astype(BF)
+    bias_row = jnp.where(
+        lax.broadcasted_iota(jnp.int32, (128, 1), 0) == 0, expb_ref[...].astype(F32).reshape(1, hid_s), 0.0
+    )
+    all_1[z, :, width:] = nt(take, bias_row.astype(BF)).astype(BF)
 
     gathers = []
     for k in range(count - 1):
@@ -377,41 +413,59 @@
 
     def arrive_a(k):
         shard = near_shard(z, k, count)
-        ref = piece(g, shard, None)
-        line_a(shard, ref, 0, 2 + k).wait_recv()
-        gathers[k].step(0)
-
-        @pl.when((shard < z) & (z < count - 1))
+        for p in range(2):
+            line_a(shard, 0, 2 + k, p).wait_recv()
+            pass_on(shard, lambda step, p=p: line_a(shard, step, 2 + k, p).start())
+            gathers[k].step(0, p)
+
+    four = count == 4
+    inner = (z > 0) & (z < count - 1)
+    across = lax.rem(z + 2, count)
+
+    def far_m(i):
+        return line_m(z, across - z, 2, i)
+
+    def relay_m(i):
+        return line_m(across, 2 * z - 3, 3, i)
+
+    def arrive_m(k, i):
+        if four:
+            return
+        shard = near_shard(z, k, count)
+
+        @pl.when(passes_on(shard))
         def _():
-            line_a(shard, ref, 1, 2 + k).start()
-
-        @pl.when((shard > z) & (z > 0))
-        def _():
-            line_a(shard, ref, -1, 2 + k).start()
-
-    def arrive_m(k):
-        shard = near_shard(z, k, count)
-        r1, r2 = all_1.at[shard], all_2.at[shard]
-        for cp in line_m(shard, r1, r2, 0, 2 + k):
-            cp.wait_recv()
-
-        @pl.when((shard < z) & (z < count - 1))
-        def _():
-            for cp in line_m(shard, r1, r2, 1, 2 + k):
-                cp.start()
-
-        @pl.when((shard > z) & (z > 0))
-        def _():
-            for cp in line_m(shard, r1, r2, -1, 2 + k):
-                cp.start()
+            line_m(shard, 0, 2 + k, i).wait_recv()
+
+        pass_on(shard, lambda step: line_m(shard, step, 2 + k, i).start())
+
+    def send_far():
+        if four:
+            for i in range(2):
+                far_m(i).start()
+
+    def relay():
+        if four:
+
+            @pl.when(inner)
+            def _():
+                for i in range(2):
+                    relay_m(i).wait_recv()
+                    relay_m(i).start()
 
     def send_m(step, k):
-        for cp in line_m(z, all_1.at[z], all_2.at[z], step, k):
-            cp.start()
-
+        for i in range(2):
+            line_m(z, step, k, i).start()
+
+    ends = (z == 0) | (z == count - 1)
     arrive_a(0)
     for cp in own_m:
         cp.wait()
+
+    @pl.when(ends)
+    def _():
+        send_far()
+        both_ways(send_m)
 
     for d in range(1, count):
         peer = lax.rem(z + d, count)
@@ -441,7 +495,11 @@
     for k in range(1, count - 1):
         arrive_a(k)
         if k == 1:
-            both_ways(send_m)
+
+            @pl.when(jnp.logical_not(ends))
+            def _():
+                both_ways(send_m)
+
         gathers[k - 1].step(1)
     depth = gathers[0].steps()
     todo = [(i, k) for k in range(count - 1) for i in range(1, depth) if not (i == 1 and k < count - 2)]
@@ -455,7 +513,13 @@
     for i, k in todo:
         if i >= links and not started:
             dm.step(0)
-            arrive_m(0)
+
+            @pl.when(inner)
+            def _():
+                send_far()
+
+            arrive_m(0, 0)
+            arrive_m(0, 1)
             started = True
         gathers[k].step(i)
     for k in range(count - 1):
@@ -463,8 +527,10 @@
     full_out = pltpu.make_async_copy(full, full_o, loc.at[4])
     full_out.start()
 
-    for k in range(1, count - 2):
-        arrive_m(k)
+    if count > 2:
+        arrive_m(1, 0)
+        arrive_m(1, 1)
+    relay()
     dm.step(1)
 
     x = attn_in_o[...]
@@ -493,11 +559,16 @@
                 mg[at, win] = jnp.where(own > 0, o, mg[at, win])
         return 0
 
-    lax.fori_loop(0, heads // 2, some_heads, 0)
+    lax.fori_loop(0, heads // 4, some_heads, 0)
+    for k in range(2, count - 1):
+        arrive_m(k, 0)
     for i in range(2, dm.steps()):
         dm.step(i)
+    lax.fori_loop(heads // 4, heads // 2, some_heads, 0)
+    for k in range(2, count - 1):
+        arrive_m(k, 1)
     merged_o[...] = mg[...].astype(BF)
-    a_out = nn(merged_o[...], full[3].reshape(width, width)) + vec_ref[0:1]
+    a_out = nn(merged_o[...], full[3].reshape(width, width)) + projb_ref[...].astype(F32).reshape(1, width)
     attn_out_o[...] = a_out
     for l in range(lat):
         at = slice(l * slots, (l + 1) * slots)
@@ -506,6 +577,8 @@
         center, inv = stats(mixed)
         xb[0, at] = (center * inv * (1.0 + mod_o[4, l : l + 1]) + mod_o[3, l : l + 1]).astype(BF)
 
+    give(0, 9)
+
     def part(ref):
         return lambda m, p: ref.at[m, pl.ds(p * half, half)]
 
@@ -513,7 +586,14 @@
         b, z, group, lambda m, p, slot: part(xb)(slot, p), lambda m, p: ag_ss.at[p, m], lambda m, p: ag_rs.at[p, m]
     )
     gather.step(0)
-    arrive_m(count - 2)
+    for k in range(count - 1):
+        shard = near_shard(z, k, count)
+
+        @pl.when(jnp.logical_not(inner & (shard == across)) if four else jnp.logical_not(passes_on(shard)))
+        def _():
+            for i in range(2):
+                line_m(shard, 0, 2 + k, i).wait_recv()
+
     hid = count * rows_s
     bias = nt(jnp.ones((8, all_1.shape[2] - width), BF), all_1[:, :, width:].reshape(hid, all_1.shape[2] - width))[0:1]
 
@@ -574,34 +654,48 @@
         g2_o[c] = tn(act[:, c], d_all[...].reshape(group * rows, width)).astype(BF)
     for m in range(group):
         zp_o[m] = nn(act[m * rows : (m + 1) * rows], all_2[...].reshape(hid, width)).astype(BF)
+    give(10, 13)
     rs.finish(din_o, half)
+    give(9, 10)
     gather.wait_sent()
     rs.rs.wait_sent()
 
     for d in range(1, count):
         small(d).wait_send()
-    both_ways(lambda step, k: line_a(z, piece(g, z, None), step, k).wait_send())
-
-    def sent_m(step, k):
-        for cp in line_m(z, all_1.at[z], all_2.at[z], step, k):
-            cp.wait_send()
-
-    both_ways(sent_m)
+
+    def sent_own(step, k):
+        for i in range(2):
+            line_a(z, step, k, i).wait_send()
+            line_m(z, step, k, i).wait_send()
+
+    both_ways(sent_own)
+    if four:
+        for i in range(2):
+            far_m(i).wait_send()
+
+        @pl.when(inner)
+        def _():
+            for i in range(2):
+                relay_m(i).wait_send()
+
     for k in range(count - 1):
         shard = near_shard(z, k, count)
 
-        @pl.when(((shard < z) & (z < count - 1)) | ((shard > z) & (z > 0)))
+        @pl.when(passes_on(shard))
         def _():
-            line_a(shard, piece(g, shard, None), 0, 2 + k).wait_send()
-            for cp in line_m(shard, all_1.at[shard], all_2.at[shard], 0, 2 + k):
-                cp.wait_send()
+            for i in range(2):
+                line_a(shard, 0, 2 + k, i).wait_send()
+                if not four:
+                    line_m(shard, 0, 2 + k, i).wait_send()
 
         gathers[k].wait_sent()
     dm.wait_sent()
     full_out.wait()
-
-
-def run_forward(dims, lat, bucket, cond, tok, cot, kept, vec, wada, own_qkv, own_proj, own_1, own_2):
+    for cp in given:
+        cp.wait()
+
+
+def run_forward(dims, lat, bucket, cond, tok, cot, kept, projb, qvb, adab, expb, wada, own_qkv, own_proj, own_1, own_2):
     group, count, rows_s, width = dims
     slots = kept.shape[1]
     rows = lat * slots
@@ -615,15 +709,16 @@
     blocks = sd((group, rows, width), BF)
     dma = pltpu.SemaphoreType.DMA
     vmem = pltpu.VMEM
+    outs = (
+        row_bf, row_bf, row_bf, row_bf, row_bf, row_f, row_f, row_bf, sd((6, lat, width), F32),
+        row_f, blocks, sd((hid, ext), BF), sd((hid, width), BF), sd((4, count, width // count, width), BF),
+    )
     return pl.pallas_call(
         functools.partial(forward_kernel, dims, lat),
-        out_shape=(
-            row_bf, row_bf, row_bf, row_bf, row_bf, row_f, row_f, row_bf, sd((6, lat, width), F32),
-            row_f, blocks, sd((hid, ext), BF), sd((hid, width), BF), sd((4, count, width // count, width), BF),
-        ),
-        in_specs=[sm] + [vm] * 5 + [hb] * 5,
-        out_specs=tuple([vm] * 13 + [hb]),
-        scratch_shapes=[
+        out_shape=outs,
+        in_specs=[sm] + [vm] * 8 + [hb] * 5,
+        out_specs=tuple([hb] * 14),
+        scratch_shapes=[vmem(item.shape, item.dtype) for item in outs[:13]] + [
             vmem((4, count, width // count, width), BF),
             vmem((count, 3, lat, width), F32), vmem((count, 3, lat, width), F32),
             vmem((rows, width), F32), vmem((rows, width), F32), vmem((rows, width), F32),
@@ -632,27 +727,42 @@
             vmem((group, rows, width), BF), vmem((group, rows, width), BF),
             vmem((group * rows, hid), BF), vmem((group * rows, hid), BF),
             vmem((group * rows, width), BF), vmem((group - 1, rows, width), BF),
-            vmem((own_1.shape[0], 128), BF),
+            vmem((16, 128) if own_1.shape[1] == width else own_1.shape, BF), vmem((8, width), F32),
             dma((count,)), dma((count,)),
-            dma((count + 1,)), dma((count,)),
+            dma((2, count + 1)), dma((2, count)),
             dma((2, count + 1)), dma((2, count)),
             dma((count - 1, 2, group)), dma((count, 2, group)),
             dma((2, group)), dma((2, group)), dma((2, group)), dma((2, group)), dma((2, group)), dma((2, group)),
-            dma((7,)),
+            dma((7,)), dma((14,)),
         ],
         compiler_params=pltpu.CompilerParams(collective_id=1, has_side_effects=True, vmem_limit_bytes=63 * MIB),
         name="forward_attention",
-    )(bucket, cond, tok, cot, kept, vec, wada, own_qkv, own_proj, own_1, own_2)
-
-
-def backward_kernel(
-    dims, lat, bucket_ref, kept_ref, tok_ref, cot_in_ref, attn_in_ref, q_ref, k_ref, v_ref, merged_ref,
-    attn_out_ref, hidden_ref, cot_ref, mod_ref, d_in_ref, vec_ref, cond_ref,
-    full_ref, g1_ref, g2_ref, zp_ref,
-    out_o, dtok_o, ga_o, gm1_o, gm2_o, small_o,
-    wbuf, gbuf, abox, ar, gm1, gm2, mr1, mr2, back_b, d3, d_attn, dm, dain, mlp, inbox, sm_send, sm_recv, dmod,
-    loc, ro_ss, ro_rs, ra_ss, ra_rs, za_ss, za_rs, zm_ss, zm_rs, gm_ss, gm_rs, ga_ss, ga_rs, sz_ss, sz_rs, sp_ss, sp_rs,
-):
+    )(bucket, cond, tok, cot, kept, projb, qvb, adab, expb, wada, own_qkv, own_proj, own_1, own_2)
+
+
+def backward_kernel(dims, lat, bucket_ref, kept_ref, redb_ref, cond_ref, *rest):
+    held, rest = rest[:12], rest[12:]
+    (full_ref, g1_ref, g2_ref, zp_ref), rest = rest[:4], rest[4:]
+    outs, rest = rest[:3], rest[3:]
+    (ga_o, gm1_o, gm2_o), rest = rest[:3], rest[3:]
+    local, rest = rest[:12], rest[12:]
+    (tok_ref, cot_in_ref, attn_in_ref, q_ref, k_ref, v_ref, merged_ref, attn_out_ref, hidden_ref, cot_ref, mod_ref,
+     d_in_ref) = local
+    small_o, rest = rest[0], rest[1:]
+    out_o, dtok_o, dain, mlp = tok_ref, cot_in_ref, d_in_ref, hidden_ref
+    (wbuf, gbuf, abox, ar, gm1, gm2, mr1, mr2, back_b, d3, d_attn, dm, inbox, sm_send, sm_recv, dmod,
+     loc, in_sem, out_sem, ro_ss, ro_rs, ra_ss, ra_rs, za_ss, za_rs, zm_ss, zm_rs, gm_ss, gm_rs, ga_ss, ga_rs, sz_ss, sz_rs,
+     sp_ss, sp_rs) = rest
+    takes = [pltpu.make_async_copy(held[k], local[k], in_sem.at[k]) for k in range(12)]
+
+    def need(*which):
+        for k in which:
+            takes[k].wait()
+
+    gives = [
+        pltpu.make_async_copy(src, dst, out_sem.at[k])
+        for k, (src, dst) in enumerate(zip((out_o, dtok_o, small_o), outs))
+    ]
     group, count, rows_s, width = dims
     b, z = lax.axis_index("batch"), lax.axis_index("tp")
     g = b % group
@@ -669,8 +779,11 @@
         pltpu.make_async_copy(full_ref.at[0], wbuf.at[1], loc.at[3]),
         pltpu.make_async_copy(zp_ref, gbuf.at[0 : group * rows], loc.at[5]),
     ]
-    for cp in loads:
+    for cp in (loads[4], loads[0], loads[1], takes[8], takes[9], takes[10], takes[11], takes[7], loads[2]):
         cp.start()
+    for k in (6, 3, 4, 5, 2, 0, 1):
+        takes[k].start()
+    loads[3].start()
     real = [kept_half(bucket_ref[z * lat + l], positions) for l in range(lat)]
     barrier(b, z, group, count)
 
@@ -691,20 +804,90 @@
     loads[0].wait()
     loads[1].wait()
 
-    def line_m(d):
-        peer = lax.rem(z + d, count)
-        at = pl.ds(pl.multiple_of(peer * rows_s, 16), rows_s)
+    four = count == 4
+    inner = (z > 0) & (z < count - 1)
+    across = lax.rem(z + 2, count)
+    sums = ((gm1, mr1), (gm2, mr2))
+
+    def rows_for(shard):
+        return pl.ds(pl.multiple_of(shard * rows_s, 16), rows_s)
+
+    def line_m(shard, peer, box, k):
         return [
             pltpu.make_async_remote_copy(
-                src_ref=src.at[at], dst_ref=dst.at[d - 1], send_sem=zm_ss.at[i, d], recv_sem=zm_rs.at[i, d],
+                src_ref=src.at[rows_for(shard)], dst_ref=dst.at[box], send_sem=zm_ss.at[i, k], recv_sem=zm_rs.at[i, box],
                 device_id=(b, peer), device_id_type=MESH,
             )
-            for i, (src, dst) in enumerate(((gm1, mr1), (gm2, mr2)))
+            for i, (src, dst) in enumerate(sums)
         ]
 
-    for d in range(1, count):
-        for cp in line_m(d):
+    def start(copies):
+        for cp in copies:
             cp.start()
+
+    def wait_in(box):
+        for cp in line_m(z, z, box, 0):
+            cp.wait_recv()
+
+    def wait_out(copies):
+        for cp in copies:
+            cp.wait_send()
+
+    def line_sends(fn):
+        if not four:
+            for d in range(1, count):
+                peer = lax.rem(z + d, count)
+                fn(line_m(peer, peer, d - 1, d - 1))
+            return
+
+        @pl.when(jnp.logical_not(inner))
+        def _():
+            fn(line_m(count - 1 - z, jnp.where(z == 0, 1, count - 2), 3, 3))
+            fn(line_m(across, across, 2, 2))
+
+        @pl.when(z < count - 1)
+        def _():
+            fn(line_m(z + 1, z + 1, 0, 0))
+
+        @pl.when(z > 0)
+        def _():
+            fn(line_m(z - 1, z - 1, 1, 1))
+
+    def line_relay(fn):
+        if four:
+
+            @pl.when(inner)
+            def _():
+                fn(line_m(across, across, 2, 2))
+
+    def relay_add():
+        if four:
+
+            @pl.when(inner)
+            def _():
+                wait_in(3)
+                for src, box in sums:
+                    at = rows_for(across)
+                    src[at] = (src[at].astype(F32) + box[3].astype(F32)).astype(BF)
+
+        line_relay(start)
+
+    def line_total():
+        def take(box):
+            wait_in(box)
+            for src, boxes in sums:
+                at = rows_for(z)
+                src[at] = (src[at].astype(F32) + boxes[box].astype(F32)).astype(BF)
+
+        if four:
+            pl.when(z > 0)(lambda: take(0))
+            pl.when(z < count - 1)(lambda: take(1))
+            take(2)
+        else:
+            for d in range(count - 1):
+                take(d)
+
+    line_sends(start)
 
     def rows_of(l):
         return slice(l * slots, (l + 1) * slots)
@@ -717,6 +900,7 @@
 
     for m in range(group - 2, 0, -2):
         rs_out.last_link(m)
+    need(7, 8, 9, 10, 11)
     for l in range(lat):
         at = rows_of(l)
         one = slice(l, l + 1)
@@ -742,6 +926,7 @@
             to = slice(c, c + chunk)
             gbuf[j * width + c : j * width + c + chunk] = tn(left(to), right).astype(BF)
 
+    need(6)
     weight_grad(3, lambda to: merged_ref[:, to], d_attn[...])
 
     heads = width // HEAD_SIZE
@@ -765,16 +950,19 @@
                     d3[j, at, win] = jnp.where(own > 0, grad, d3[j, at, win].astype(F32)).astype(BF)
         return 0
 
+    need(3, 4, 5)
     lax.fori_loop(0, heads // 4, some_heads, 0)
     for i in range(rs_out.links - 1, 0, -1):
         rs_out.link(i)
+    relay_add()
     lax.fori_loop(heads // 4, heads // 2, some_heads, 0)
     rs_out.finish(mlp, half)
-    mlp[...] += vec_ref[1:2]
+    mlp[...] += redb_ref[...].astype(F32).reshape(1, width)
     for l in range(lat):
         dmod[5, l : l + 1] = total(cot_ref[rows_of(l)].astype(F32) * mlp[rows_of(l)])
     rs_out.rs.wait_sent()
 
+    need(2)
     for j in range(3):
         weight_grad(j, lambda to, j=j: d3[j, :, to], attn_in_ref[...])
 
@@ -849,6 +1037,7 @@
         high = rows.astype(BF)
         return nn(pick, high) + nn(pick, (rows - high.astype(F32)).astype(BF))
 
+    need(0, 1)
     for l in range(lat):
         at = rows_of(l)
         one = slice(l, l + 1)
@@ -860,6 +1049,8 @@
         dmod[1, one] = total(d_ai * n)
         d_sel = back_b[at] + back(n, inv, d_ai * (1.0 + mod_ref[1, one]))
         dtok_o[l] = (cot_in_ref[l].astype(F32) + put(pick, d_sel)).astype(BF)
+
+    gives[1].start()
 
     cols = 6 * width // count
     vectors = [
@@ -893,6 +1084,7 @@
         pick = placing(kept_ref[one], positions)
         delta = (mod_ref[2, one] * attn_out_ref[at] + mod_ref[5, one] * mlp[at]) * row_mask(real[l], slots)
         out_o[l] = (tok_ref[l].astype(F32) + put(pick, delta)).astype(BF)
+    gives[0].start()
     for d in range(1, count):
         ref = sm_recv.at[lax.rem(z - d + count, count)]
         pltpu.make_async_remote_copy(
@@ -915,11 +1107,6 @@
         b, z, group, lambda m, p, slot: small_o.at[slot], lambda m, p: sp_ss.at[m], lambda m, p: sp_rs.at[m], halves=1
     )
     sp.step(0)
-    for t in range(3, count + links - 1):
-        wave_round(t)
-        if t - 2 < sp.steps():
-            sp.step(t - 2)
-
     def spread(out, ss, rs):
         def region(m, p, slot):
             lo, ln = parts[p]
@@ -928,20 +1115,20 @@
         return Gather(b, z, group, region, lambda m, p: ss.at[p, m], lambda m, p: rs.at[p, m])
 
     g_at = pl.ds(pl.multiple_of(g * rows_s, 16), rows_s)
-    z_at = pl.ds(pl.multiple_of(z * rows_s, 16), rows_s)
-    for d in range(1, count):
-        for cp in line_m(d):
-            cp.wait_recv()
-    for own, box, out in ((gm1, mr1, gm1_o), (gm2, mr2, gm2_o)):
-        acc = own[z_at].astype(F32)
-        for d in range(count - 1):
-            acc = acc + box[d].astype(F32)
-        out[g_at] = acc.astype(BF)
+    line_total()
+    for own, out in ((gm1, gm1_o), (gm2, gm2_o)):
+        out[g_at] = own[rows_for(z)]
     spread_1 = spread(gm1_o, gm_ss.at[0], gm_rs.at[0])
     spread_2 = spread(gm2_o, gm_ss.at[1], gm_rs.at[1])
     spread_1.step(0)
     spread_2.step(0)
-    wave_round(count + links - 1)
+    for t in range(3, count + links):
+        wave_round(t)
+        if t - 2 < sp.steps():
+            sp.step(t - 2)
+        if t == 4:
+            spread_1.step(1)
+            spread_2.step(1)
     acc = own_slice(z)[...].astype(F32)
     for w in range(count - 1):
         line_a(w).wait_recv()
@@ -950,25 +1137,32 @@
     spread_a = spread(ga_o, ga_ss, ga_rs)
     spread_a.step(0)
     for i in range(1, spread_a.steps()):
-        for item in (spread_1, spread_2, spread_a):
-            item.step(i)
-    for i in range(max(1, count + links - 3), sp.steps()):
+        for item in (spread_1, spread_2):
+            if i > 1:
+                item.step(i)
+        spread_a.step(i)
+    for i in range(max(1, count + links - 2), sp.steps()):
         sp.step(i)
+    sp.wait_core()
+    gives[2].start()
+    for item in (spread_1, spread_2, spread_a):
+        item.wait_core()
     for item in (sp, spread_a, spread_1, spread_2):
-        item.wait_core()
         item.wait_sent()
+    for cp in gives:
+        cp.wait()
     for rs in waves:
         rs.wait_sent()
     for w in range(count - 1):
         line_a(w).wait_send()
     for d in range(1, count):
         small(d).wait_send()
-        for cp in line_m(d):
-            cp.wait_send()
+    line_sends(wait_out)
+    line_relay(wait_out)
 
 
 def run_backward(
-    dims, lat, bucket, kept, tok, cot_in, attn_in, q, k, v, merged, attn_out, hidden, cot, mod, d_in, vec, cond,
+    dims, lat, bucket, kept, tok, cot_in, attn_in, q, k, v, merged, attn_out, hidden, cot, mod, d_in, redb, cond,
     full, g1, g2, zp,
 ):
     group, count, rows_s, width = dims
@@ -980,34 +1174,36 @@
     dma = pltpu.SemaphoreType.DMA
     vmem = pltpu.VMEM
     ext = g1.shape[1]
+    boxes = max(4, count - 1)
     small = (group, 4, cond.shape[0], width)
+    held = (tok, cot_in, attn_in, q, k, v, merged, attn_out, hidden, cot, mod, d_in)
     return pl.pallas_call(
         functools.partial(backward_kernel, dims, lat),
         out_shape=(
-            sd(tok.shape, BF), sd(tok.shape, BF), sd((group * rows_s, width), BF),
-            sd((group * rows_s, ext), BF), sd((group * rows_s, width), BF), sd(small, F32),
+            sd(tok.shape, BF), sd(tok.shape, BF), sd(small, F32),
+            sd((group * rows_s, width), BF), sd((group * rows_s, ext), BF), sd((group * rows_s, width), BF),
         ),
-        in_specs=[sm] + [vm] * 15 + [hb] * 4,
-        out_specs=tuple([vm] * 6),
-        scratch_shapes=[
+        in_specs=[sm] + [vm] * 3 + [hb] * 16,
+        out_specs=tuple([hb] * 3 + [vm] * 3),
+        scratch_shapes=[vmem(item.shape, item.dtype) for item in held] + [
+            vmem(small, F32),
             vmem((2, width, width), BF),
             vmem((4 * width, width), BF),
             vmem((count, group - 1, rows_s, width), BF),
             vmem((count - 1, rows_s, width), BF),
             vmem(g1.shape, BF), vmem(g2.shape, BF),
-            vmem((count - 1, rows_s, ext), BF), vmem((count - 1, rows_s, width), BF),
+            vmem((boxes, rows_s, ext), BF), vmem((boxes, rows_s, width), BF),
             vmem((rows, width), F32),
             vmem((3, rows, width), BF),
             vmem((rows, width), BF), vmem((rows, width), BF),
-            vmem((rows, width), F32), vmem((rows, width), F32),
             vmem((group - 1, rows, width), BF),
             vmem((count, 4, lat, width), F32), vmem((count, 4, lat, width), F32),
             vmem((6, lat, width), F32),
-            dma((6,)),
+            dma((6,)), dma((12,)), dma((3,)),
             dma((2, group)), dma((2, group)),
             dma((count, 2, group)), dma((count, 2, group)),
             dma((count,)), dma((count,)),
-            dma((2, count)), dma((2, count)),
+            dma((2, boxes)), dma((2, boxes)),
             dma((2, 2, group)), dma((2, 2, group)),
             dma((2, group)), dma((2, group)),
             dma((count,)), dma((count,)),
@@ -1015,42 +1211,53 @@
         ],
         compiler_params=pltpu.CompilerParams(collective_id=3, has_side_effects=True, vmem_limit_bytes=63 * MIB),
         name="backward_attention",
-    )(bucket, kept, tok, cot_in, attn_in, q, k, v, merged, attn_out, hidden, cot, mod, d_in, vec, cond, full, g1, g2, zp)
-
-
-def widen_kernel(dims, ga_ref, gm1_ref, gm2_ref, small_ref, qkv_o, proj_o, exp_o, red_o, ada_o, vec_o, addb_o,
-                 qkv, proj, exp, red, ada, sem):
+    )(bucket, kept, redb, cond, *held, full, g1, g2, zp)
+
+
+def widen_kernel(dims, ga_h, gm1_h, gm2_h, small_h, qkv_o, proj_o, exp_o, red_o, ada_o, adab_o, pair_o, projb_o, redb_o, expb_o,
+                 ga_ref, gm1_ref, gm2_ref, small_ref, qkv, proj, exp, red, ada, sem):
     group, count, rows_s, width = dims
     ds = width // count
     cols = ada.shape[0]
     members = small_ref.shape[0] * small_ref.shape[2]
-
-    def out(src, dst, k):
+    z = lax.axis_index("tp")
+
+    def move(src, dst, k):
         cp = pltpu.make_async_copy(src, dst, sem.at[k])
         cp.start()
         return cp
 
+    loads = [move(small_h, small_ref, 5), move(gm2_h, gm2_ref, 6), move(gm1_h, gm1_ref, 7), move(ga_h, ga_ref, 8)]
+
     def item(k):
         return small_ref[:, k].reshape(members, width)
 
+    loads[0].wait()
     pair = jnp.concatenate([item(0), item(1)], axis=1)
-    start = lax.rem(lax.axis_index("tp") * cols, width)
+    start = lax.rem(z * cols, width)
     pair = pltpu.roll(pair, lax.rem(2 * width - start, 2 * width), 1)[:, 0:cols]
-    addb_o[...] = jnp.sum(pair, axis=0, keepdims=True)
     ada[...] = tn(pair.astype(BF), item(3).astype(BF))
-    done = [out(ada, ada_o, 0)]
+    done = [move(ada, ada_o, 0)]
+    loads[1].wait()
     red[...] = gm2_ref[...].astype(F32)
-    done.append(out(red, red_o, 1))
+    done.append(move(red, red_o, 1))
+    loads[2].wait()
+    exp[...] = gm1_ref[:, 0:width].T.astype(F32)
+    done.append(move(exp, exp_o, 2))
+    loads[3].wait()
     qkv[...] = ga_ref[0 : 3 * ds].astype(F32)
-    done.append(out(qkv, qkv_o, 2))
+    done.append(move(qkv, qkv_o, 3))
     proj[...] = ga_ref[3 * ds :].astype(F32)
-    done.append(out(proj, proj_o, 3))
-    exp[...] = gm1_ref[:, 0:width].T.astype(F32)
-    done.append(out(exp, exp_o, 4))
+    done.append(move(proj, proj_o, 4))
+    adab_o[...] = jnp.sum(pair, axis=0)
     acc = small_ref[0, 2]
     for i in range(1, small_ref.shape[0]):
         acc = acc + small_ref[i, 2]
-    vec_o[...] = acc
+    redb_o[...] = acc[0]
+    projb_o[...] = acc[1]
+    pair_o[...] = pltpu.roll(acc, lax.rem(width - z * ds, width), 1)[2:4, 0:ds]
+    corner = lax.broadcasted_iota(jnp.int32, (8, 1), 0) + lax.broadcasted_iota(jnp.int32, (1, 128), 1)
+    expb_o[...] = nt(jnp.where(corner == 0, 1.0, 0.0).astype(BF), gm1_ref[:, width:])[0]
     for cp in done:
         cp.wait()
 
@@ -1060,17 +1267,21 @@
     ds = width // count
     vm = pl.BlockSpec(memory_space=pltpu.VMEM)
     hb = pl.BlockSpec(memory_space=pl.ANY)
-    big = [(3 * ds, width), (ds, width), (width, gm1.shape[0]), gm2.shape, (cols, width)]
-    vecs = [small.shape[2:], (1, cols)]
+    hid_s = gm1.shape[0]
+    big = [(3 * ds, width), (ds, width), (width, hid_s), gm2.shape, (cols, width)]
+    vecs = [(cols,), (2, ds), (width,), (width,), (hid_s,)]
+    given = (ga, gm1, gm2, small)
     return pl.pallas_call(
         functools.partial(widen_kernel, dims),
         out_shape=tuple(jax.ShapeDtypeStruct(item, F32) for item in big + vecs),
-        in_specs=[vm] * 4,
-        out_specs=tuple([hb] * 5 + [vm] * 2),
-        scratch_shapes=[pltpu.VMEM(item, F32) for item in big] + [pltpu.SemaphoreType.DMA((5,))],
+        in_specs=[hb] * 4,
+        out_specs=tuple([hb] * 5 + [vm] * 5),
+        scratch_shapes=[pltpu.VMEM(item.shape, item.dtype) for item in given]
+        + [pltpu.VMEM(item, F32) for item in big]
+        + [pltpu.SemaphoreType.DMA((9,))],
         compiler_params=pltpu.CompilerParams(vmem_limit_bytes=60 * MIB),
         name="widen_gradients",
-    )(ga, gm1, gm2, small)
+    )(*given)
 
 
 def body(
@@ -1083,25 +1294,13 @@
     dims = (group, count, shard_f // group, width)
     cols = ada_bias.shape[0]
 
-    def padded(part, size):
-        return jnp.pad(part.astype(F32), (0, size - part.shape[0]))
-
-    def framed(part):
-        return lax.dynamic_update_slice(jnp.zeros((width,), F32), part.astype(F32), (lax.axis_index("tp") * shard_w,))
-
-    vec = jnp.concatenate(
-        [
-            proj_bias.astype(F32), reduce_bias.astype(F32), framed(qv_bias[0]), framed(qv_bias[1]),
-            padded(ada_bias, 2 * width), padded(expand_bias, 2 * width),
-        ]
-    ).reshape(8, width)
     (attn_in, queries, key_rows, value_rows, merged, attn_out, hidden, cot, mod, d_in, zp, g1, g2, full) = run_forward(
-        dims, lat, bucket, conditioning, tokens, out_grad, kept_index, vec,
-        w_ada.T, jnp.swapaxes(w_qkv, 1, 2), w_proj, w_expand.T, w_reduce,
+        dims, lat, bucket, conditioning, tokens, out_grad, kept_index, proj_bias, qv_bias, ada_bias, expand_bias,
+        w_ada.T, jnp.swapaxes(w_qkv, 1, 2), w_proj, w_expand, w_reduce,
     )
-    output, tokens_grad, ga, gm1, gm2, small = run_backward(
+    output, tokens_grad, small, ga, gm1, gm2 = run_backward(
         dims, lat, bucket, kept_index, tokens, out_grad, attn_in, queries, key_rows, value_rows, merged,
-        attn_out, hidden, cot, mod, d_in, vec, conditioning,
+        attn_out, hidden, cot, mod, d_in, reduce_bias, conditioning,
         full.reshape(4, width, width), g1, g2, zp.reshape(-1, width),
     )
 
@@ -1111,22 +1310,21 @@
         return items
 
     ga, gm1, gm2 = over_batch((ga, gm1, gm2))
-    qkv_grad, proj_grad, expand_grad, reduce_grad, ada_grad, sums, ada_add = run_widen(dims, cols, ga, gm1, gm2, small)
-    ada_grad, sums, ada_add = over_batch((ada_grad, sums, ada_add))
-    pair_grad = lax.dynamic_slice_in_dim(sums[2:4], lax.axis_index("tp") * shard_w, shard_w, 1)
+    qkv_grad, proj_grad, expand_grad, reduce_grad, *sums = run_widen(dims, cols, ga, gm1, gm2, small)
+    ada_grad, ada_add, pair_grad, proj_add, reduce_add = over_batch(tuple(sums[:5]))
     return (
         output,
         tokens_grad,
         ada_grad.T,
-        ada_add.reshape(cols),
+        ada_add,
         jnp.swapaxes(qkv_grad.reshape(3, shard_w, width), 1, 2),
         pair_grad,
         proj_grad,
-        sums[1],
+        proj_add,
         expand_grad,
-        gm1[:, width].astype(F32),
+        sums[5],
         reduce_grad,
-        sums[0],
+        reduce_add,
     )
 
 

time: 336 us -> 299 us (0.89)
  the two profiles are of different devices: /device:TPU:0 before, /device:TPU:17 now
where the time goes in v3:
time: 299 us; the launch traced here: 294 us
  Pallas kernels  290 us (97%)
    pallas_call x1, Pallas kernels, run_backward(): pl.pallas_call(functools.partial(backward_kernel, dims, lat), out_shape=(...  140 us
    pallas_call x1, Pallas kernels, run_forward(): pl.pallas_call(functools.partial(forward_kernel, dims, lat), out_shape=ou...  138 us
    pallas_call x1, Pallas kernels, run_widen(): pl.pallas_call(functools.partial(widen_kernel, dims), out_shape=tuple((ja...  11.7 us

profile of v3, /device:TPU:17, one launch (start us, length us, event | category | flops | bytes accessed | tf_op | source)
XLA Modules:
  0.0 293.9 jit_solution(6909782891777904247)
XLA Ops:
  0.6 138.3 %forward_attention.1 = (bf16[256,1152]{1,0:T(8,128)(2,1)}, bf16[256,1152]{1,0:T(8,128)(2,1)}, bf16[256,1152]{1,0:T(8,128)(2,1)}, bf16[256,1152]{1,0:T(8,128)(2,1...) custom-call(s32[8]{0:T(128)} %bucket_ref.3, ...), custom_call_target="tpu_custom_call" | custom-call | tf_op jit(solution)/shard_map/forward_attention/pallas_call | solution.py:716
  138.9 140.4 %backward_attention.1 = (bf16[2,256,1152]{2,1,0:T(8,128)(2,1)}, bf16[2,256,1152]{2,1,0:T(8,128)(2,1)}, f32[8,4,8,1152]{3,2,1,0:T(8,128)}, bf16[1152,1152]{1,0:T(...) custom-call(s32[8]{0:T(128)} %bucket_ref.3, s32[2,128]{1,0:T(2,128)} %kept_ref.3, ...), custom_call_target="tpu_custom_call" | custom-call | tf_op jit(solution)/shard_map/backward_attention/pallas_call | solution.py:1180
  279.3 0.0 copy-start.1
  279.3 11.7 %widen_gradients.1 = (f32[864,1152]{1,0:T(8,128)}, f32[288,1152]{1,0:T(8,128)}, f32[1152,1152]{1,0:T(8,128)}, f32[1152,1152]{1,0:T(8,128)}, f32[1728,1152]{1,0:T...) custom-call(bf16[1152,1152]{1,0:T(8,128)(2,1)} %get-tuple-element.58.ga_h, ...), custom_call_target="tpu_custom_call" | custom-call | tf_op jit(solution)/shard_map/widen_gradients/pallas_call | solution.py:1274
  291.0 0.0 copy-start
  291.0 0.0 copy-done.1
  291.0 1.0 copy.29
  292.0 0.7 copy-done
  292.7 1.0 copy.30
Async XLA Ops:
  279.3 11.7 %copy-start.1 = (bf16[2,256,1152]{2,1,0:T(8,128)(2,1)S(1)}, bf16[2,256,1152]{2,1,0:T(8,128)(2,1)}, u32[]{:S(2)}) copy-start(bf16[2,256,1152]{2,1,0:T(8,128)(2,1)} %get-tuple-element.84) | copy-start | bytes 3538948
  291.0 1.7 copy-start

commit v4 on v3

--- a/solution.py
+++ b/solution.py
@@ -521,6 +521,8 @@
             arrive_m(0, 0)
             arrive_m(0, 1)
             started = True
+        if (i, k) == todo[-1]:
+            relay()
         gathers[k].step(i)
     for k in range(count - 1):
         gathers[k].wait_core()
@@ -530,7 +532,6 @@
     if count > 2:
         arrive_m(1, 0)
         arrive_m(1, 1)
-    relay()
     dm.step(1)
 
     x = attn_in_o[...]
@@ -586,6 +587,7 @@
         b, z, group, lambda m, p, slot: part(xb)(slot, p), lambda m, p: ag_ss.at[p, m], lambda m, p: ag_rs.at[p, m]
     )
     gather.step(0)
+    gather.step(1)
     for k in range(count - 1):
         shard = near_shard(z, k, count)
 
@@ -615,16 +617,23 @@
         gather.wait(1, p)
         dm.wait(1, p)
     forward(((1, 0), (1, 1)))
-    for i in range(1, gather.steps()):
-        gather.step(i)
+    links = gather.steps() - 1
+
+    def fresh_pairs(i):
         fresh = [[m ^ order[i - 1] for m in span(order[: i - 1])] for order in gather.orders]
-        for m0, m1 in zip(*fresh):
-            forward(((m0, 0), (m1, 1)))
-        for m0, m1 in zip(*fresh):
-            for item in (gather, dm):
-                item.wait(m0 ^ 1, 0)
-                item.wait(m1 ^ 1, 1)
-            forward(((m0 ^ 1, 0), (m1 ^ 1, 1)))
+        return list(zip(*fresh))
+
+    def forward_both(m0, m1):
+        forward(((m0, 0), (m1, 1)))
+        for item in (gather, dm):
+            item.wait(m0 ^ 1, 0)
+            item.wait(m1 ^ 1, 1)
+        forward(((m0 ^ 1, 0), (m1 ^ 1, 1)))
+
+    for i in range(1, links):
+        for m0, m1 in fresh_pairs(i):
+            forward_both(m0, m1)
+        gather.step(i + 1)
 
     mine = lambda m, p: y.at[pl.ds(m * rows + p * half, half)]
     arrived = lambda m, p: inbox.at[m - 1, pl.ds(p * half, half)]
@@ -639,10 +648,28 @@
         y[at] = nn(dpre[at], all_1[:, :, 0:width].reshape(hid, width)).astype(BF)
 
     chunks = [slice(c, min(c + 128, hid)) for c in range(0, hid, 128)]
-    rs.send_core(part_in)
-    for m in range(group - 2, 0, -2):
+    def to_sibling(m):
+        part_in(m)
+        for p in range(2):
+            rs.rs.send(m, p)
+
+    whole = [m for m in range(group - 2, 0, -2) if all(rs.rs.top(m, p) == rs.rs.orders[p][-1] for p in range(2))]
+    pairs = fresh_pairs(links)
+    for m in whole:
+        forward_both(m, m)
+        to_sibling(m ^ 1)
         part_in(m)
         rs.last_link(m)
+    for m0, m1 in pairs:
+        if m0 not in whole:
+            forward_both(m0, m1)
+    for m in range(group - 1, 0, -2):
+        if m ^ 1 not in whole:
+            to_sibling(m)
+    for m in range(group - 2, 0, -2):
+        if m not in whole:
+            part_in(m)
+            rs.last_link(m)
     part_in(0)
     ones = jnp.ones((group * rows, g1_o.shape[1] - width), BF)
     for c in chunks:
@@ -743,12 +770,11 @@
 def backward_kernel(dims, lat, bucket_ref, kept_ref, redb_ref, cond_ref, *rest):
     held, rest = rest[:12], rest[12:]
     (full_ref, g1_ref, g2_ref, zp_ref), rest = rest[:4], rest[4:]
-    outs, rest = rest[:3], rest[3:]
-    (ga_o, gm1_o, gm2_o), rest = rest[:3], rest[3:]
+    outs, rest = rest[:6], rest[6:]
     local, rest = rest[:12], rest[12:]
     (tok_ref, cot_in_ref, attn_in_ref, q_ref, k_ref, v_ref, merged_ref, attn_out_ref, hidden_ref, cot_ref, mod_ref,
      d_in_ref) = local
-    small_o, rest = rest[0], rest[1:]
+    (small_o, ga_o, gm1_o, gm2_o), rest = rest[:4], rest[4:]
     out_o, dtok_o, dain, mlp = tok_ref, cot_in_ref, d_in_ref, hidden_ref
     (wbuf, gbuf, abox, ar, gm1, gm2, mr1, mr2, back_b, d3, d_attn, dm, inbox, sm_send, sm_recv, dmod,
      loc, in_sem, out_sem, ro_ss, ro_rs, ra_ss, ra_rs, za_ss, za_rs, zm_ss, zm_rs, gm_ss, gm_rs, ga_ss, ga_rs, sz_ss, sz_rs,
@@ -761,7 +787,7 @@
 
     gives = [
         pltpu.make_async_copy(src, dst, out_sem.at[k])
-        for k, (src, dst) in enumerate(zip((out_o, dtok_o, small_o), outs))
+        for k, (src, dst) in enumerate(zip((out_o, dtok_o, small_o, ga_o, gm1_o, gm2_o), outs))
     ]
     group, count, rows_s, width = dims
     b, z = lax.axis_index("batch"), lax.axis_index("tp")
@@ -932,7 +958,7 @@
     heads = width // HEAD_SIZE
 
     def some_heads(step, _):
-        for h in (step, step + heads // 2):
+        for h in [step + i * (heads // 4) for i in range(4)]:
             win, own = head_window(h, width)
             for l in range(lat):
                 at = pl.ds(l * slots, slots)
@@ -951,11 +977,11 @@
         return 0
 
     need(3, 4, 5)
-    lax.fori_loop(0, heads // 4, some_heads, 0)
+    lax.fori_loop(0, heads // 8, some_heads, 0)
     for i in range(rs_out.links - 1, 0, -1):
         rs_out.link(i)
     relay_add()
-    lax.fori_loop(heads // 4, heads // 2, some_heads, 0)
+    lax.fori_loop(heads // 8, heads // 4, some_heads, 0)
     rs_out.finish(mlp, half)
     mlp[...] += redb_ref[...].astype(F32).reshape(1, width)
     for l in range(lat):
@@ -1085,28 +1111,30 @@
         delta = (mod_ref[2, one] * attn_out_ref[at] + mod_ref[5, one] * mlp[at]) * row_mask(real[l], slots)
         out_o[l] = (tok_ref[l].astype(F32) + put(pick, delta)).astype(BF)
     gives[0].start()
-    for d in range(1, count):
-        ref = sm_recv.at[lax.rem(z - d + count, count)]
-        pltpu.make_async_remote_copy(
-            src_ref=ref, dst_ref=ref, send_sem=sz_ss.at[d], recv_sem=sz_rs.at[d],
-            device_id=(b, lax.rem(z + d, count)), device_id_type=MESH,
-        ).wait_recv()
-    small_own.wait()
-    small_o[0] = jnp.zeros(small_o.shape[1:], F32)
-    for i in range(2):
-        for t in range(count):
-            small_o[0, i, lat * t : lat * (t + 1)] = sm_recv[t, i]
-    for i in range(2):
-        acc = sm_recv[0, 2 + i]
-        for t in range(1, count):
-            acc = acc + sm_recv[t, 2 + i]
-        small_o[0, 2, lat * i : lat * (i + 1)] = acc
-    cond = cond_ref[...].astype(F32)
-    small_o[0, 3] = (cond / (1.0 + jnp.exp(-cond))).astype(BF).astype(F32)
+    def small_in():
+        for d in range(1, count):
+            ref = sm_recv.at[lax.rem(z - d + count, count)]
+            pltpu.make_async_remote_copy(
+                src_ref=ref, dst_ref=ref, send_sem=sz_ss.at[d], recv_sem=sz_rs.at[d],
+                device_id=(b, lax.rem(z + d, count)), device_id_type=MESH,
+            ).wait_recv()
+        small_own.wait()
+        small_o[0] = jnp.zeros(small_o.shape[1:], F32)
+        for i in range(2):
+            for t in range(count):
+                small_o[0, i, lat * t : lat * (t + 1)] = sm_recv[t, i]
+        for i in range(2):
+            acc = sm_recv[0, 2 + i]
+            for t in range(1, count):
+                acc = acc + sm_recv[t, 2 + i]
+            small_o[0, 2, lat * i : lat * (i + 1)] = acc
+        cond = cond_ref[...].astype(F32)
+        small_o[0, 3] = (cond / (1.0 + jnp.exp(-cond))).astype(BF).astype(F32)
+
     sp = Gather(
         b, z, group, lambda m, p, slot: small_o.at[slot], lambda m, p: sp_ss.at[m], lambda m, p: sp_rs.at[m], halves=1
     )
-    sp.step(0)
+
     def spread(out, ss, rs):
         def region(m, p, slot):
             lo, ln = parts[p]
@@ -1124,11 +1152,11 @@
     spread_2.step(0)
     for t in range(3, count + links):
         wave_round(t)
-        if t - 2 < sp.steps():
-            sp.step(t - 2)
         if t == 4:
             spread_1.step(1)
             spread_2.step(1)
+            small_in()
+            sp.step(0)
     acc = own_slice(z)[...].astype(F32)
     for w in range(count - 1):
         line_a(w).wait_recv()
@@ -1140,13 +1168,13 @@
         for item in (spread_1, spread_2):
             if i > 1:
                 item.step(i)
+        sp.step(i)
         spread_a.step(i)
-    for i in range(max(1, count + links - 2), sp.steps()):
-        sp.step(i)
     sp.wait_core()
     gives[2].start()
-    for item in (spread_1, spread_2, spread_a):
+    for item, k in ((spread_1, 4), (spread_2, 5), (spread_a, 3)):
         item.wait_core()
+        gives[k].start()
     for item in (sp, spread_a, spread_1, spread_2):
         item.wait_sent()
     for cp in gives:
@@ -1184,9 +1212,10 @@
             sd((group * rows_s, width), BF), sd((group * rows_s, ext), BF), sd((group * rows_s, width), BF),
         ),
         in_specs=[sm] + [vm] * 3 + [hb] * 16,
-        out_specs=tuple([hb] * 3 + [vm] * 3),
+        out_specs=tuple([hb] * 6),
         scratch_shapes=[vmem(item.shape, item.dtype) for item in held] + [
-            vmem(small, F32),
+            vmem(small, F32), vmem((group * rows_s, width), BF), vmem((group * rows_s, ext), BF),
+            vmem((group * rows_s, width), BF),
             vmem((2, width, width), BF),
             vmem((4 * width, width), BF),
             vmem((count, group - 1, rows_s, width), BF),
@@ -1199,7 +1228,7 @@
             vmem((group - 1, rows, width), BF),
             vmem((count, 4, lat, width), F32), vmem((count, 4, lat, width), F32),
             vmem((6, lat, width), F32),
-            dma((6,)), dma((12,)), dma((3,)),
+            dma((6,)), dma((12,)), dma((6,)),
             dma((2, group)), dma((2, group)),
             dma((count, 2, group)), dma((count, 2, group)),
             dma((count,)), dma((count,)),
@@ -1214,8 +1243,8 @@
     )(bucket, kept, redb, cond, *held, full, g1, g2, zp)
 
 
-def widen_kernel(dims, ga_h, gm1_h, gm2_h, small_h, qkv_o, proj_o, exp_o, red_o, ada_o, adab_o, pair_o, projb_o, redb_o, expb_o,
-                 ga_ref, gm1_ref, gm2_ref, small_ref, qkv, proj, exp, red, ada, sem):
+def widen_kernel(dims, ga_h, gm1_h, gm2_h, small_h, out_h, dtok_h, out_o, dtok_o, qkv_o, proj_o, exp_o, red_o, ada_o, adab_o, pair_o, projb_o, redb_o, expb_o,
+                 ga_ref, gm1_ref, gm2_ref, small_ref, out_ref, dtok_ref, qkv, proj, exp, red, ada, sem):
     group, count, rows_s, width = dims
     ds = width // count
     cols = ada.shape[0]
@@ -1227,20 +1256,23 @@
         cp.start()
         return cp
 
-    loads = [move(small_h, small_ref, 5), move(gm2_h, gm2_ref, 6), move(gm1_h, gm1_ref, 7), move(ga_h, ga_ref, 8)]
+    loads = [
+        move(gm2_h, gm2_ref, 6), move(small_h, small_ref, 5), move(gm1_h, gm1_ref, 7), move(ga_h, ga_ref, 8),
+        move(out_h, out_ref, 9), move(dtok_h, dtok_ref, 10),
+    ]
 
     def item(k):
         return small_ref[:, k].reshape(members, width)
 
     loads[0].wait()
+    red[...] = gm2_ref[...].astype(F32)
+    done = [move(red, red_o, 1)]
+    loads[1].wait()
     pair = jnp.concatenate([item(0), item(1)], axis=1)
     start = lax.rem(z * cols, width)
     pair = pltpu.roll(pair, lax.rem(2 * width - start, 2 * width), 1)[:, 0:cols]
     ada[...] = tn(pair.astype(BF), item(3).astype(BF))
-    done = [move(ada, ada_o, 0)]
-    loads[1].wait()
-    red[...] = gm2_ref[...].astype(F32)
-    done.append(move(red, red_o, 1))
+    done.append(move(ada, ada_o, 0))
     loads[2].wait()
     exp[...] = gm1_ref[:, 0:width].T.astype(F32)
     done.append(move(exp, exp_o, 2))
@@ -1249,6 +1281,10 @@
     done.append(move(qkv, qkv_o, 3))
     proj[...] = ga_ref[3 * ds :].astype(F32)
     done.append(move(proj, proj_o, 4))
+    loads[4].wait()
+    done.append(move(out_ref, out_o, 11))
+    loads[5].wait()
+    done.append(move(dtok_ref, dtok_o, 12))
     adab_o[...] = jnp.sum(pair, axis=0)
     acc = small_ref[0, 2]
     for i in range(1, small_ref.shape[0]):
@@ -1262,7 +1298,7 @@
         cp.wait()
 
 
-def run_widen(dims, cols, ga, gm1, gm2, small):
+def run_widen(dims, cols, ga, gm1, gm2, small, output, tokens_grad):
     group, count, rows_s, width = dims
     ds = width // count
     vm = pl.BlockSpec(memory_space=pltpu.VMEM)
@@ -1270,15 +1306,16 @@
     hid_s = gm1.shape[0]
     big = [(3 * ds, width), (ds, width), (width, hid_s), gm2.shape, (cols, width)]
     vecs = [(cols,), (2, ds), (width,), (width,), (hid_s,)]
-    given = (ga, gm1, gm2, small)
+    given = (ga, gm1, gm2, small, output, tokens_grad)
+    rows = jax.ShapeDtypeStruct(output.shape, BF)
     return pl.pallas_call(
         functools.partial(widen_kernel, dims),
-        out_shape=tuple(jax.ShapeDtypeStruct(item, F32) for item in big + vecs),
-        in_specs=[hb] * 4,
-        out_specs=tuple([hb] * 5 + [vm] * 5),
+        out_shape=(rows, rows) + tuple(jax.ShapeDtypeStruct(item, F32) for item in big + vecs),
+        in_specs=[hb] * 6,
+        out_specs=tuple([hb] * 7 + [vm] * 5),
         scratch_shapes=[pltpu.VMEM(item.shape, item.dtype) for item in given]
         + [pltpu.VMEM(item, F32) for item in big]
-        + [pltpu.SemaphoreType.DMA((9,))],
+        + [pltpu.SemaphoreType.DMA((13,))],
         compiler_params=pltpu.CompilerParams(vmem_limit_bytes=60 * MIB),
         name="widen_gradients",
     )(*given)
@@ -1310,7 +1347,9 @@
         return items
 
     ga, gm1, gm2 = over_batch((ga, gm1, gm2))
-    qkv_grad, proj_grad, expand_grad, reduce_grad, *sums = run_widen(dims, cols, ga, gm1, gm2, small)
+    output, tokens_grad, qkv_grad, proj_grad, expand_grad, reduce_grad, *sums = run_widen(
+        dims, cols, ga, gm1, gm2, small, output, tokens_grad
+    )
     ada_grad, ada_add, pair_grad, proj_add, reduce_add = over_batch(tuple(sums[:5]))
     return (
         output,

time: 299 us -> 294 us (0.983)
  Pallas kernels: 290 us -> 287 us
where the time goes in v4:
time: 294 us; the launch traced here: 288 us
  Pallas kernels  287 us (98%)
    pallas_call x1, Pallas kernels, run_backward(): pl.pallas_call(functools.partial(backward_kernel, dims, lat), out_shape=(...  139 us
    pallas_call x1, Pallas kernels, run_forward(): pl.pallas_call(functools.partial(forward_kernel, dims, lat), out_shape=ou...  136 us
    pallas_call x1, Pallas kernels, run_widen(): pl.pallas_call(functools.partial(widen_kernel, dims), out_shape=(rows, ro...  12.5 us

profile of v4, /device:TPU:17, one launch (start us, length us, event | category | flops | bytes accessed | tf_op | source)
XLA Modules:
  0.0 288.3 jit_solution(1177257988666026647)
XLA Ops:
  0.6 136.3 %forward_attention.1 = (bf16[256,1152]{1,0:T(8,128)(2,1)}, bf16[256,1152]{1,0:T(8,128)(2,1)}, bf16[256,1152]{1,0:T(8,128)(2,1)}, bf16[256,1152]{1,0:T(8,128)(2,1...) custom-call(s32[8]{0:T(128)} %bucket_ref.3, ...), custom_call_target="tpu_custom_call" | custom-call | tf_op jit(solution)/shard_map/forward_attention/pallas_call | solution.py:743
  137.0 138.6 %backward_attention.1 = (bf16[2,256,1152]{2,1,0:T(8,128)(2,1)}, bf16[2,256,1152]{2,1,0:T(8,128)(2,1)}, f32[8,4,8,1152]{3,2,1,0:T(8,128)}, bf16[1152,1152]{1,0:T(...) custom-call(s32[8]{0:T(128)} %bucket_ref.3, s32[2,128]{1,0:T(2,128)} %kept_ref.3, ...), custom_call_target="tpu_custom_call" | custom-call | tf_op jit(solution)/shard_map/backward_attention/pallas_call | solution.py:1208
  275.6 12.5 %widen_gradients.1 = (bf16[2,256,1152]{2,1,0:T(8,128)(2,1)}, bf16[2,256,1152]{2,1,0:T(8,128)(2,1)}, f32[864,1152]{1,0:T(8,128)}, f32[288,1152]{1,0:T(8,128)}, f3...) custom-call(bf16[1152,1152]{1,0:T(8,128)(2,1)} %get-tuple-element.58, ...), custom_call_target="tpu_custom_call" | custom-call | tf_op jit(solution)/shard_map/widen_gradients/pallas_call | solution.py:1311

commit v5 on v4

--- a/solution.py
+++ b/solution.py
@@ -464,7 +464,6 @@
 
     @pl.when(ends)
     def _():
-        send_far()
         both_ways(send_m)
 
     for d in range(1, count):
@@ -494,11 +493,13 @@
 
     for k in range(1, count - 1):
         arrive_a(k)
-        if k == 1:
+        if k == count - 2:
 
             @pl.when(jnp.logical_not(ends))
             def _():
                 both_ways(send_m)
+
+            send_far()
 
         gathers[k - 1].step(1)
     depth = gathers[0].steps()
@@ -513,10 +514,6 @@
     for i, k in todo:
         if i >= links and not started:
             dm.step(0)
-
-            @pl.when(inner)
-            def _():
-                send_far()
 
             arrive_m(0, 0)
             arrive_m(0, 1)

time: 294 us -> 283 us (0.963)
  Pallas kernels: 287 us -> 277 us
    pallas_call x1, Pallas kernels: 136 us -> 126 us  [run_forward(): pl.pallas_call(functools.partial(forward_kernel, dims, lat), out_shape=ou...]
where the time goes in v5:
time: 283 us; the launch traced here: 278 us
  Pallas kernels  277 us (98%)
    pallas_call x1, Pallas kernels, run_backward(): pl.pallas_call(functools.partial(backward_kernel, dims, lat), out_shape=(...  138 us
    pallas_call x1, Pallas kernels, run_forward(): pl.pallas_call(functools.partial(forward_kernel, dims, lat), out_shape=ou...  126 us
    pallas_call x1, Pallas kernels, run_widen(): pl.pallas_call(functools.partial(widen_kernel, dims), out_shape=(rows, ro...  12.5 us

profile of v5, /device:TPU:17, one launch (start us, length us, event | category | flops | bytes accessed | tf_op | source)
XLA Modules:
  0.0 277.7 jit_solution(18050321401423766706)
XLA Ops:
  0.6 125.8 %forward_attention.1 = (bf16[256,1152]{1,0:T(8,128)(2,1)}, bf16[256,1152]{1,0:T(8,128)(2,1)}, bf16[256,1152]{1,0:T(8,128)(2,1)}, bf16[256,1152]{1,0:T(8,128)(2,1...) custom-call(s32[8]{0:T(128)} %bucket_ref.3, ...), custom_call_target="tpu_custom_call" | custom-call | tf_op jit(solution)/shard_map/forward_attention/pallas_call | solution.py:740
  126.5 138.5 %backward_attention.1 = (bf16[2,256,1152]{2,1,0:T(8,128)(2,1)}, bf16[2,256,1152]{2,1,0:T(8,128)(2,1)}, f32[8,4,8,1152]{3,2,1,0:T(8,128)}, bf16[1152,1152]{1,0:T(...) custom-call(s32[8]{0:T(128)} %bucket_ref.3, s32[2,128]{1,0:T(2,128)} %kept_ref.3, ...), custom_call_target="tpu_custom_call" | custom-call | tf_op jit(solution)/shard_map/backward_attention/pallas_call | solution.py:1205
  265.0 12.5 %widen_gradients.1 = (bf16[2,256,1152]{2,1,0:T(8,128)(2,1)}, bf16[2,256,1152]{2,1,0:T(8,128)(2,1)}, f32[864,1152]{1,0:T(8,128)}, f32[288,1152]{1,0:T(8,128)}, f3...) custom-call(bf16[1152,1152]{1,0:T(8,128)(2,1)} %get-tuple-element.58, ...), custom_call_target="tpu_custom_call" | custom-call | tf_op jit(solution)/shard_map/widen_gradients/pallas_call | solution.py:1308
